TPU v7x, 32 devices: a whole 2x2x4 slice. The times are simulated.
32 devices in a mesh: rows: 2 (over y), cols: 8 (over z, x), fsdp: 2 (over core).
Axes of the slice: x: 2, y: 2, z: 4, core: 2. Of those that a mesh axis runs over, the one named last changes fastest.
Arguments:
- latent: bfloat16 [2, 2, 4, 128, 256], P(None, 'fsdp', None, 'rows', 'cols'), may hold values from -6 to 6
- time_embed: float32 [2, 2, 8, 4, 1024], P(None, 'fsdp', 'cols'), may hold values from -6 to 6
- image_rows: int32 [2, 2, 8, 4], P(None, 'fsdp', 'cols'), may hold values from 0 to 64, as said below
- pred_grad: bfloat16 [2, 2, 4, 128, 256], P(None, 'fsdp', None, 'rows', 'cols'), may hold values from -6 to 6
- embed_weight: bfloat16 [1536, 64], P(('rows', 'cols', 'fsdp')), may hold values from -0.75 to 0.75
- adaptive_weight: bfloat16 [1024, 7680], P(('rows', 'cols', 'fsdp')), may hold values from -0.1875 to 0.1875
- project_weight: bfloat16 [1536, 4608], P(('rows', 'cols', 'fsdp')), may hold values from -0.15625 to 0.15625
- output_weight: bfloat16 [1536, 1536], P(('rows', 'cols', 'fsdp')), may hold values from -0.15625 to 0.15625
- gate_up_weight: bfloat16 [1536, 8192], P(('rows', 'cols', 'fsdp')), may hold values from -0.15625 to 0.15625
- down_weight: bfloat16 [4096, 1536], P(('rows', 'cols', 'fsdp')), may hold values from -0.09375 to 0.09375
- final_weight: bfloat16 [1536, 64], P(('rows', 'cols', 'fsdp')), may hold values from -0.15625 to 0.15625
- norm_gains: bfloat16 [1536, 6], P(('rows', 'cols', 'fsdp')), may hold values from 0.25 to 1.75
Outputs:
- prediction: float32 [2, 2, 4, 128, 256], P(None, 'fsdp', None, 'rows', 'cols')
- latent_grad: float32 [2, 2, 4, 128, 256], P(None, 'fsdp', None, 'rows', 'cols')
- embed_grad: float32 [1536, 64], P(('rows', 'cols', 'fsdp'))
- adaptive_grad: float32 [1024, 7680], P(('rows', 'cols', 'fsdp'))
- project_grad: float32 [1536, 4608], P(('rows', 'cols', 'fsdp'))
- output_grad: float32 [1536, 1536], P(('rows', 'cols', 'fsdp'))
- gate_up_grad: float32 [1536, 8192], P(('rows', 'cols', 'fsdp'))
- down_grad: float32 [4096, 1536], P(('rows', 'cols', 'fsdp'))
- final_grad: float32 [1536, 64], P(('rows', 'cols', 'fsdp'))
- gain_grad: float32 [1536, 6], P(('rows', 'cols', 'fsdp'))
Inputs may be any that keep to these rules, and one draw needn't show every extreme that they name: `image_rows`: each row of 4 heights sums to 64; in every micro-batch and group one column strip holds a single image of all 64 patch rows.
All inputs are finite; a program needn't handle non-finite values.
Results may differ from a plain program's by a relative error of at most 0.014.
Values may be sent and summed in bfloat16 or wider, within the bound.
No kernel may reach another device: no remote copies, remote signals or barrier semaphores. Data moves between devices by JAX's collectives and lax.ppermute only.
A program may use at most 512 MiB of HBM per device.

v0:
```python
from functools import partial

import jax
import jax.numpy as jnp
from jax import lax
from jax.sharding import PartitionSpec as P

D = 1536
HEADS = 24
HD = 64
FF = 4096
CHANNELS = 4
PIN = 64
IMGS = 4


epsilon = 1e-06
highest = lax.Precision.HIGHEST
negative = -1e30


def extended(cells, sides, width):
    for axis, dim in sides:
        count = lax.axis_size(axis)
        ends = count - 1
        head = lax.slice_in_dim(cells, 0, width, axis=dim)
        tail = lax.slice_in_dim(cells, cells.shape[dim] - width, cells.shape[dim], axis=dim)
        cells = jnp.concatenate(
            [
                lax.ppermute(tail, axis, [(i, (i + 1) % count) for i in range(ends)]),
                cells,
                lax.ppermute(head, axis, [((i + 1) % count, i) for i in range(ends)]),
            ],
            axis=dim,
        )
    return cells


def rms_norm(values, gain):
    return values * lax.rsqrt(jnp.mean(values * values, axis=-1, keepdims=True) + epsilon) * gain


def layer_norm(values):
    centred = values - jnp.mean(values, axis=-1, keepdims=True)
    return centred * lax.rsqrt(jnp.mean(centred * centred, axis=-1, keepdims=True) + epsilon)


def contract_last(left, right):
    return lax.dot_general(
        left, right, (((1,), (1,)), ((), ())), preferred_element_type=jnp.float32
    )


def contract_first(left, right):
    return lax.dot_general(
        left, right, (((0,), (0,)), ((), ())), preferred_element_type=jnp.float32
    )


def exact_first(left, right):
    return lax.dot_general(
        left, right, (((0,), (0,)), ((), ())), precision=highest, preferred_element_type=jnp.float32
    )


def pixel_rim(pixel_tile):
    return extended(pixel_tile, (("rows", 1), ("cols", 2)), 1)


def patch_rim(patch_grid):
    return extended(patch_grid, (("rows", 0), ("cols", 1)), 1)


def extract_patches(padded, rows_tile, cols_tile):
    windows = [
        padded[:, a : a + 2 * rows_tile : 2, b : b + 2 * cols_tile : 2]
        for a in range(4)
        for b in range(4)
    ]
    return jnp.stack(windows, axis=1).reshape(PIN, rows_tile * cols_tile).T


def fold_core(padded_grid):
    outer_rows = padded_grid.shape[0]
    outer_cols = padded_grid.shape[1]
    pieces = padded_grid.reshape(outer_rows, outer_cols, CHANNELS, 2, 2, 2, 2)
    total = jnp.zeros((outer_rows + 1, outer_cols + 1, CHANNELS, 2, 2), jnp.float32)
    for upper in range(2):
        for left in range(2):
            shifted = jnp.pad(
                pieces[:, :, :, upper, :, left, :],
                ((upper, 1 - upper), (left, 1 - left), (0, 0), (0, 0), (0, 0)),
            )
            total = total + shifted
    canvas = total.transpose(2, 0, 3, 1, 4).reshape(
        CHANNELS, 2 * outer_rows + 2, 2 * outer_cols + 2
    )
    return canvas[:, 3 : 2 * outer_rows - 1, 3 : 2 * outer_cols - 1]


def strip_layout(heights, seq_rows):
    starts = jnp.cumsum(heights) - heights
    rows_all = jnp.arange(seq_rows, dtype=jnp.int32)
    image_of = jnp.sum((rows_all[:, None] >= starts[None, 1:]).astype(jnp.int32), axis=1)
    start_of = jnp.sum(
        jnp.where(
            image_of[:, None] == jnp.arange(IMGS, dtype=jnp.int32)[None, :], starts[None, :], 0
        ),
        axis=1,
    )
    return (image_of, rows_all - start_of)


def rope_tables(row_place, column):
    quarter = HD // 4
    frequency = 10000.0 ** (-jnp.arange(quarter, dtype=jnp.float32) / quarter)
    row_angle = row_place.astype(jnp.float32)[:, None] * frequency[None, :]
    col_angle = column.astype(jnp.float32)[:, None] * frequency[None, :]
    angles = jnp.concatenate([row_angle, row_angle, col_angle, col_angle], axis=1)
    return (jnp.cos(angles), jnp.sin(angles))


def rotate(values, cosine, sine_table):
    tok_count = values.shape[0]
    split = values.reshape(tok_count, HEADS, 2, 2, HD // 4)
    swapped = jnp.stack([-split[:, :, :, 1, :], split[:, :, :, 0, :]], axis=3).reshape(
        tok_count, HEADS, HD
    )
    plain = values.reshape(tok_count, HEADS, HD)
    return (plain * cosine[:, None, :] + swapped * sine_table[:, None, :]).reshape(tok_count, D)


def attn_input(embedded, scale_attn, gain_pre):
    return rms_norm(embedded, gain_pre) * (1.0 + scale_attn)


def query_key(cosine, sine_table, queries, keys, gain_query, gain_key):
    return (
        rotate(rms_norm(queries, gain_query), cosine, sine_table),
        rotate(rms_norm(keys, gain_key), cosine, sine_table),
    )


def after_attention(embedded, attn_out, gate_attn, gain_post, scale_ffn, gain_pre):
    mixed = embedded + jnp.tanh(gate_attn) * rms_norm(attn_out, gain_post)
    return (mixed, rms_norm(mixed, gain_pre) * (1.0 + scale_ffn))


def activate(gate_up):
    return jax.nn.silu(gate_up[:, :FF]) * gate_up[:, FF:]


def after_ffn(mixed, ffn_out, gate_ffn, gain_post, scale_out):
    final_state = mixed + jnp.tanh(gate_ffn) * rms_norm(ffn_out, gain_post)
    return layer_norm(final_state) * (1.0 + scale_out)


def attend(queries, keys, values, image_of, head_count):
    length = queries.shape[0]
    block_rows = min(512, length)
    score_scale = HD ** (-0.5)
    q_heads = queries.reshape(length // block_rows, block_rows, head_count, HD)
    k_heads = keys.reshape(length, head_count, HD)
    v_heads = values.reshape(length, head_count, HD)

    def one_block(inputs):
        q_block, block_image = inputs
        scores = (
            jnp.einsum("qhd,khd->hqk", q_block, k_heads, preferred_element_type=jnp.float32)
            * score_scale
        )
        same_image = block_image[:, None] == image_of[None, :]
        scores = jnp.where(same_image[None], scores, negative)
        row_top = jnp.max(scores, axis=-1, keepdims=True)
        raised = jnp.exp(scores - row_top)
        row_total = jnp.sum(raised, axis=-1, keepdims=True)
        chances = (raised / row_total).astype(jnp.bfloat16)
        result = jnp.einsum("hqk,khd->qhd", chances, v_heads, preferred_element_type=jnp.float32)
        return (
            result.reshape(block_rows, head_count * HD).astype(jnp.bfloat16),
            (row_top + jnp.log(row_total))[:, :, 0],
        )

    outputs, log_total = lax.map(one_block, (q_heads, image_of.reshape(-1, block_rows)))
    return (outputs.reshape(length, head_count * HD), log_total)


def attend_back(queries, keys, values, grads, image_of, log_total, head_count):
    length = queries.shape[0]
    block_rows = min(512, length)
    score_scale = HD ** (-0.5)
    q_heads = queries.reshape(length // block_rows, block_rows, head_count, HD)
    g_heads = grads.reshape(length // block_rows, block_rows, head_count, HD)
    k_heads = keys.reshape(length, head_count, HD)
    v_heads = values.reshape(length, head_count, HD)

    def one_block(carry, inputs):
        grad_keys, grad_values = carry
        q_block, g_block, block_image, block_total = inputs
        scores = (
            jnp.einsum("qhd,khd->hqk", q_block, k_heads, preferred_element_type=jnp.float32)
            * score_scale
        )
        same_image = block_image[:, None] == image_of[None, :]
        chances = jnp.where(same_image[None], jnp.exp(scores - block_total[:, :, None]), 0.0)
        grad_values = grad_values + jnp.einsum(
            "hqk,qhd->khd",
            chances.astype(jnp.bfloat16),
            g_block,
            preferred_element_type=jnp.float32,
        )
        grad_chances = jnp.einsum(
            "qhd,khd->hqk", g_block, v_heads, preferred_element_type=jnp.float32
        )
        inner = jnp.sum(chances * grad_chances, axis=-1, keepdims=True)
        grad_scores = (chances * (grad_chances - inner)).astype(jnp.bfloat16)
        grad_q = (
            jnp.einsum("hqk,khd->qhd", grad_scores, k_heads, preferred_element_type=jnp.float32)
            * score_scale
        )
        grad_keys = (
            grad_keys
            + jnp.einsum("hqk,qhd->khd", grad_scores, q_block, preferred_element_type=jnp.float32)
            * score_scale
        )
        return ((grad_keys, grad_values), grad_q.reshape(block_rows, head_count * HD))

    zeros = jnp.zeros((length, head_count, HD), jnp.float32)
    carried, grad_queries = lax.scan(
        one_block, (zeros, zeros), (q_heads, g_heads, image_of.reshape(-1, block_rows), log_total)
    )
    return (
        grad_queries.reshape(length, head_count * HD),
        carried[0].reshape(length, head_count * HD),
        carried[1].reshape(length, head_count * HD),
    )


def run_micro(gathered, pixel_tile, temb_rows, heights, grad_tile):
    w_embed, w_adaptive, w_project, w_output, w_gate_up, w_down, w_final, gain_table = gathered
    gain_cols = gain_table.astype(jnp.float32)
    rows_tile = pixel_tile.shape[1] // 2
    cols_tile = pixel_tile.shape[2] // 2
    tok_count = rows_tile * cols_tile
    row_devices = lax.axis_size("rows")
    seq_rows = rows_tile * row_devices
    seq_len = seq_rows * cols_tile
    head_count = HEADS // row_devices
    head_width = head_count * HD
    tile_shape = (tok_count, row_devices, head_width)
    strip_shape = (seq_len, 1, head_width)
    patches = extract_patches(pixel_rim(pixel_tile), rows_tile, cols_tile)
    embedded = contract_last(patches, w_embed)
    row_image, row_place = strip_layout(heights, seq_rows)
    first_row = lax.axis_index("rows") * rows_tile
    token_image = jnp.repeat(lax.dynamic_slice_in_dim(row_image, first_row, rows_tile), cols_tile)
    token_place = jnp.repeat(lax.dynamic_slice_in_dim(row_place, first_row, rows_tile), cols_tile)
    token_column = jnp.tile(jnp.arange(cols_tile, dtype=jnp.int32), rows_tile)
    onehot = (token_image[:, None] == jnp.arange(IMGS, dtype=jnp.int32)[None, :]).astype(
        jnp.float32
    )
    condition = jax.nn.silu(temb_rows).astype(jnp.bfloat16)
    per_image = jnp.dot(condition, w_adaptive, preferred_element_type=jnp.float32)
    modulation = jnp.dot(onehot, per_image, precision=highest)
    scale_attn = modulation[:, 0:D]
    gate_attn = modulation[:, D : 2 * D]
    scale_ffn = modulation[:, 2 * D : 3 * D]
    gate_ffn = modulation[:, 3 * D : 4 * D]
    scale_out = modulation[:, 4 * D : 5 * D]
    normed, attn_input_back = jax.vjp(attn_input, embedded, scale_attn, gain_cols[:, 0])
    normed_b = normed.astype(jnp.bfloat16)
    projected = jnp.dot(normed_b, w_project, preferred_element_type=jnp.float32)
    cosine, sine_table = rope_tables(token_place, token_column)
    rotated, query_key_back = jax.vjp(
        partial(query_key, cosine, sine_table),
        projected[:, :D],
        projected[:, D : 2 * D],
        gain_cols[:, 1],
        gain_cols[:, 2],
    )
    heads_q, heads_k, heads_v = (
        lax.all_to_all(
            rotated[0].astype(jnp.bfloat16).reshape(tile_shape),
            "rows",
            split_axis=1,
            concat_axis=0,
            tiled=True,
        ),
        lax.all_to_all(
            rotated[1].astype(jnp.bfloat16).reshape(tile_shape),
            "rows",
            split_axis=1,
            concat_axis=0,
            tiled=True,
        ),
        lax.all_to_all(
            projected[:, 2 * D :].astype(jnp.bfloat16).reshape(tile_shape),
            "rows",
            split_axis=1,
            concat_axis=0,
            tiled=True,
        ),
    )
    heads_q = heads_q.reshape(seq_len, head_width)
    heads_k = heads_k.reshape(seq_len, head_width)
    heads_v = heads_v.reshape(seq_len, head_width)
    strip_image = jnp.repeat(row_image, cols_tile)
    attended, log_total = attend(heads_q, heads_k, heads_v, strip_image, head_count)
    attended_tile = lax.all_to_all(
        attended.reshape(strip_shape), "rows", split_axis=0, concat_axis=1, tiled=True
    ).reshape(tok_count, D)
    attn_out = jnp.dot(attended_tile, w_output, preferred_element_type=jnp.float32)
    (mixed, normed_ffn), after_attention_back = jax.vjp(
        after_attention, embedded, attn_out, gate_attn, gain_cols[:, 3], scale_ffn, gain_cols[:, 4]
    )
    normed_ffn_b = normed_ffn.astype(jnp.bfloat16)
    gate_up = jnp.dot(normed_ffn_b, w_gate_up, preferred_element_type=jnp.float32)
    hidden, activate_back = jax.vjp(activate, gate_up)
    hidden_b = hidden.astype(jnp.bfloat16)
    ffn_out = jnp.dot(hidden_b, w_down, preferred_element_type=jnp.float32)
    final_normed, after_ffn_back = jax.vjp(
        after_ffn, mixed, ffn_out, gate_ffn, gain_cols[:, 5], scale_out
    )
    final_b = final_normed.astype(jnp.bfloat16)
    pieces = (
        jnp.dot(final_b, w_final, preferred_element_type=jnp.float32)
        .astype(jnp.bfloat16)
        .reshape(rows_tile, cols_tile, PIN)
    )
    prediction = fold_core(patch_rim(pieces).astype(jnp.float32))
    grad_patches = extract_patches(pixel_rim(grad_tile), rows_tile, cols_tile)
    grad_final = contract_last(grad_patches, w_final)
    grad_mixed_late, grad_ffn_out, grad_gate_ffn, grad_gain_post_ffn, grad_scale_out = (
        after_ffn_back(grad_final)
    )
    ffn_grad_b = grad_ffn_out.astype(jnp.bfloat16)
    grad_hidden = contract_last(ffn_grad_b, w_down)
    grad_gate_up = activate_back(grad_hidden)[0]
    gate_up_grad_b = grad_gate_up.astype(jnp.bfloat16)
    grad_normed_ffn = contract_last(gate_up_grad_b, w_gate_up)
    (
        grad_embedded_late,
        grad_attn_out,
        grad_gate_attn,
        grad_gain_post_attn,
        grad_scale_ffn,
        grad_gain_pre_ffn,
    ) = after_attention_back((grad_mixed_late, grad_normed_ffn))
    attn_grad_b = grad_attn_out.astype(jnp.bfloat16)
    grad_attended = contract_last(attn_grad_b, w_output).astype(jnp.bfloat16)
    heads_grad = lax.all_to_all(
        grad_attended.reshape(tile_shape), "rows", split_axis=1, concat_axis=0, tiled=True
    ).reshape(seq_len, head_width)
    grad_q, grad_k, grad_v = attend_back(
        heads_q, heads_k, heads_v, heads_grad, strip_image, log_total, head_count
    )
    tiles_q, tiles_k, tiles_v = (
        lax.all_to_all(
            grad_q.astype(jnp.bfloat16).reshape(strip_shape),
            "rows",
            split_axis=0,
            concat_axis=1,
            tiled=True,
        ),
        lax.all_to_all(
            grad_k.astype(jnp.bfloat16).reshape(strip_shape),
            "rows",
            split_axis=0,
            concat_axis=1,
            tiled=True,
        ),
        lax.all_to_all(
            grad_v.astype(jnp.bfloat16).reshape(strip_shape),
            "rows",
            split_axis=0,
            concat_axis=1,
            tiled=True,
        ),
    )
    grad_queries, grad_keys, grad_gain_query, grad_gain_key = query_key_back(
        (
            tiles_q.reshape(tok_count, D).astype(jnp.float32),
            tiles_k.reshape(tok_count, D).astype(jnp.float32),
        )
    )
    project_back = jnp.concatenate(
        [
            grad_queries.astype(jnp.bfloat16),
            grad_keys.astype(jnp.bfloat16),
            tiles_v.reshape(tok_count, D),
        ],
        axis=1,
    )
    grad_normed = contract_last(project_back, w_project)
    grad_embedded_early, grad_scale_attn, grad_gain_pre_attn = attn_input_back(grad_normed)
    embed_back = (grad_embedded_early + grad_embedded_late).astype(jnp.bfloat16)
    grad_pieces = (
        jnp.dot(embed_back, w_embed, preferred_element_type=jnp.float32)
        .astype(jnp.bfloat16)
        .reshape(rows_tile, cols_tile, PIN)
    )
    latent_grad = fold_core(patch_rim(grad_pieces).astype(jnp.float32))
    grad_modulation = jnp.concatenate(
        [grad_scale_attn, grad_gate_attn, grad_scale_ffn, grad_gate_ffn, grad_scale_out], axis=1
    )
    grad_per_image = exact_first(onehot, grad_modulation)
    record = dict(
        patches=patches,
        embed_back=embed_back,
        normed=normed_b,
        project_back=project_back,
        attended=attended_tile,
        attn_back=attn_grad_b,
        normed_ffn=normed_ffn_b,
        gate_up_back=gate_up_grad_b,
        hidden=hidden_b,
        ffn_back=ffn_grad_b,
        final=final_b,
        pieces_back=grad_patches,
        modulation=exact_first(condition.astype(jnp.float32), grad_per_image),
        gains=jnp.stack(
            [
                grad_gain_pre_attn,
                grad_gain_query,
                grad_gain_key,
                grad_gain_post_attn,
                grad_gain_pre_ffn,
                grad_gain_post_ffn,
            ],
            axis=1,
        ),
    )
    return (prediction, latent_grad, record)


def joined(records, name):
    return jnp.concatenate([record[name] for record in records], axis=0)


def summed(records, name):
    return jnp.sum(jnp.stack([record[name] for record in records]), axis=0)


def ffn_terms(records):
    return (
        contract_first(joined(records, "normed_ffn"), joined(records, "gate_up_back")),
        contract_first(joined(records, "hidden"), joined(records, "ffn_back")),
    )


def other_terms(records):
    return (
        contract_first(joined(records, "embed_back"), joined(records, "patches")),
        summed(records, "modulation"),
        contract_first(joined(records, "normed"), joined(records, "project_back")),
        contract_first(joined(records, "attended"), joined(records, "attn_back")),
        contract_first(joined(records, "final"), joined(records, "pieces_back")),
        summed(records, "gains"),
    )


def shards(
    latent,
    time_embed,
    image_rows,
    pred_grad,
    embed_weight,
    adaptive_weight,
    project_weight,
    output_weight,
    gate_up_weight,
    down_weight,
    final_weight,
    norm_gains,
):
    micro_count = latent.shape[0]
    results = []
    for m in range(micro_count):
        gathered = (
            lax.all_gather(embed_weight, ("rows", "cols", "fsdp"), axis=0, tiled=True),
            lax.all_gather(adaptive_weight, ("rows", "cols", "fsdp"), axis=0, tiled=True),
            lax.all_gather(project_weight, ("rows", "cols", "fsdp"), axis=0, tiled=True),
            lax.all_gather(output_weight, ("rows", "cols", "fsdp"), axis=0, tiled=True),
            lax.all_gather(gate_up_weight, ("rows", "cols", "fsdp"), axis=0, tiled=True),
            lax.all_gather(down_weight, ("rows", "cols", "fsdp"), axis=0, tiled=True),
            lax.all_gather(final_weight, ("rows", "cols", "fsdp"), axis=0, tiled=True),
            lax.all_gather(norm_gains, ("rows", "cols", "fsdp"), axis=0, tiled=True),
        )
        results.append(
            run_micro(
                gathered, latent[m, 0], time_embed[m, 0, 0], image_rows[m, 0, 0], pred_grad[m, 0]
            )
        )
    records = [result[2] for result in results]
    ffn_part = ffn_terms(records)
    ffn_shares = (
        lax.psum_scatter(ffn_part[0], ("rows", "cols", "fsdp"), scatter_dimension=0, tiled=True),
        lax.psum_scatter(ffn_part[1], ("rows", "cols", "fsdp"), scatter_dimension=0, tiled=True),
    )
    other_part = other_terms(records)
    other_shares = (
        lax.psum_scatter(other_part[0], ("rows", "cols", "fsdp"), scatter_dimension=0, tiled=True),
        lax.psum_scatter(other_part[1], ("rows", "cols", "fsdp"), scatter_dimension=0, tiled=True),
        lax.psum_scatter(other_part[2], ("rows", "cols", "fsdp"), scatter_dimension=0, tiled=True),
        lax.psum_scatter(other_part[3], ("rows", "cols", "fsdp"), scatter_dimension=0, tiled=True),
        lax.psum_scatter(other_part[4], ("rows", "cols", "fsdp"), scatter_dimension=0, tiled=True),
        lax.psum_scatter(other_part[5], ("rows", "cols", "fsdp"), scatter_dimension=0, tiled=True),
    )
    predictions = jnp.stack([result[0] for result in results])[:, None]
    latent_grads = jnp.stack([result[1] for result in results])[:, None]
    return (
        predictions,
        latent_grads,
        other_shares[0],
        other_shares[1],
        other_shares[2],
        other_shares[3],
        ffn_shares[0],
        ffn_shares[1],
        other_shares[4],
        other_shares[5],
    )


def solution(mesh):
    placed = (
        P(None, "fsdp", None, "rows", "cols"),
        P(None, "fsdp", "cols", None, None),
        P(None, "fsdp", "cols", None),
        P(None, "fsdp", None, "rows", "cols"),
        P(("rows", "cols", "fsdp"), None),
        P(("rows", "cols", "fsdp"), None),
        P(("rows", "cols", "fsdp"), None),
        P(("rows", "cols", "fsdp"), None),
        P(("rows", "cols", "fsdp"), None),
        P(("rows", "cols", "fsdp"), None),
        P(("rows", "cols", "fsdp"), None),
        P(("rows", "cols", "fsdp"), None),
    )
    return jax.shard_map(
        shards,
        mesh=mesh,
        in_specs=placed,
        out_specs=(
            P(None, "fsdp", None, "rows", "cols"),
            P(None, "fsdp", None, "rows", "cols"),
            P(("rows", "cols", "fsdp"), None),
            P(("rows", "cols", "fsdp"), None),
            P(("rows", "cols", "fsdp"), None),
            P(("rows", "cols", "fsdp"), None),
            P(("rows", "cols", "fsdp"), None),
            P(("rows", "cols", "fsdp"), None),
            P(("rows", "cols", "fsdp"), None),
            P(("rows", "cols", "fsdp"), None),
        ),
        check_vma=False,
    )
```

profile of v0, /device:TPU:0, one launch (start us, length us, event | category | flops | bytes accessed | tf_op | source)
XLA Modules:
  0.0 3341.6 jit_solution(15557792334905361580)
XLA Ops:
  42.2 41.4 %all_gather.32 = bf16[1536,64]{1,0:T(8,128)(2,1)S(1)} all-gather(bf16[48,64]{1,0:T(8,128)(2,1)S(1)} %copy-done.213), channel_id=1, replica_groups=mesh['rows'=2,'cols'=8,'fsdp'=2] {'rows','cols','fsdp'}, dimensions={0}, use_global_device_ids=true | all-gather | bytes 202752 | tf_op jit(solution)/shard_map/all_gather | solution.py:480
  85.0 37.8 %all-gather = bf16[32,48,6]{1,2,0:T(8,128)(2,1)S(1)} all-gather(bf16[1,48,6]{1,2,0:T(8,128)(2,1)S(1)} %bitcast.804), channel_id=1, replica_groups=mesh['rows'=2,'cols'=8,'fsdp'=2] {'rows','cols','fsdp'}, dimensions={0}, use_global_device_ids=true | all-gather | bytes 19008 | tf_op jit(solution)/shard_map/all_gather | solution.py:487
  132.8 42.7 %all_gather.39 = bf16[1536,64]{1,0:T(8,128)(2,1)} all-gather(bf16[48,64]{1,0:T(8,128)(2,1)} %param.30), channel_id=1, replica_groups=mesh['rows'=2,'cols'=8,'fsdp'=2] {'rows','cols','fsdp'}, dimensions={0}, use_global_device_ids=true | all-gather | bytes 202752 | tf_op jit(solution)/shard_map/all_gather | solution.py:486
  221.1 15.3 collective-permute-start.26
  345.0 20.9 all-to-all-done.1
  372.9 24.2 all-to-all-done.2
  417.1 20.1 all-to-all-done
  441.1 78.1 %while.56 = (s32[]{:T(128)}, bf16[2,512,768]{2,1,0:T(8,128)(2,1)}, f32[2,12,512]{2,1,0:T(8,128)S(1)}, s32[2,512]{1,0:T(2,128)S(1)}, bf16[2,512,12,64]{1,3,2,0:T(...) while((s32[]{:T(128)}, bf16[2,512,768]{2,1,0:T(8,128)(2,1)}, ...), condition=%wide.region_9.10_spmd.clone, body=%wide.region_6.9_spmd.clone.sunk | while | flops 1687021568 | bytes 186367344 | solution.py:184
  441.7 12.3 fusion.331
  454.0 12.7 fusion.332
  481.0 12.3 fusion.331
  493.4 12.3 fusion.332
  531.5 21.4 all-to-all-done.3
  573.4 21.9 fusion.228
  634.9 19.0 fusion.154
  662.9 21.9 multiply_reduce_fusion.9
  721.9 172.2 %while.58 = (s32[]{:T(128)}, f32[1024,12,64]{0,2,1:T(8,128)}, f32[1024,12,64]{0,2,1:T(8,128)}, bf16[2,512,768]{2,1,0:T(8,128)(2,1)}, bf16[2,512,12,64]{1,3,2,0:T...) while((s32[]{:T(128)}, f32[1024,12,64]{0,2,1:T(8,128)}, ...), condition=%wide.region_37.38_spmd.clone, body=%wide.region_35.37_spmd.clone.sunk | while | flops 4126140416 | bytes 215417744 | solution.py:229
  734.2 18.1 multiply_reduce_fusion.44
  752.3 21.2 multiply_convert_fusion.12
  794.1 13.1 bitcast_add_fusion.9
  819.1 18.1 multiply_reduce_fusion.44
  837.3 21.2 multiply_convert_fusion.12
  880.0 14.0 bitcast_add_fusion.9
  1077.2 76.1 %while.57 = (s32[]{:T(128)}, bf16[2,512,768]{2,1,0:T(8,128)(2,1)}, f32[2,12,512]{2,1,0:T(8,128)S(1)}, s32[2,512]{1,0:T(2,128)S(1)}, bf16[2,512,12,64]{1,3,2,0:T(...) while((s32[]{:T(128)}, bf16[2,512,768]{2,1,0:T(8,128)(2,1)}, ...), condition=%wide.region_24.25_spmd.clone, body=%wide.region_21.24_spmd.clone.sunk | while | flops 1687021568 | bytes 186367344 | solution.py:184
  1089.6 12.3 fusion.337
  1127.7 12.3 fusion.337
  1195.6 21.5 fusion.230
  1244.9 19.1 fusion.155
  1273.1 21.9 multiply_reduce_fusion.3
  1336.9 171.9 %while.59 = (s32[]{:T(128)}, f32[1024,12,64]{0,2,1:T(8,128)}, f32[1024,12,64]{0,2,1:T(8,128)}, bf16[2,512,768]{2,1,0:T(8,128)(2,1)}, bf16[2,512,12,64]{1,3,2,0:T...) while((s32[]{:T(128)}, f32[1024,12,64]{0,2,1:T(8,128)}, ...), condition=%wide.region_48.49_spmd.clone, body=%wide.region_46.48_spmd.clone.sunk | while | flops 4126140416 | bytes 215417744 | solution.py:229
  1349.1 18.2 multiply_reduce_fusion.45
  1367.3 21.2 multiply_convert_fusion.13
  1409.0 13.1 bitcast_add_fusion.11
  1433.9 18.2 multiply_reduce_fusion.45
  1452.1 21.2 multiply_convert_fusion.13
  1494.6 14.0 bitcast_add_fusion.11
  1536.5 14.9 multiply_reduce_fusion.13
  1619.6 21.6 multiply_dynamic-update-slice_fusion.8
  1669.3 20.4 fusion.92
  1691.6 35.5 %fusion.76 = f32[1536,4608]{1,0:T(8,128)} fusion(bf16[512,1536]{1,0:T(8,128)(2,1)} %bitcast.771, bf16[512,1536]{1,0:T(8,128)(2,1)S(1)} %copy-done.74, bf16[512,1536]{1,0:T(8,128)(2,1)S(1)} %copy-done.73, bf16[512,1536]{1,0:T(8,128)(2,1)} %bitcast.769, bf16[512,1536]{1,0:T(8,128)(2,1)} %get-tuple-element.688, bf16[512,1536]{1,0:T(8,128)(2,1)} %get-tuple-element.689, ...), kind=kOutput, calls=%fused_computation.105 | convolution fusion | flops 14558429184 | bytes 40894464 | tf_op jit(solution)/shard_map/dot_general | solution.py:55
  1764.2 16.3 fusion.207
  1780.5 28.2 convolution_add_fusion
  1810.6 34.2 %fusion.72 = f32[1536,8192]{1,0:T(8,128)} fusion(bf16[512,8192]{1,0:T(8,128)(2,1)} %add_convert_fusion, bf16[512,8192]{1,0:T(8,128)(2,1)} %add_convert_fusion.1, bf16[512,1536]{1,0:T(8,128)(2,1)S(1)} %copy-done.72, bf16[512,1536]{1,0:T(8,128)(2,1)S(1)} %copy-done.70), kind=kOutput, calls=%fused_computation.96 | convolution fusion | flops 25809649664 | bytes 70254592 | tf_op jit(solution)/shard_map/dot_general | solution.py:55
  1942.2 141.2 %reduce-scatter.17.cloned.1.call-done = f32[48,1536]{1,0:T(8,128)} async-done(((f32[1536,1536]{1,0:T(8,128)}), f32[48,1536]{1,0:T(8,128)}) %reduce-scatter.17.cloned.1.call-update) | async-done | bytes 294928 | tf_op jit(solution)/shard_map/reduce_scatter | solution.py:505
  2083.4 252.5 %reduce-scatter.21.cloned.1.call-done = f32[128,1536]{1,0:T(8,128)} async-done(((f32[4096,1536]{1,0:T(8,128)}), f32[128,1536]{1,0:T(8,128)}) %reduce-scatter.21.cloned.1.call-update) | async-done | bytes 786448 | tf_op jit(solution)/shard_map/reduce_scatter | solution.py:498
  2335.9 270.6 %reduce-scatter.15.cloned.1.call-done = f32[48,4608]{1,0:T(8,128)} async-done(((f32[1536,4608]{1,0:T(8,128)}), f32[48,4608]{1,0:T(8,128)}) %reduce-scatter.15.cloned.1.call-update) | async-done | bytes 884752 | tf_op jit(solution)/shard_map/reduce_scatter | solution.py:504
  2606.4 290.3 %reduce-scatter.13.cloned.1.call-done = f32[32,7680]{1,0:T(8,128)} async-done(((f32[1024,7680]{1,0:T(8,128)}), f32[32,7680]{1,0:T(8,128)}) %reduce-scatter.13.cloned.1.call-update) | async-done | bytes 983056 | tf_op jit(solution)/shard_map/reduce_scatter | solution.py:503
  2896.7 438.2 %reduce-scatter.19.cloned.1.call-done = f32[48,8192]{1,0:T(8,128)} async-done(((f32[1536,8192]{1,0:T(8,128)}), f32[48,8192]{1,0:T(8,128)}) %reduce-scatter.19.cloned.1.call-update) | async-done | bytes 1572880 | tf_op jit(solution)/shard_map/reduce_scatter | solution.py:497
  (1191 shorter events, 1122.9 us)
Async XLA Ops:
  7.2 247.9 %all-gather.7.cloned.1.call-start = ((), (), s32[]{:S(2)}) async-start(), calls=%async_computation.24 | async-start | bytes 16220160 | tf_op jit(solution)/shard_map/all_gather | solution.py:481
  7.9 280.3 %all-gather.9.cloned.1.call-start = ((), (), s32[]{:S(2)}) async-start(), calls=%async_computation.25 | async-start | bytes 14598144 | tf_op jit(solution)/shard_map/all_gather | solution.py:482
  8.7 550.3 %all-gather.11.cloned.1.call-start = ((), (), s32[]{:S(2)}) async-start(), calls=%async_computation.26 | async-start | bytes 4866048 | tf_op jit(solution)/shard_map/all_gather | solution.py:483
  9.4 564.0 %all-gather.13.cloned.1.call-start = ((), (), s32[]{:S(2)}) async-start(), calls=%async_computation.27 | async-start | bytes 25952256 | tf_op jit(solution)/shard_map/all_gather | solution.py:484
  10.0 594.1 %all-gather.15.cloned.1.call-start = ((), (), s32[]{:S(2)}) async-start(), calls=%async_computation.28 | async-start | bytes 12976128 | tf_op jit(solution)/shard_map/all_gather | solution.py:485
  11.5 174.9 %collective-permute-start = (bf16[4,1,32]{1,2,0:T(8,128)(2,1)}, bf16[4,1,32]{1,2,0:T(8,128)(2,1)}, u32[]{:S(2)}, u32[]{:S(2)}) collective-permute-start(bf16[4,1,32]{1,2,0:T(8,128)(2,1)} %get-tuple-element.678), channel_id=1, source_target_pairs={{0,16},{1,17},{2,18},{3,19},{4,20},{5,21},{6,22},{7,23},{8,24},{9,... | collective-permute-start | bytes 776 | tf_op jit(solution)/shard_map/ppermute | solution.py:30
  17.0 170.8 %collective-permute-start.1 = (bf16[4,1,32]{1,2,0:T(8,128)(2,1)}, bf16[4,1,32]{1,2,0:T(8,128)(2,1)}, u32[]{:S(2)}, u32[]{:S(2)}) collective-permute-start(bf16[4,1,32]{1,2,0:T(8,128)(2,1)} %get-tuple-element.679), channel_id=1, source_target_pairs={{16,0},{17,1},{18,2},{19,3},{20,4},{21,5},{22,6},{23,7},{24,8},{25... | collective-permute-start | bytes 776 | tf_op jit(solution)/shard_map/ppermute | solution.py:32
  19.0 175.2 %collective-permute-start.8 = (bf16[4,1,32]{1,2,0:T(8,128)(2,1)}, bf16[4,1,32]{1,2,0:T(8,128)(2,1)}, u32[]{:S(2)}, u32[]{:S(2)}) collective-permute-start(bf16[4,1,32]{1,2,0:T(8,128)(2,1)} %get-tuple-element.686), channel_id=1, source_target_pairs={{0,16},{1,17},{2,18},{3,19},{4,20},{5,21},{6,22},{7,23},{8,24},{9,... | collective-permute-start | bytes 776 | tf_op jit(solution)/shard_map/ppermute | solution.py:30
  24.7 170.8 %collective-permute-start.9 = (bf16[4,1,32]{1,2,0:T(8,128)(2,1)}, bf16[4,1,32]{1,2,0:T(8,128)(2,1)}, u32[]{:S(2)}, u32[]{:S(2)}) collective-permute-start(bf16[4,1,32]{1,2,0:T(8,128)(2,1)} %get-tuple-element.687), channel_id=1, source_target_pairs={{16,0},{17,1},{18,2},{19,3},{20,4},{21,5},{22,6},{23,7},{24,8},{25... | collective-permute-start | bytes 776 | tf_op jit(solution)/shard_map/ppermute | solution.py:32
  27.5 169.9 %collective-permute-start.16 = (bf16[4,1,32]{1,2,0:T(8,128)(2,1)}, bf16[4,1,32]{1,2,0:T(8,128)(2,1)}, u32[]{:S(2)}, u32[]{:S(2)}) collective-permute-start(bf16[4,1,32]{1,2,0:T(8,128)(2,1)} %get-tuple-element.672), channel_id=1, source_target_pairs={{0,16},{1,17},{2,18},{3,19},{4,20},{5,21},{6,22},{7,23},{8,24},{9,... | collective-permute-start | bytes 776 | tf_op jit(solution)/shard_map/ppermute | solution.py:30
  186.4 10.9 collective-permute-start.17
  187.7 14.1 collective-permute-start.24
  204.1 15.7 collective-permute-start.2
  206.7 14.4 collective-permute-start.3
  208.8 31.3 collective-permute-start.10
  213.4 28.0 collective-permute-start.11
  214.7 38.5 %collective-permute-start.18 = (bf16[4,66,1]{1,2,0:T(2,128)(2,1)}, bf16[4,66,1]{1,2,0:T(2,128)(2,1)}, u32[]{:S(2)}, u32[]{:S(2)}) collective-permute-start(bf16[4,66,1]{1,2,0:T(2,128)(2,1)} %get-tuple-element.670), channel_id=1, source_target_pairs={{0,2},{2,4},{4,6},{6,8},{8,10},{10,12},{12,14},{1,3},{3,5},{5,7},{... | collective-permute-start | bytes 1592 | tf_op jit(solution)/shard_map/ppermute | solution.py:30
  219.8 33.4 collective-permute-start.19
  221.1 309.4 %collective-permute-start.26 = (bf16[4,66,1]{1,2,0:T(2,128)(2,1)}, bf16[4,66,1]{1,2,0:T(2,128)(2,1)}, u32[]{:S(2)}, u32[]{:S(2)}) collective-permute-start(bf16[4,66,1]{1,2,0:T(2,128)(2,1)} %get-tuple-element.680), channel_id=1, source_target_pairs={{0,2},{2,4},{4,6},{6,8},{8,10},{10,12},{12,14},{1,3},{3,5},{5,7},{... | collective-permute-start | bytes 1592 | tf_op jit(solution)/shard_map/ppermute | solution.py:30
  240.1 290.4 %collective-permute-start.27 = (bf16[4,66,1]{1,2,0:T(2,128)(2,1)}, bf16[4,66,1]{1,2,0:T(2,128)(2,1)}, u32[]{:S(2)}, u32[]{:S(2)}) collective-permute-start(bf16[4,66,1]{1,2,0:T(2,128)(2,1)} %get-tuple-element.681), channel_id=1, source_target_pairs={{2,0},{4,2},{6,4},{8,6},{10,8},{12,10},{14,12},{3,1},{5,3},{7,5},{... | collective-permute-start | bytes 1592 | tf_op jit(solution)/shard_map/ppermute | solution.py:32
  337.0 28.8 all-to-all-start.1
  365.9 31.3 all-to-all-start.2
  397.2 40.0 %all-to-all-start = ((bf16[512,2,768]{2,0,1:T(8,128)(2,1)}), bf16[512,2,768]{2,0,1:T(8,128)(2,1)}, u32[]{:S(2)}, u32[]{:S(2)}) async-start(bf16[512,2,768]{2,0,1:T(8,128)(2,1)} %bitcast.738), calls=%async_computation | async-start | bytes 3145728 | tf_op jit(solution)/shard_map/all_to_all | solution.py:282
  524.5 28.4 all-to-all-start.3
  703.2 15.9 all-to-all-start.8
  900.2 24.4 all-to-all-start.10
  924.6 24.2 all-to-all-start.9
  948.8 87.6 %all-to-all-start.6 = ((bf16[512,2,768]{2,0,1:T(8,128)(2,1)}), bf16[512,2,768]{2,0,1:T(8,128)(2,1)}, u32[]{:S(2)}, u32[]{:S(2)}) async-start(bf16[512,2,768]{2,0,1:T(8,128)(2,1)} %bitcast.734), calls=%async_computation.6 | async-start | bytes 3145728 | tf_op jit(solution)/shard_map/all_to_all | solution.py:296
  1036.5 15.9 all-to-all-start.5
  1052.3 22.0 all-to-all-start.4
  1158.6 16.9 all-to-all-start.7
  1313.4 15.9 all-to-all-start.12
  1329.3 185.6 %all-to-all-start.11 = ((bf16[2,2,196608]{2,1,0:T(2,128)(2,1)}), bf16[2,2,196608]{2,1,0:T(2,128)(2,1)}, u32[]{:S(2)}, u32[]{:S(2)}) async-start(bf16[2,2,196608]{2,1,0:T(2,128)(2,1)} %reshape.1276), calls=%async_computation.11 | async-start | bytes 3145728 | tf_op jit(solution)/shard_map/all_to_all | solution.py:372
  1514.9 16.9 all-to-all-start.14
  1531.8 35.3 %all-to-all-start.13 = ((bf16[2,2,196608]{2,1,0:T(2,128)(2,1)}), bf16[2,2,196608]{2,1,0:T(2,128)(2,1)}, u32[]{:S(2)}, u32[]{:S(2)}) async-start(bf16[2,2,196608]{2,1,0:T(2,128)(2,1)} %reshape.1274), calls=%async_computation.13 | async-start | bytes 3145728 | tf_op jit(solution)/shard_map/all_to_all | solution.py:358
  1567.1 41.6 %all-to-all-start.15 = ((bf16[2,2,196608]{2,1,0:T(2,128)(2,1)}), bf16[2,2,196608]{2,1,0:T(2,128)(2,1)}, u32[]{:S(2)}, u32[]{:S(2)}) async-start(bf16[2,2,196608]{2,1,0:T(2,128)(2,1)} %reshape.1270), calls=%async_computation.15 | async-start | bytes 3145728 | tf_op jit(solution)/shard_map/all_to_all | solution.py:372
  1571.7 360.8 %reduce-scatter.25.cloned.1.call-start = ((), (), s32[]{:S(2)}) async-start(), calls=%async_computation.36 | async-start | bytes 811008
  1642.5 291.5 %reduce-scatter.23.cloned.1.call-start = ((), (), s32[]{:S(2)}) async-start(), calls=%async_computation.35 | async-start | bytes 811008 | tf_op jit(solution)/shard_map/reduce_scatter | solution.py:506
  1646.4 295.8 %reduce-scatter.11.cloned.1.call-start = ((), (), s32[]{:S(2)}) async-start(), calls=%async_computation.29 | async-start | bytes 811008 | tf_op jit(solution)/shard_map/reduce_scatter | solution.py:502
  1658.1 425.3 %reduce-scatter.17.cloned.1.call-start = ((), (), s32[]{:S(2)}) async-start(), calls=%async_computation.32 | async-start | bytes 9732096 | tf_op jit(solution)/shard_map/reduce_scatter | solution.py:505
  1667.5 668.4 %reduce-scatter.21.cloned.1.call-start = ((), (), s32[]{:S(2)}) async-start(), calls=%async_computation.34 | async-start | bytes 25952256 | tf_op jit(solution)/shard_map/reduce_scatter | solution.py:498
  1689.8 916.6 %reduce-scatter.15.cloned.1.call-start = ((), (), s32[]{:S(2)}) async-start(), calls=%async_computation.31 | async-start | bytes 29196288 | tf_op jit(solution)/shard_map/reduce_scatter | solution.py:504
  1727.2 1169.5 %reduce-scatter.13.cloned.1.call-start = ((), (), s32[]{:S(2)}) async-start(), calls=%async_computation.30 | async-start | bytes 32440320 | tf_op jit(solution)/shard_map/reduce_scatter | solution.py:503
  1808.8 1526.1 %reduce-scatter.19.cloned.1.call-start = ((), (), s32[]{:S(2)}) async-start(), calls=%async_computation.33 | async-start | bytes 51904512 | tf_op jit(solution)/shard_map/reduce_scatter | solution.py:497
  1856.7 10.6 collective-permute-start.6
  1900.4 11.5 collective-permute-start.20
  1906.0 10.3 collective-permute-start.28
  1912.1 12.3 collective-permute-start.22
  (248 other events, 4208.4 us)
Sparse Core Ops, SparseCore 0:
  10.9 116.1 all-gather.6
  130.0 103.8 all-gather.8
  236.8 62.5 all-gather.10
  302.2 177.4 all-gather.12
  482.4 99.7 all-gather.14
  1642.6 98.9 reduce-scatter.24
  1747.3 94.5 reduce-scatter.22
  1847.6 94.6 reduce-scatter.10
  1948.7 134.6 reduce-scatter.16
  2091.4 244.4 reduce-scatter.20
  2342.9 263.5 reduce-scatter.14
  2613.3 283.4 reduce-scatter.12
  2903.7 431.1 reduce-scatter.18
where the time goes:
time: 3360 us; the launch traced here: 3340 us
  waiting for transfers between devices  1550 us (46%)
  matrix products  759 us (23%)
  other arithmetic  394 us (12%)
  local copies, waits for them, and re-layouts  331 us (10%)
  starting transfers between devices  170 us (5%)
  blocking collectives  122 us (4%)
    reduce_scatter x1, waiting for transfers between devices, shards(): lax.psum_scatter(ffn_part[0], ('rows', 'cols', 'fsdp'), scatter_dimension...  438 us
    reduce_scatter x1, waiting for transfers between devices, shards(): lax.psum_scatter(other_part[1], ('rows', 'cols', 'fsdp'), scatter_dimensi...  290 us
    reduce_scatter x1, waiting for transfers between devices, shards(): lax.psum_scatter(other_part[2], ('rows', 'cols', 'fsdp'), scatter_dimensi...  271 us
    reduce_scatter x1, waiting for transfers between devices, shards(): lax.psum_scatter(ffn_part[1], ('rows', 'cols', 'fsdp'), scatter_dimension...  252 us
    reduce_scatter x1, waiting for transfers between devices, shards(): lax.psum_scatter(other_part[3], ('rows', 'cols', 'fsdp'), scatter_dimensi...  141 us
    dot_general x12, matrix products, contract_last(): lax.dot_general(left, right, (((1,), (1,)), ((), ())), preferred_element_...  140 us
    dot_general x6, matrix products, contract_first(): lax.dot_general(left, right, (((0,), (0,)), ((), ())), preferred_element_...  105 us
    unnamed x554, local copies, waits for them, and re-layouts  97.7 us
  transfers between devices with their start and end apart: 61, of which 21 were waited for; matrix products, arithmetic and copies ran while one was open for 27% of the time, Pallas kernels for 0%

commit v1 on v0

v1 whole, which is shorter than its diff:
```python
from functools import partial

import jax
import jax.numpy as jnp
from jax import lax
from jax.experimental import pallas as pl
from jax.experimental.pallas import tpu as pltpu
from jax.sharding import PartitionSpec as P

D = 1536
HEADS = 24
HD = 64
FF = 4096
CHANNELS = 4
PIN = 64
IMGS = 4
CELL = 16
LANES = 128
ALL = ("rows", "cols", "fsdp")

epsilon = 1e-06
highest = lax.Precision.HIGHEST
mask_level = 256.0
f32 = jnp.float32
bf16 = jnp.bfloat16
vmem_bytes = 60 * 1024 * 1024


def dot_nn(left, right):
    return lax.dot_general(left, right, (((1,), (0,)), ((), ())), preferred_element_type=f32)


def dot_nt(left, right):
    return lax.dot_general(left, right, (((1,), (1,)), ((), ())), preferred_element_type=f32)


def dot_tn(left, right):
    return lax.dot_general(left, right, (((0,), (0,)), ((), ())), preferred_element_type=f32)


def row_mean(values):
    return jnp.mean(values, axis=-1, keepdims=True)


def inverse_rms(values):
    return lax.rsqrt(row_mean(values * values) + epsilon)


def whole(shape):
    zeros = (0,) * len(shape)
    return pl.BlockSpec(shape, lambda i: zeros, pipeline_mode=pl.Buffered(1))


def picked(image, table):
    choice = table[IMGS - 1 : IMGS, :]
    for index in range(IMGS - 2, -1, -1):
        choice = jnp.where(image == index, table[index : index + 1, :], choice)
    return choice


def image_sums(onehot, product):
    upper = product.astype(bf16)
    lower = (product - upper.astype(f32)).astype(bf16)
    return dot_nn(onehot, upper) + dot_nn(onehot, lower)


def matmul_rows(
    name, lefts, weight, kind, tile, row_ins, consts, row_outs, sum_rows, chunk_body,
    before=None, after=None, block_scratch=(), flops=0,
):
    tokens = lefts[0].shape[0]
    width = weight.shape[1] if kind == "nn" else weight.shape[0]
    depth = weight.shape[0] if kind == "nn" else weight.shape[1]
    block = min(256, tokens)
    chunk = 32
    tiles = width // tile
    blocks = tokens // block
    counts = (len(lefts), len(row_ins), len(consts), len(row_outs), len(sum_rows))

    def kernel(*refs):
        refs = list(refs)
        take = lambda n: [refs.pop(0) for _ in range(n)]
        left_refs = take(counts[0])
        weight_ref = take(1)[0]
        in_refs, const_refs = take(counts[1]), take(counts[2])
        out_refs, sum_refs = take(counts[3]), take(counts[4])
        total = refs.pop(0)
        scratch = refs
        step = pl.program_id(0)

        @pl.when(step < tiles)
        def _():
            offset = 0
            value = None
            for left in left_refs:
                size = left.shape[1]
                if kind == "nn":
                    term = dot_nn(left[...], weight_ref[offset : offset + size, :])
                else:
                    term = dot_nt(left[...], weight_ref[:, offset : offset + size])
                value = term if value is None else value + term
                offset += size
            total[:, pl.ds(pl.multiple_of(step * tile, tile), tile)] = value

        @pl.when(step == tiles)
        def _():
            for ref in sum_refs:
                ref[...] = jnp.zeros_like(ref)

        @pl.when(step >= tiles)
        def _():
            start = pl.multiple_of((step - tiles) * block, block)
            if before is not None:
                before(in_refs, const_refs, out_refs, scratch)

            def one(index, carry):
                low = pl.multiple_of(index * chunk, chunk)
                rows = pl.ds(low, chunk)
                chunk_body(
                    total[pl.ds(pl.multiple_of(start + low, chunk), chunk), :],
                    rows, in_refs, const_refs, out_refs, scratch,
                )
                return carry

            lax.fori_loop(0, block // chunk, one, 0)
            if after is not None:
                after(in_refs, const_refs, out_refs, sum_refs, scratch)

    def row_map(i):
        return (jnp.maximum(i - tiles, 0), 0)

    def col_map(i):
        return (0, jnp.maximum(i - tiles, 0))

    weight_shape = (depth, tile) if kind == "nn" else (tile, depth)
    if kind == "nn":
        weight_spec = pl.BlockSpec(weight_shape, lambda i: (0, jnp.minimum(i, tiles - 1)))
    else:
        weight_spec = pl.BlockSpec(weight_shape, lambda i: (jnp.minimum(i, tiles - 1), 0))
    in_specs = [whole(left.shape) for left in lefts] + [weight_spec]
    for array in row_ins:
        if array.shape[0] == tokens:
            in_specs.append(pl.BlockSpec((block, array.shape[1]), row_map))
        else:
            in_specs.append(pl.BlockSpec((array.shape[0], block), col_map))
    in_specs += [whole(array.shape) for array in consts]
    out_specs = [pl.BlockSpec((block, cols), row_map) for cols, _ in row_outs]
    out_specs += [pl.BlockSpec((count, width), lambda i: (0, 0)) for count in sum_rows]
    out_shape = [jax.ShapeDtypeStruct((tokens, cols), kind_) for cols, kind_ in row_outs]
    out_shape += [jax.ShapeDtypeStruct((count, width), f32) for count in sum_rows]
    return pl.pallas_call(
        kernel,
        grid=(tiles + blocks,),
        in_specs=in_specs,
        out_specs=out_specs,
        out_shape=out_shape,
        scratch_shapes=[pltpu.VMEM((tokens, width), f32)]
        + [pltpu.VMEM((block, cols), kind_) for cols, kind_ in block_scratch],
        compiler_params=pltpu.CompilerParams(vmem_limit_bytes=vmem_bytes),
        cost_estimate=pl.CostEstimate(
            flops=2 * tokens * width * depth,
            bytes_accessed=2 * (width * depth + tokens * depth) + 8 * tokens * width,
            transcendentals=0,
        ),
        name=name,
    )(*lefts, weight, *row_ins, *consts)


def swapped(values, first):
    return jnp.where(first, pltpu.roll(values, LANES - 16, 1), pltpu.roll(values, 16, 1))


def first_lanes(rows):
    lane = lax.broadcasted_iota(jnp.int32, (rows, LANES), 1)
    return lax.rem(lane, 32) < 16


def project_rows(patches, image, cosine, sine, w_embed, pre_table, weights, gains, place):
    tokens = patches.shape[0]
    chunk = 32
    tile = 256
    blocks = D // tile
    pieces = place is not None
    count = len(weights)
    share = 0 if not pieces else D // len(place[1][0])

    def kernel(*refs):
        refs = list(refs)
        patches_ref, image_ref, cos_ref, sin_ref, embed_ref, pre_ref, gain_ref = refs[:7]
        weight_refs = refs[7 : 7 + count]
        rest = refs[7 + count :]
        if pieces:
            me_ref, embedded_ref, normed_ref, out_ref, hat_ref, inverse_ref = rest[:6]
            weight_ref, total, sems = rest[6:]
        else:
            embedded_ref, normed_ref, out_ref, hat_ref, inverse_ref, total = rest
            weight_ref = weight_refs[0]
        step = pl.program_id(0)

        def copies(part):
            half = len(place[1][part]) // 2
            listed = []
            for index, mask in enumerate(place[1][part]):
                low = pl.multiple_of((me_ref[0] ^ mask) * share, share)
                source = weight_refs[2 * part + index // half]
                listed.append(
                    pltpu.make_async_copy(
                        source.at[pl.ds((index % half) * share, share), :],
                        weight_ref.at[pl.ds(low, share), :],
                        sems.at[index],
                    )
                )
            return listed

        if pieces:
            for part in range(3):

                @pl.when(step == part)
                def _():
                    for copy in copies(part):
                        copy.start()

        @pl.when(step == 0)
        def _():
            total[...] = dot_nt(patches_ref[...], embed_ref[...])

            def one(index, carry):
                rows = pl.ds(pl.multiple_of(index * chunk, chunk), chunk)
                value = total[rows, :]
                embedded_ref[rows, :] = value
                normed_ref[rows, :] = (
                    value * inverse_rms(value) * picked(image_ref[rows, :1], pre_ref[...])
                ).astype(bf16)
                return carry

            lax.fori_loop(0, tokens // chunk, one, 0)

        if pieces:
            for part in range(3):

                @pl.when(step == part)
                def _():
                    for copy in copies(part):
                        copy.wait()

        for index in range(blocks):
            cols = slice(index * tile, (index + 1) * tile)
            total[:, cols] = dot_nn(normed_ref[...], weight_ref[:, cols])

        @pl.when(step < 2)
        def _():
            gain = gain_ref[pl.ds(step, 1), :]

            def one(index, carry):
                rows = pl.ds(pl.multiple_of(index * chunk, chunk), chunk)
                value = total[rows, :]
                inverse = inverse_rms(value)
                hat = value * inverse
                hat_ref[rows, :] = hat.astype(bf16)
                inverse_ref[rows, :] = jnp.broadcast_to(inverse, (chunk, LANES))
                scaled = hat * gain
                first = first_lanes(chunk)
                cos_rows = cos_ref[rows, :]
                sin_rows = sin_ref[rows, :]
                for lane in range(0, D, LANES):
                    part = scaled[:, lane : lane + LANES]
                    turned = part * cos_rows + swapped(part, first) * sin_rows
                    out_ref[rows, lane : lane + LANES] = turned.astype(bf16)
                return carry

            lax.fori_loop(0, tokens // chunk, one, 0)

        @pl.when(step == 2)
        def _():
            out_ref[...] = total[...].astype(bf16)

    weight_specs = [pl.BlockSpec((D, D), lambda i: (0, i))]
    if pieces:
        weight_specs = [pl.BlockSpec(memory_space=pl.ANY)] * count
        weight_specs.append(pl.BlockSpec(memory_space=pltpu.SMEM))
        weights = list(weights) + [place[0]]
    out_specs = [
        pl.BlockSpec((tokens, D), lambda i: (0, 0), pipeline_mode=pl.Buffered(1)),
        pl.BlockSpec((tokens, D), lambda i: (0, 0), pipeline_mode=pl.Buffered(1)),
        pl.BlockSpec((tokens, D), lambda i: (0, i)),
        pl.BlockSpec((tokens, D), lambda i: (0, jnp.minimum(i, 1))),
        pl.BlockSpec((tokens, LANES), lambda i: (0, jnp.minimum(i, 1))),
    ]
    out_shape = [
        jax.ShapeDtypeStruct((tokens, D), f32),
        jax.ShapeDtypeStruct((tokens, D), bf16),
        jax.ShapeDtypeStruct((tokens, 3 * D), bf16),
        jax.ShapeDtypeStruct((tokens, 2 * D), bf16),
        jax.ShapeDtypeStruct((tokens, 2 * LANES), f32),
    ]
    scratch = [pltpu.VMEM((tokens, D), f32)]
    if pieces:
        out_specs.append(pl.BlockSpec((D, D), lambda i: (0, i)))
        out_shape.append(jax.ShapeDtypeStruct((D, 3 * D), bf16))
        scratch.append(pltpu.SemaphoreType.DMA((len(place[1][0]),)))
    results = pl.pallas_call(
        kernel,
        grid=(3,),
        in_specs=[
            whole(patches.shape),
            whole(image.shape),
            whole(cosine.shape),
            whole(sine.shape),
            whole(w_embed.shape),
            whole(pre_table.shape),
            whole(gains.shape),
        ]
        + weight_specs,
        out_specs=out_specs,
        out_shape=out_shape,
        scratch_shapes=scratch,
        compiler_params=pltpu.CompilerParams(vmem_limit_bytes=vmem_bytes),
        cost_estimate=pl.CostEstimate(
            flops=6 * tokens * D * D, bytes_accessed=6 * D * D + 24 * tokens * D, transcendentals=0
        ),
        name="project_rows",
    )(patches, image, cosine, sine, w_embed, pre_table, gains, *weights)
    return list(results) + ([] if pieces else [weights[0]])


def attention_grads(which, normed, project_back, attended, attn_back, place):
    tokens = normed.shape[0]
    tile = 256
    tiles = D // tile
    side = D // 3
    masks = place[1][which]
    share = D // len(masks)

    def kernel(left_ref, back_ref, other_ref, attn_ref, me_ref, out_ref, held, sems):
        step = pl.program_id(0)
        rows = pl.ds(pl.multiple_of(step * tile, tile), tile)
        held[rows, :D] = dot_tn(left_ref[...], back_ref[...]).astype(bf16)
        held[rows, D:] = dot_tn(other_ref[...], attn_ref[...]).astype(bf16)

        @pl.when(step == tiles - 1)
        def _():
            listed = []
            for index, mask in enumerate(masks):
                low = pl.multiple_of((me_ref[0] ^ mask) * share, share)
                listed.append(
                    pltpu.make_async_copy(
                        held.at[pl.ds(low, share), :],
                        out_ref.at[pl.ds(index * share, share), :],
                        sems.at[index],
                    )
                )
            for copy in listed:
                copy.start()
            for copy in listed:
                copy.wait()

    return pl.pallas_call(
        kernel,
        grid=(tiles,),
        in_specs=[
            pl.BlockSpec((tokens, tile), lambda i: (0, i)),
            pl.BlockSpec((tokens, D), lambda i: (0, which), pipeline_mode=pl.Buffered(1)),
            pl.BlockSpec((tokens, tile), lambda i: (0, i)),
            pl.BlockSpec((tokens, side), lambda i: (0, which), pipeline_mode=pl.Buffered(1)),
            pl.BlockSpec(memory_space=pltpu.SMEM),
        ],
        out_specs=pl.BlockSpec(memory_space=pl.ANY),
        out_shape=jax.ShapeDtypeStruct((D, D + side), bf16),
        scratch_shapes=[
            pltpu.VMEM((D, D + side), bf16),
            pltpu.SemaphoreType.DMA((len(masks),)),
        ],
        compiler_params=pltpu.CompilerParams(vmem_limit_bytes=vmem_bytes),
        cost_estimate=pl.CostEstimate(
            flops=2 * tokens * D * (D + side),
            bytes_accessed=2 * D * (D + side) + 8 * tokens * D,
            transcendentals=0,
        ),
        name="attention_grads",
    )(normed, project_back, attended, attn_back, place[0])


def head_lanes(shape, axis, head):
    lane = lax.broadcasted_iota(jnp.int32, shape, axis)
    return (lane >= HD) == (head == 1)


def attend(queries, keys, values, spec_of, width, query_image, key_image):
    length = queries.shape[0]
    pairs = width // LANES
    part = min(256, length)

    def kernel(q_ref, k_ref, v_ref, qi_ref, ki_ref, out_ref, log_ref):
        key_block = k_ref[...]
        value_turned = v_ref[...].T
        key_parts = []
        value_parts = []
        for head in range(2):
            mine = head_lanes((length, LANES), 1, head)
            key_parts.append(jnp.where(mine, key_block, ki_ref[...]))
            value_parts.append(
                jnp.where(head_lanes((LANES, length), 0, head), value_turned, jnp.ones((), bf16))
            )

        def one(index, carry):
            rows = pl.ds(pl.multiple_of(index * part, part), part)
            query = q_ref[rows, :] * jnp.asarray(HD ** (-0.5), bf16)
            turned = []
            for head in range(2):
                mine = head_lanes((part, LANES), 1, head)
                scores = dot_nt(key_parts[head], jnp.where(mine, query, qi_ref[rows, :]))
                top = jnp.max(scores, axis=0, keepdims=True)
                raised = jnp.exp(scores - top).astype(bf16)
                result = dot_nn(value_parts[head], raised)
                lane = HD * (1 - head)
                count = result[lane : lane + 1, :]
                turned.append(result[head * HD : (head + 1) * HD, :] / count)
                log_ref[0, pl.ds(head, 1), rows] = top + jnp.log(count)
            out_ref[rows, :] = jnp.concatenate(turned, axis=0).T.astype(bf16)
            return carry

        lax.fori_loop(0, length // part, one, 0)

    return pl.pallas_call(
        kernel,
        grid=(pairs,),
        in_specs=[
            pl.BlockSpec((length, LANES), spec_of(0)),
            pl.BlockSpec((length, LANES), spec_of(1)),
            pl.BlockSpec((length, LANES), spec_of(2)),
            whole(query_image.shape),
            whole(key_image.shape),
        ],
        out_specs=[
            pl.BlockSpec((length, LANES), lambda i: (0, i)),
            pl.BlockSpec((1, 2, length), lambda i: (i, 0, 0)),
        ],
        out_shape=[
            jax.ShapeDtypeStruct((length, width), bf16),
            jax.ShapeDtypeStruct((pairs, 2, length), f32),
        ],
        compiler_params=pltpu.CompilerParams(vmem_limit_bytes=vmem_bytes),
        cost_estimate=pl.CostEstimate(
            flops=16 * pairs * length * length * HD * 4,
            bytes_accessed=8 * length * width,
            transcendentals=2 * pairs * length * length,
        ),
        name="attend",
    )(queries, keys, values, query_image, key_image)


def attend_back(
    queries, keys, values, spec_of, width, attended, grads, log_total, query_image, key_image
):
    length = queries.shape[0]
    pairs = width // LANES
    part = min(256, length)
    score_scale = HD ** (-0.5)

    def kernel(
        q_ref, k_ref, v_ref, o_ref, g_ref, log_ref, qi_ref, ki_ref,
        dq_ref, dk_ref, dv_ref, key_sum, value_sum,
    ):
        key_block = k_ref[...]
        value_block = v_ref[...]
        key_turned = key_block.T
        key_parts = []
        value_parts = []
        for head in range(2):
            mine = head_lanes((length, LANES), 1, head)
            key_parts.append(jnp.where(mine, key_block, ki_ref[...]))
            value_parts.append(jnp.where(mine, value_block, jnp.zeros((), bf16)))
        key_sum[...] = jnp.zeros_like(key_sum)
        value_sum[...] = jnp.zeros_like(value_sum)
        sel_rows = lax.broadcasted_iota(jnp.int32, (8, LANES), 0)
        sel_lanes = lax.broadcasted_iota(jnp.int32, (8, LANES), 1)
        select = jnp.where(
            sel_rows == jnp.where(sel_lanes >= HD, 1, 0), jnp.ones((), f32), jnp.zeros((), f32)
        ).astype(bf16)

        def one(index, carry):
            rows = pl.ds(pl.multiple_of(index * part, part), part)
            query = q_ref[rows, :] * jnp.asarray(score_scale, bf16)
            grad = g_ref[rows, :]
            product = grad.astype(f32) * o_ref[rows, :].astype(f32)
            upper = product.astype(bf16)
            lower = (product - upper.astype(f32)).astype(bf16)
            inner = dot_nt(select, upper) + dot_nt(select, lower)
            turned = []
            for head in range(2):
                mine = head_lanes((part, LANES), 1, head)
                scores = dot_nt(key_parts[head], jnp.where(mine, query, qi_ref[rows, :]))
                chances = jnp.exp(scores - log_ref[0, pl.ds(head, 1), rows])
                grad_chances = dot_nt(value_parts[head], grad)
                grad_scores = (chances * (grad_chances - inner[head : head + 1, :])).astype(bf16)
                value_sum[head] += dot_nn(chances.astype(bf16), grad)
                key_sum[head] += dot_nn(grad_scores, query)
                result = dot_nn(key_turned, grad_scores)
                turned.append(result[head * HD : (head + 1) * HD, :])
            dq_ref[rows, :] = (jnp.concatenate(turned, axis=0).T * score_scale).astype(bf16)
            return carry

        lax.fori_loop(0, length // part, one, 0)
        lower_lanes = head_lanes((length, LANES), 1, 0)
        dk_ref[...] = jnp.where(lower_lanes, key_sum[0], key_sum[1]).astype(bf16)
        dv_ref[...] = jnp.where(lower_lanes, value_sum[0], value_sum[1]).astype(bf16)

    column = pl.BlockSpec((length, LANES), lambda i: (0, i))
    return pl.pallas_call(
        kernel,
        grid=(pairs,),
        in_specs=[
            pl.BlockSpec((length, LANES), spec_of(0)),
            pl.BlockSpec((length, LANES), spec_of(1)),
            pl.BlockSpec((length, LANES), spec_of(2)),
            column,
            column,
            pl.BlockSpec((1, 2, length), lambda i: (i, 0, 0)),
            whole(query_image.shape),
            whole(key_image.shape),
        ],
        out_specs=[column] * 3,
        out_shape=[jax.ShapeDtypeStruct((length, width), bf16)] * 3,
        scratch_shapes=[
            pltpu.VMEM((2, length, LANES), f32),
            pltpu.VMEM((2, length, LANES), f32),
        ],
        compiler_params=pltpu.CompilerParams(vmem_limit_bytes=vmem_bytes),
        cost_estimate=pl.CostEstimate(
            flops=40 * pairs * length * length * HD * 4,
            bytes_accessed=16 * length * width,
            transcendentals=2 * pairs * length * length,
        ),
        name="attend_back",
    )(queries, keys, values, attended, grads, log_total, query_image, key_image)


def gate_up_rows(normed, weight):
    tokens = normed.shape[0]
    tile = 256
    tiles = FF // tile
    chunk = 64

    def kernel(left_ref, gate_weight, up_weight, hidden_ref, gate_ref, up_ref, gate_sum, up_sum):
        gate_sum[...] = dot_nn(left_ref[...], gate_weight[...])
        up_sum[...] = dot_nn(left_ref[...], up_weight[...])

        def one(index, carry):
            rows = pl.ds(pl.multiple_of(index * chunk, chunk), chunk)
            gate = gate_sum[rows, :]
            up = up_sum[rows, :]
            hidden_ref[rows, :] = (gate / (1.0 + jnp.exp(-gate)) * up).astype(bf16)
            gate_ref[rows, :] = gate.astype(bf16)
            up_ref[rows, :] = up.astype(bf16)
            return carry

        lax.fori_loop(0, tokens // chunk, one, 0)

    out = pl.BlockSpec((tokens, tile), lambda i: (0, i))
    return pl.pallas_call(
        kernel,
        grid=(tiles,),
        in_specs=[
            whole(normed.shape),
            pl.BlockSpec((D, tile), lambda i: (0, i)),
            pl.BlockSpec((D, tile), lambda i: (0, i + tiles)),
        ],
        out_specs=[out] * 3,
        out_shape=[jax.ShapeDtypeStruct((tokens, FF), bf16)] * 3,
        scratch_shapes=[pltpu.VMEM((tokens, tile), f32), pltpu.VMEM((tokens, tile), f32)],
        compiler_params=pltpu.CompilerParams(vmem_limit_bytes=vmem_bytes),
        cost_estimate=pl.CostEstimate(
            flops=4 * tokens * D * FF, bytes_accessed=4 * D * FF + 6 * tokens * FF, transcendentals=0
        ),
        name="gate_up_rows",
    )(normed, weight, weight)


def gate_up_back(ffn_back, weight, gate, up):
    tokens = ffn_back.shape[0]
    tile = 256
    tiles = FF // tile
    chunk = 64

    def kernel(left_ref, weight_ref, gate_ref, up_ref, gate_back, up_back, total):
        total[...] = dot_nt(left_ref[...], weight_ref[...])

        def one(index, carry):
            rows = pl.ds(pl.multiple_of(index * chunk, chunk), chunk)
            grad = total[rows, :]
            gate_rows = gate_ref[rows, :].astype(f32)
            share = 1.0 / (1.0 + jnp.exp(-gate_rows))
            active = gate_rows * share
            up_back[rows, :] = (grad * active).astype(bf16)
            slope = share + active * (1.0 - share)
            gate_back[rows, :] = (grad * up_ref[rows, :].astype(f32) * slope).astype(bf16)
            return carry

        lax.fori_loop(0, tokens // chunk, one, 0)

    column = pl.BlockSpec((tokens, tile), lambda i: (0, i))
    return pl.pallas_call(
        kernel,
        grid=(tiles,),
        in_specs=[
            whole(ffn_back.shape),
            pl.BlockSpec((tile, D), lambda i: (i, 0)),
            column,
            column,
        ],
        out_specs=[column] * 2,
        out_shape=[jax.ShapeDtypeStruct((tokens, FF), bf16)] * 2,
        scratch_shapes=[pltpu.VMEM((tokens, tile), f32)],
        compiler_params=pltpu.CompilerParams(vmem_limit_bytes=vmem_bytes),
        cost_estimate=pl.CostEstimate(
            flops=2 * tokens * D * FF, bytes_accessed=2 * D * FF + 8 * tokens * FF, transcendentals=0
        ),
        name="gate_up_back",
    )(ffn_back, weight, gate, up)


def output_rows(attended, weight, embedded, image, post_table, pre_table):
    def body(value, rows, ins, consts, outs, scratch):
        hat = value * inverse_rms(value)
        image_rows = ins[1][rows, :1]
        mixed = ins[0][rows, :] + picked(image_rows, consts[0][...]) * hat
        outs[0][rows, :] = value
        outs[1][rows, :] = mixed
        outs[2][rows, :] = (
            mixed * inverse_rms(mixed) * picked(image_rows, consts[1][...])
        ).astype(bf16)

    return matmul_rows(
        "output_rows", [attended], weight, "nn", 256, [embedded, image], [post_table, pre_table],
        [(D, f32), (D, f32), (D, bf16)], [], body,
    )


def down_rows(hidden, weight, mixed, image, onehot, grad_patches, post_table, out_table, w_final):
    def before(ins, consts, outs, scratch):
        scratch[0][...] = dot_nt(ins[3][...], consts[2][...])

    def body(value, rows, ins, consts, outs, scratch):
        inverse = inverse_rms(value)
        hat = value * inverse
        image_rows = ins[1][rows, :1]
        post = picked(image_rows, consts[0][...])
        final_state = ins[0][rows, :] + post * hat
        centred = final_state - row_mean(final_state)
        spread = inverse_rms(centred)
        levelled = centred * spread
        scale = picked(image_rows, consts[1][...])
        outs[0][rows, :] = (levelled * scale).astype(bf16)
        grad = scratch[0][rows, :]
        scratch[1][rows, :] = grad * levelled
        back = grad * scale
        late = spread * (back - row_mean(back) - levelled * row_mean(back * levelled))
        outs[1][rows, :] = late
        scratch[2][rows, :] = late * hat
        back = late * post
        outs[2][rows, :] = (inverse * (back - hat * row_mean(back * hat))).astype(bf16)

    def after(ins, consts, outs, sums, scratch):
        outs[3][...] = dot_nn(outs[0][...], consts[2][...]).astype(bf16)
        one = ins[2][...]
        sums[0][...] += image_sums(one, scratch[1][...])
        sums[1][...] += image_sums(one, scratch[2][...])

    return matmul_rows(
        "down_rows", [hidden], weight, "nn", 256, [mixed, image, onehot, grad_patches],
        [post_table, out_table, w_final],
        [(D, bf16), (D, f32), (D, bf16), (PIN, bf16)], [8, 8], body,
        before=before, after=after, block_scratch=[(D, f32)] * 3,
    )


def ffn_back_rows(
    gate_back, up_back, weight, late, mixed, attn_out, image, onehot, post_table, pre_table
):
    def body(value, rows, ins, consts, outs, scratch):
        image_rows = ins[3][rows, :1]
        mixed_rows = ins[1][rows, :]
        inverse = inverse_rms(mixed_rows)
        hat = mixed_rows * inverse
        scratch[0][rows, :] = value * hat
        back = value * picked(image_rows, consts[1][...])
        early = ins[0][rows, :] + inverse * (back - hat * row_mean(back * hat))
        outs[0][rows, :] = early
        attn_rows = ins[2][rows, :]
        inverse = inverse_rms(attn_rows)
        hat = attn_rows * inverse
        scratch[1][rows, :] = early * hat
        back = early * picked(image_rows, consts[0][...])
        outs[1][rows, :] = (inverse * (back - hat * row_mean(back * hat))).astype(bf16)

    def after(ins, consts, outs, sums, scratch):
        one = ins[4][...]
        sums[0][...] += image_sums(one, scratch[0][...])
        sums[1][...] += image_sums(one, scratch[1][...])

    return matmul_rows(
        "ffn_back_rows", [gate_back, up_back], weight, "nt", 256,
        [late, mixed, attn_out, image, onehot], [post_table, pre_table],
        [(D, f32), (D, bf16)], [8, 8], body, after=after, block_scratch=[(D, f32)] * 2,
    )


def project_back_rows(
    project_back, weight, embedded, late, image, onehot, pre_table, w_embed
):
    def body(value, rows, ins, consts, outs, scratch):
        embedded_rows = ins[0][rows, :]
        inverse = inverse_rms(embedded_rows)
        hat = embedded_rows * inverse
        scratch[0][rows, :] = value * hat
        back = value * picked(ins[2][rows, :1], consts[0][...])
        early = inverse * (back - hat * row_mean(back * hat))
        outs[0][rows, :] = (early + ins[1][rows, :]).astype(bf16)

    def after(ins, consts, outs, sums, scratch):
        outs[1][...] = dot_nn(outs[0][...], consts[1][...]).astype(bf16)
        sums[0][...] += image_sums(ins[3][...], scratch[0][...])

    return matmul_rows(
        "project_back_rows", [project_back], weight, "nt", 256,
        [embedded, late, image, onehot], [pre_table, w_embed],
        [(D, bf16), (PIN, bf16)], [8], body, after=after, block_scratch=[(D, f32)],
    )


def turn_back(grad_q, grad_k, hats, inverses, cosine, sine, gains):
    tokens = grad_q.shape[0]
    block = min(256, tokens)
    chunk = 32

    def kernel(gq_ref, gk_ref, hat_ref, inv_ref, cos_ref, sin_ref, gain_ref, out_ref, sum_ref):
        @pl.when(pl.program_id(0) == 0)
        def _():
            sum_ref[...] = jnp.zeros_like(sum_ref)

        for which, grad_ref in enumerate((gq_ref, gk_ref)):
            gain = gain_ref[which : which + 1, :]

            def one(index, carry):
                rows = pl.ds(pl.multiple_of(index * chunk, chunk), chunk)
                first = first_lanes(chunk)
                cos_rows = cos_ref[rows, :]
                sin_rows = sin_ref[rows, :]
                pieces = []
                for lane in range(0, D, LANES):
                    part = grad_ref[rows, lane : lane + LANES].astype(f32)
                    pieces.append(part * cos_rows - swapped(part, first) * sin_rows)
                turned = jnp.concatenate(pieces, axis=1)
                hat = hat_ref[rows, which * D : (which + 1) * D].astype(f32)
                inverse = inv_ref[rows, which * LANES : which * LANES + 1]
                back = turned * gain
                out_ref[rows, which * D : (which + 1) * D] = (
                    inverse * (back - hat * row_mean(back * hat))
                ).astype(bf16)
                return carry + jnp.sum((turned * hat).reshape(chunk // 8, 8, D), axis=0)

            total = lax.fori_loop(0, block // chunk, one, jnp.zeros((8, D), f32))
            sum_ref[which : which + 1, :] += jnp.sum(total, axis=0, keepdims=True)

    row = lambda cols: pl.BlockSpec((block, cols), lambda i: (i, 0))
    return pl.pallas_call(
        kernel,
        grid=(tokens // block,),
        in_specs=[
            row(D), row(D), row(2 * D), row(2 * LANES), row(LANES), row(LANES), whole(gains.shape)
        ],
        out_specs=[row(2 * D), pl.BlockSpec((8, D), lambda i: (0, 0))],
        out_shape=[
            jax.ShapeDtypeStruct((tokens, 2 * D), bf16),
            jax.ShapeDtypeStruct((8, D), f32),
        ],
        compiler_params=pltpu.CompilerParams(vmem_limit_bytes=vmem_bytes),
        cost_estimate=pl.CostEstimate(
            flops=40 * tokens * D, bytes_accessed=12 * tokens * D, transcendentals=0
        ),
        name="turn_back",
    )(grad_q, grad_k, hats, inverses, cosine, sine, gains)


def to_strips(tiles):
    micros = tiles.shape[0]
    count = lax.axis_size("rows")
    parts = count // micros
    me = lax.axis_index("rows")
    slots = []
    for shift in range(micros):
        pairs = [(q, ((q % micros - shift) % micros) * parts + q // micros) for q in range(count)]
        sent = lax.dynamic_index_in_dim(tiles, (me % micros - shift) % micros, 0, keepdims=False)
        if any(a != b for a, b in pairs):
            sent = lax.ppermute(sent, "rows", pairs)
        slots.append(sent)
    stacked = jnp.stack(slots)
    order = (jnp.arange(micros) - me // parts) % micros
    ordered = jnp.concatenate(
        [lax.dynamic_index_in_dim(stacked, order[d], 0) for d in range(micros)], axis=0
    )
    kinds, height, width = ordered.shape[1:]
    return ordered.transpose(1, 0, 2, 3).reshape(kinds, micros * height, width)


def from_strips(strip, micros):
    count = lax.axis_size("rows")
    parts = count // micros
    me = lax.axis_index("rows")
    kinds, height, width = strip.shape
    tiles = strip.reshape(kinds, micros, height // micros, width).transpose(1, 0, 2, 3)
    slots = []
    for shift in range(micros):
        pairs = [(((q % micros - shift) % micros) * parts + q // micros, q) for q in range(count)]
        sent = lax.dynamic_index_in_dim(tiles, (me // parts + shift) % micros, 0, keepdims=False)
        if any(a != b for a, b in pairs):
            sent = lax.ppermute(sent, "rows", pairs)
        slots.append(sent)
    stacked = jnp.stack(slots)
    return jnp.concatenate(
        [
            lax.dynamic_index_in_dim(stacked, (me % micros - m) % micros, 0)
            for m in range(micros)
        ],
        axis=0,
    )


def neighbour_pairs(axis, parts):
    count = lax.axis_size(axis)
    ups = [(i, i + 1) for i in range(count - 1) if (i + 1) % parts != 0]
    return ups, [(b, a) for a, b in ups]


def neighbours(values, axis, dim, parts):
    ups, downs = neighbour_pairs(axis, parts)
    head = lax.slice_in_dim(values, 0, 1, axis=dim)
    tail = lax.slice_in_dim(values, values.shape[dim] - 1, values.shape[dim], axis=dim)
    if len(ups) == 0:
        return jnp.zeros_like(head), jnp.zeros_like(tail)
    return lax.ppermute(tail, axis, ups), lax.ppermute(head, axis, downs)


def sides(parts):
    return (("cols", 1, lax.axis_size("cols")), ("rows", 0, parts))


def extract_patches(strip, parts):
    for axis, dim, span in sides(parts):
        before, after = neighbours(strip, axis, dim + 1, span)
        strip = jnp.concatenate([before, strip, after], axis=dim + 1)
    kinds, height, width = strip.shape
    sets = kinds // CHANNELS
    rows, cols = height // 2 - 1, width // 2 - 1
    cells = (
        strip.reshape(sets, CHANNELS, rows + 1, 2, cols + 1, 2)
        .transpose(0, 2, 4, 1, 3, 5)
        .reshape(sets, rows + 1, cols + 1, CELL)
    )
    windows = [cells[:, u : u + rows, v : v + cols] for u in range(2) for v in range(2)]
    return jnp.concatenate(windows, axis=-1).reshape(sets, rows * cols, PIN)


def fold_patches(pieces, rows, cols, parts):
    grid = pieces.astype(f32).reshape(rows, cols, 2, 2, CELL)
    cells = jnp.zeros((rows + 1, cols + 1, CELL), f32)
    for u in range(2):
        for v in range(2):
            cells = cells + jnp.pad(grid[:, :, u, v], ((u, 1 - u), (v, 1 - v), (0, 0)))
    for axis, dim, span in sides(parts):
        before, after = neighbours(cells, axis, dim, span)
        middle = list(cells.shape)
        middle[dim] -= 2
        cells = cells + jnp.concatenate([before, jnp.zeros(middle, f32), after], axis=dim)
    canvas = (
        cells.reshape(rows + 1, cols + 1, CHANNELS, 2, 2)
        .transpose(2, 0, 3, 1, 4)
        .reshape(CHANNELS, 2 * rows + 2, 2 * cols + 2)
    )
    return canvas[:, 1:-1, 1:-1]


def window_order(weight):
    rows = weight.shape[0]
    return weight.reshape(rows, CHANNELS, 2, 2, 2, 2).transpose(0, 2, 4, 1, 3, 5).reshape(rows, PIN)


def channel_order(weight):
    rows = weight.shape[0]
    return weight.reshape(rows, 2, 2, CHANNELS, 2, 2).transpose(0, 3, 1, 4, 2, 5).reshape(rows, PIN)


def strip_layout(heights, seq_rows):
    starts = jnp.cumsum(heights) - heights
    rows_all = jnp.arange(seq_rows, dtype=jnp.int32)
    image_of = jnp.sum((rows_all[:, None] >= starts[None, 1:]).astype(jnp.int32), axis=1)
    start_of = jnp.sum(
        jnp.where(
            image_of[:, None] == jnp.arange(IMGS, dtype=jnp.int32)[None, :], starts[None, :], 0
        ),
        axis=1,
    )
    return (image_of, rows_all - start_of)


def rope_tables(row_place, column):
    quarter = HD // 4
    frequency = 10000.0 ** (-jnp.arange(quarter, dtype=f32) / quarter)
    row_angle = row_place.astype(f32)[:, None] * frequency[None, :]
    col_angle = column.astype(f32)[:, None] * frequency[None, :]
    angles = jnp.concatenate([row_angle, row_angle, col_angle, col_angle] * 2, axis=1)
    sign = jnp.where(jnp.arange(LANES) % 32 < 16, -1.0, 1.0)
    return (jnp.cos(angles), jnp.sin(angles) * sign[None, :])


def gather_all(shard):
    return lax.all_gather(shard, ALL, axis=0, tiled=True)


def scatter_all(part):
    return lax.psum_scatter(part, ALL, scatter_dimension=0, tiled=True)


def bits_of(axis):
    return lax.axis_size(axis).bit_length() - 1


def orders():
    first = [("fsdp", bit) for bit in range(bits_of("fsdp"))]
    main = [("cols", 0), ("rows", 0), ("cols", 1)]
    rest = [("rows", bit) for bit in range(1, bits_of("rows"))]
    rest += [("cols", bit) for bit in range(2, bits_of("cols"))]
    return [first + main[turn:] + main[:turn] + rest for turn in range(3)]


def block_masks(order):
    base = {"fsdp": 0, "cols": bits_of("fsdp"), "rows": bits_of("fsdp") + bits_of("cols")}
    steps = len(order)
    return [
        sum(
            ((index >> (steps - 1 - step)) & 1) << (base[axis] + bit)
            for step, (axis, bit) in enumerate(order)
        )
        for index in range(1 << steps)
    ]


def swap(values, axis, bit):
    return lax.ppermute(values, axis, [(i, i ^ (1 << bit)) for i in range(lax.axis_size(axis))])


def gather_near(shards_, picks):
    steps = [list(reversed(order)) for order in picks]
    held = list(shards_)
    for step in range(len(steps[0])):
        received = [swap(value, *steps[k][step]) for k, value in enumerate(held)]
        if step == len(steps[0]) - 1:
            return list(zip(held, received))
        held = [jnp.concatenate(pair, axis=0) for pair in zip(held, received)]


def scatter_near(parts, picks):
    terms = [[part] for part in parts]
    kind = [part.dtype for part in parts]
    half = [part.shape[0] // 2 for part in parts]
    total = lambda values: sum(value.astype(f32) for value in values)
    for step in range(len(picks[0])):
        sent = []
        for k in range(len(parts)):
            sent.append(total([term[half[k] :] for term in terms[k]]).astype(kind[k]))
        received = [swap(value, *picks[k][step]) for k, value in enumerate(sent)]
        for k in range(len(parts)):
            terms[k] = [term[: half[k]] for term in terms[k]] + [received[k]]
            half[k] //= 2
    return [total(values) for values in terms]


def exchange_heads(parts, micros):
    groups = [[m * parts + s for s in range(parts)] for m in range(micros)]

    def spread(values):
        return lax.all_to_all(
            values, "rows", split_axis=1, concat_axis=0, tiled=True, axis_index_groups=groups
        )

    def collect(values):
        return lax.all_to_all(
            values, "rows", split_axis=0, concat_axis=1, tiled=True, axis_index_groups=groups
        )

    return spread, collect


def shards(
    latent,
    time_embed,
    image_rows,
    pred_grad,
    embed_weight,
    adaptive_weight,
    project_weight,
    output_weight,
    gate_up_weight,
    down_weight,
    final_weight,
    norm_gains,
):
    micros = latent.shape[0]
    row_devices = lax.axis_size("rows")
    parts = row_devices // micros
    row_index = lax.axis_index("rows")
    micro, piece = row_index // parts, row_index % parts
    device = (row_index * lax.axis_size("cols") + lax.axis_index("cols")) * lax.axis_size(
        "fsdp"
    ) + lax.axis_index("fsdp")
    rows = latent.shape[3] // 2 * micros
    cols = latent.shape[4] // 2
    tokens = rows * cols
    seq_rows = rows * parts
    length = seq_rows * cols

    devices = lax.axis_size(ALL)
    share = D // devices
    near = share % 16 == 0
    picks = orders()
    place = None
    if near:
        place = (device.astype(jnp.int32).reshape(1), [block_masks(order) for order in picks])

    small = jnp.concatenate(
        [
            window_order(embed_weight),
            window_order(final_weight),
            norm_gains,
            jnp.zeros((norm_gains.shape[0], 2 * LANES - 2 * PIN - 6), bf16),
        ],
        axis=1,
    )
    temb = lax.dynamic_index_in_dim(time_embed, micro, 0, keepdims=False)[0, 0]
    condition = jax.nn.silu(temb).astype(bf16)
    if near:
        wide = condition.reshape(-1, 2 * LANES)
        both = gather_near([jnp.concatenate([small, wide], axis=0)], picks[:1])[0]
        both = jnp.concatenate(both, axis=0).reshape(devices, share + wide.shape[0], 2 * LANES)
        small = both[:, :share]
        conditions = both[:, share:].reshape(devices * IMGS, condition.shape[1])
        source = jnp.asarray(place[1][0], jnp.int32)
        chosen = ((jnp.arange(devices, dtype=jnp.int32) ^ device)[:, None] == source[None, :]).astype(bf16)
        small = dot_nn(chosen, small.reshape(devices, share * 2 * LANES)).astype(bf16)
        small = small.reshape(D, 2 * LANES)
    else:
        small = gather_all(small)
        conditions = gather_all(condition)
    w_embed = small[:, :PIN]
    w_final = small[:, PIN : 2 * PIN]
    gains = small[:, 2 * PIN : 2 * PIN + 6].astype(f32).T

    rows_held = adaptive_weight.shape[0]
    conditions = lax.dynamic_slice_in_dim(conditions, device * rows_held, rows_held, axis=1)
    per_image = dot_nn(conditions, adaptive_weight)
    if near:
        per_image = scatter_near([per_image], picks[:1])[0]
        thirds = [project_weight[:, k * D : (k + 1) * D] for k in range(3)]
        project_pieces = [piece for pair in gather_near(thirds, picks) for piece in pair]
    else:
        per_image = scatter_all(per_image)
        project_pieces = [gather_all(project_weight)]
    w_output = gather_all(output_weight)
    w_gate_up = gather_all(gate_up_weight)
    w_down = gather_all(down_weight)

    tiles = jnp.concatenate([latent[:, 0], pred_grad[:, 0]], axis=1)
    patches, grad_patches = extract_patches(to_strips(tiles), parts)

    heights = lax.dynamic_index_in_dim(image_rows, micro, 0, keepdims=False)[0, 0]
    row_image, row_place = strip_layout(heights, seq_rows)
    first_row = piece * rows
    my_image = lax.dynamic_slice_in_dim(row_image, first_row, rows)
    my_place = lax.dynamic_slice_in_dim(row_place, first_row, rows)
    token_image = jnp.repeat(my_image, cols)
    cosine, sine = rope_tables(
        jnp.repeat(my_place, cols), jnp.tile(jnp.arange(cols, dtype=jnp.int32), rows)
    )
    image = jnp.broadcast_to(token_image[:, None], (tokens, LANES))
    onehot = (token_image[None, :] == jnp.arange(8, dtype=jnp.int32)[:, None]).astype(bf16)
    strip_image = jnp.repeat(row_image, cols)
    head_lane = jnp.arange(LANES, dtype=jnp.int32)[None, :] % HD
    same = strip_image[:, None] == head_lane
    query_image = jnp.where(same, -mask_level, 0.0).astype(bf16)
    key_image = jnp.where(same | (head_lane >= IMGS), 0.0, mask_level).astype(bf16)

    modulation = per_image.reshape(IMGS, 5, D)
    scale_attn = 1.0 + modulation[:, 0]
    gate_attn = jnp.tanh(modulation[:, 1])
    scale_ffn = 1.0 + modulation[:, 2]
    gate_ffn = jnp.tanh(modulation[:, 3])
    scale_out = 1.0 + modulation[:, 4]
    table = lambda values: jnp.concatenate([values, values], axis=0)
    attn_pre = table(scale_attn * gains[0])
    attn_post = table(gate_attn * gains[3])
    ffn_pre = table(scale_ffn * gains[4])
    ffn_post = table(gate_ffn * gains[5])
    out_scale = table(scale_out)
    turn_gains = jnp.concatenate([gains[1:3], jnp.zeros((6, D), f32)], axis=0)

    embedded, normed, projected, hats, inverses, w_project = project_rows(
        patches, image, cosine, sine, w_embed, attn_pre, project_pieces, turn_gains, place
    )
    if parts == 1:
        pairs = D // LANES
        heads = (projected, projected, projected)
        spec_of = lambda which: (lambda i: (0, which * pairs + i))
        width = D
    else:
        spread, collect = exchange_heads(parts, micros)
        heads = tuple(spread(projected[:, w * D : (w + 1) * D]) for w in range(3))
        spec_of = lambda which: (lambda i: (0, i))
        width = D // parts
    attended_heads, log_total = attend(*heads, spec_of, width, query_image, key_image)
    attended = attended_heads if parts == 1 else collect(attended_heads)
    attn_out, mixed, normed_ffn = output_rows(
        attended, w_output, embedded, image, attn_post, ffn_pre
    )
    hidden, gate, up = gate_up_rows(normed_ffn, w_gate_up)
    final, late, ffn_back, pieces, sum_out, sum_ffn_post = down_rows(
        hidden, w_down, mixed, image, onehot, grad_patches, ffn_post, out_scale, w_final
    )
    down_grad = dot_tn(hidden, ffn_back).astype(bf16)
    ffn_back, down_grad = lax.optimization_barrier((ffn_back, down_grad))
    down_share = scatter_all(down_grad)
    prediction = from_strips(fold_patches(pieces, rows, cols, parts), micros)

    gate_back, up_back = gate_up_back(ffn_back, w_down, gate, up)
    gate_grad = dot_tn(normed_ffn, gate_back).astype(bf16)
    gate_back, gate_grad = lax.optimization_barrier((gate_back, gate_grad))
    gate_share = scatter_all(gate_grad)
    up_grad = dot_tn(normed_ffn, up_back).astype(bf16)
    up_back, up_grad = lax.optimization_barrier((up_back, up_grad))
    up_share = scatter_all(up_grad)
    early, attn_back, sum_ffn_pre, sum_attn_post = ffn_back_rows(
        gate_back, up_back, w_gate_up, late, mixed, attn_out, image, onehot, attn_post, ffn_pre
    )
    grad_attended = dot_nt(attn_back, w_output).astype(bf16)
    if parts > 1:
        grad_attended = spread(grad_attended)
    grads = attend_back(
        *heads, spec_of, width, attended_heads, grad_attended, log_total, query_image, key_image
    )
    if parts > 1:
        grads = tuple(collect(grad) for grad in grads)
    turned, sum_turn = turn_back(grads[0], grads[1], hats, inverses, cosine, sine, turn_gains)
    project_back = jnp.concatenate([turned, grads[2]], axis=1)
    if near:
        parts_held = [
            attention_grads(k, normed, project_back, attended, attn_back, place) for k in range(3)
        ]
        held = scatter_near(parts_held, picks)
        project_share = jnp.concatenate([value[:, :D] for value in held], axis=1)
        output_share = jnp.concatenate([value[:, D:] for value in held], axis=1)
    else:
        project_share = scatter_all(dot_tn(normed, project_back).astype(bf16))
        output_share = scatter_all(dot_tn(attended, attn_back).astype(bf16))
    embed_back, grad_pieces, sum_attn_pre = project_back_rows(
        project_back, w_project, embedded, early, image, onehot, attn_pre, w_embed
    )
    latent_grad = from_strips(fold_patches(grad_pieces, rows, cols, parts), micros)

    sum_attn_pre, sum_attn_post = sum_attn_pre[:IMGS], sum_attn_post[:IMGS]
    sum_ffn_pre, sum_ffn_post = sum_ffn_pre[:IMGS], sum_ffn_post[:IMGS]
    grad_modulation = jnp.stack(
        [
            gains[0] * sum_attn_pre,
            (1.0 - gate_attn * gate_attn) * gains[3] * sum_attn_post,
            gains[4] * sum_ffn_pre,
            (1.0 - gate_ffn * gate_ffn) * gains[5] * sum_ffn_post,
            sum_out[:IMGS],
        ],
        axis=1,
    ).reshape(IMGS, 5 * D)
    if near:
        wide = grad_modulation.astype(bf16).reshape(16, -1)
        pair = gather_near([wide], picks[:1])[0]
        grad_modulations = jnp.concatenate(pair, axis=0).astype(f32).reshape(-1, 5 * D)
    else:
        grad_modulations = gather_all(grad_modulation)
    adaptive_share = lax.dot_general(
        conditions.astype(f32),
        grad_modulations,
        (((0,), (0,)), ((), ())),
        precision=highest,
        preferred_element_type=f32,
    )
    gain_grads = jnp.stack(
        [
            jnp.sum(scale_attn * sum_attn_pre, axis=0),
            sum_turn[0],
            sum_turn[1],
            jnp.sum(gate_attn * sum_attn_post, axis=0),
            jnp.sum(scale_ffn * sum_ffn_pre, axis=0),
            jnp.sum(gate_ffn * sum_ffn_post, axis=0),
        ],
        axis=1,
    )
    small_grads = jnp.concatenate(
        [
            dot_tn(embed_back, patches),
            dot_tn(final, grad_patches),
            gain_grads,
            jnp.zeros((D, 2 * LANES - 2 * PIN - 6), f32),
        ],
        axis=1,
    )
    if near:
        chosen = ((source ^ device)[:, None] == jnp.arange(devices, dtype=jnp.int32)[None, :]).astype(f32)
        small_grads = jnp.dot(
            chosen, small_grads.reshape(devices, share * 2 * LANES), precision=highest
        ).reshape(D, 2 * LANES)
        small_share = scatter_near([small_grads], picks[:1])[0]
    else:
        small_share = scatter_all(small_grads)
    return (
        prediction[:, None],
        latent_grad[:, None],
        channel_order(small_share[:, :PIN]),
        adaptive_share,
        project_share.astype(f32),
        output_share.astype(f32),
        jnp.concatenate([gate_share, up_share], axis=1).astype(f32),
        down_share.astype(f32),
        channel_order(small_share[:, PIN : 2 * PIN]),
        small_share[:, 2 * PIN : 2 * PIN + 6],
    )


def solution(mesh):
    canvas = P(None, "fsdp", None, "rows", "cols")
    weight = P(ALL, None)
    return jax.shard_map(
        shards,
        mesh=mesh,
        in_specs=(canvas, P(None, "fsdp", "cols", None, None), P(None, "fsdp", "cols", None), canvas)
        + (weight,) * 8,
        out_specs=(canvas, canvas) + (weight,) * 8,
        check_vma=False,
    )
```

time: 3360 us -> 1070 us (0.32)
  waiting for transfers between devices: 1550 us -> 179 us
  matrix products: 759 us -> 79.4 us
  Pallas kernels: 0 us -> 505 us
  other arithmetic: 394 us -> 71.3 us
  local copies, waits for them, and re-layouts: 331 us -> 130 us
  blocking collectives: 122 us -> 0 us
  starting transfers between devices: 170 us -> 79.1 us
    reduce_scatter x7 -> x3, waiting for transfers between devices: 1400 us -> 0.01 us  [scatter_all(): return lax.psum_scatter(part, ALL, scatter_dimension=0, tiled=True)]
    dot_general x66 -> x10, matrix products: 759 us -> 79.4 us  [the longest x5 64.8 us: dot_tn(): lax.dot_general(left, right, (((0,), (0,)), ((), ())), preferred_element_...]
    pallas_call x0 -> x13, Pallas kernels: none -> 505 us  [the longest x4 150 us: matmul_rows(): pl.pallas_call(kernel, grid=(tiles + blocks,), in_specs=in_specs, out_spe...]
    ppermute x32 -> x59, waiting for transfers between devices: 13.1 us -> 178 us  [the longest x50 178 us: swap(): lax.ppermute(values, axis, [(i, i ^ 1 << bit) for i in range(lax.axis_siz...]
    convert_element_type x40 -> x18, other arithmetic: 189 us -> 31.2 us  [the longest x12 25.2 us: scatter_near(): sent.append(total([term[half[k]:] for term in terms[k]]).astype(kind[k]))]
    all_to_all x16 -> x0, waiting for transfers between devices: 129 us -> none  [the longest x2 32.1 us: run_micro(): lax.all_to_all(attended.reshape(strip_shape), 'rows', split_axis=0, conca...]
    all_gather x3 -> x0, blocking collectives: 122 us -> none  [the longest x1 42.7 us: shards(): lax.all_gather(final_weight, ('rows', 'cols', 'fsdp'), axis=0, tiled=True)]
    reduce_sum x19 -> x1, other arithmetic: 109 us -> 0.87 us  [shards(): jnp.sum(gate_ffn * sum_ffn_post, axis=0)]
  transfers between devices with their start and end apart: 61 -> 65, of which waited for: 21 -> 20; matrix products, arithmetic and copies ran while one was open for 27% -> 24% of each run, Pallas kernels for 0% -> 43%
where the time goes in v1:
time: 1070 us; the launch traced here: 1060 us
  Pallas kernels  505 us (47%)
  waiting for transfers between devices  179 us (17%)
  local copies, waits for them, and re-layouts  130 us (12%)
  matrix products  79.4 us (7%)
  starting transfers between devices  79.1 us (7%)
  other arithmetic  71.3 us (7%)
  between operations  19.9 us (2%)
    ppermute x50, waiting for transfers between devices, swap(): lax.ppermute(values, axis, [(i, i ^ 1 << bit) for i in range(lax.axis_siz...  178 us
    pallas_call x4, Pallas kernels, matmul_rows(): pl.pallas_call(kernel, grid=(tiles + blocks,), in_specs=in_specs, out_spe...  150 us
    pallas_call x1, Pallas kernels, attend_back(): pl.pallas_call(kernel, grid=(pairs,), in_specs=[pl.BlockSpec((length, LAN...  80.5 us
    pallas_call x1, Pallas kernels, attend(): pl.pallas_call(kernel, grid=(pairs,), in_specs=[pl.BlockSpec((length, LAN...  79.7 us
    dot_general x5, matrix products, dot_tn(): lax.dot_general(left, right, (((0,), (0,)), ((), ())), preferred_element_...  64.8 us
    pallas_call x1, Pallas kernels, project_rows(): pl.pallas_call(kernel, grid=(3,), in_specs=[whole(patches.shape), whole(i...  59.9 us
    ppermute x50, starting transfers between devices, swap(): lax.ppermute(values, axis, [(i, i ^ 1 << bit) for i in range(lax.axis_siz...  56 us
    pallas_call x1, Pallas kernels, gate_up_rows(): pl.pallas_call(kernel, grid=(tiles,), in_specs=[whole(normed.shape), pl.B...  41.7 us
  transfers between devices with their start and end apart: 65, of which 20 were waited for; matrix products, arithmetic and copies ran while one was open for 24% of the time, Pallas kernels for 43%

profile of v1, /device:TPU:0, one launch (start us, length us, event | category | flops | bytes accessed | tf_op | source)
XLA Modules:
  0.0 1063.9 jit_solution(9121323235019371441)
XLA Ops:
  28.9 3.9 concatenate.158
  40.4 3.4 collective-permute-start.1
  46.8 3.6 collective-permute-start.4
  52.1 4.2 reshape.231
  56.2 4.7 copy.133
  82.0 11.4 %collective-permute-done.6 = bf16[512,256]{1,0:T(8,128)(2,1)S(1)} collective-permute-done((bf16[512,256]{1,0:T(8,128)(2,1)S(1)}, bf16[512,256]{1,0:T(8,128)(2,1)S(1)}, u32[]{:S(2)}, u32[]{:S(2)}) %collective-permute-start.6) | collective-permute-done | bytes 262176 | tf_op jit(solution)/shard_map/ppermute | solution.py:949
  109.5 12.8 %collective-permute-done.20 = bf16[192,1536]{1,0:T(8,128)(2,1)} collective-permute-done((bf16[192,1536]{1,0:T(8,128)(2,1)}, bf16[192,1536]{1,0:T(8,128)(2,1)}, u32[]{:S(2)}, u32[]{:S(2)}) %collective-permute-start.20) | collective-permute-done | bytes 589856 | tf_op jit(solution)/shard_map/ppermute | solution.py:949
  132.1 28.9 %collective-permute-done.9 = f32[32,7680]{1,0:T(8,128)S(1)} collective-permute-done((f32[32,7680]{1,0:T(8,128)S(1)}, f32[32,7680]{1,0:T(8,128)S(1)}, u32[]{:S(2)}, u32[]{:S(2)}) %collective-permute-start.9) | collective-permute-done | bytes 983072 | tf_op jit(solution)/shard_map/ppermute | solution.py:949
  165.7 12.1 %collective-permute-done.26 = bf16[384,1536]{1,0:T(8,128)(2,1)S(1)} collective-permute-done((bf16[384,1536]{1,0:T(8,128)(2,1)S(1)}, bf16[384,1536]{1,0:T(8,128)(2,1)S(1)}, u32[]{:S(2)}, u32[]{:S(2)}) %collective-permute-start.26) | collective-permute-done | bytes 1179680 | tf_op jit(solution)/shard_map/ppermute | solution.py:949
  179.4 14.4 %collective-permute-done.16 = bf16[384,1536]{1,0:T(8,128)(2,1)S(1)} collective-permute-done((bf16[384,1536]{1,0:T(8,128)(2,1)S(1)}, bf16[384,1536]{1,0:T(8,128)(2,1)S(1)}, u32[]{:S(2)}, u32[]{:S(2)}) %collective-permute-start.16) | collective-permute-done | bytes 1179680 | tf_op jit(solution)/shard_map/ppermute | solution.py:949
  195.3 3.7 collective-permute-start.12
  199.1 6.1 collective-permute-done.12
  212.5 59.9 %project_rows.1 = (f32[1024,1536]{1,0:T(8,128)}, bf16[1024,1536]{1,0:T(8,128)(2,1)}, bf16[1024,4608]{1,0:T(8,128)(2,1)}, bf16[1024,3072]{1,0:T(8,128)(2,1)}, f32...) custom-call(bf16[1024,64]{1,0:T(8,128)(2,1)} %bitcast.173, s32[1024,128]{1,0:T(8,128)} %broadcast_in_dim.77.refs_1_.refs_3_.refs_6_.refs_4_, ...), custom_call_target="tpu_custom_call" | custom-call | flops 14495514624 | bytes 51904512 | tf_op jit(solution)/shard_map/project_rows/pallas_call | solution.py:301
  272.4 79.7 %attend.1 = (bf16[1024,1536]{1,0:T(8,128)(2,1)}, f32[12,2,1024]{2,1,0:T(2,128)}) custom-call(bf16[1024,4608]{1,0:T(8,128)(2,1)} %get-tuple-element.50.q_ref.k_ref.v_ref, bf16[1024,4608]{1,0:T(8,128)(2,1)} %get-tuple-element.50.q_ref.k_ref.v_ref, bf16[1024,4608]{1,0:T(8,128)(2,1)} %get-tuple-element.50.q_ref.k_ref.v_ref, ...), custom_call_target="tpu_custom_call" | custom-call | flops 51539607552 | bytes 12582912 | tf_op jit(solution)/shard_map/attend/pallas_call | solution.py:424
  352.1 20.7 %output_rows.1 = (f32[1024,1536]{1,0:T(8,128)}, f32[1024,1536]{1,0:T(8,128)}, bf16[1024,1536]{1,0:T(8,128)(2,1)}) custom-call(bf16[1024,1536]{1,0:T(8,128)(2,1)} %get-tuple-element.51.refs_0_.o_ref.other_ref, bf16[1536,1536]{1,0:T(8,128)(2,1)} %all-gather.4.cloned.1.call-done.refs_1_, f32[1024,1536]{1,0:T(8,128)} %get-tuple-element.52.refs_2_, ...), custom_call_target="tpu_custom_call" | custom-call | flops 4831838208 | bytes 20447232 | tf_op jit(solution)/shard_map/output_rows/pallas_call | solution.py:151
  372.8 41.7 %gate_up_rows.1 = (bf16[1024,4096]{1,0:T(8,128)(2,1)}, bf16[1024,4096]{1,0:T(8,128)(2,1)}, bf16[1024,4096]{1,0:T(8,128)(2,1)}) custom-call(bf16[1024,1536]{1,0:T(8,128)(2,1)} %get-tuple-element.53.left_ref, bf16[1536,8192]{1,0:T(8,128)(2,1)} %all-gather.6.cloned.1.call-done.gate_weight.up_weight.refs_2_, ...), custom_call_target="tpu_custom_call" | custom-call | flops 25769803776 | bytes 50331648 | tf_op jit(solution)/shard_map/gate_up_rows/pallas_call | solution.py:560
  414.5 43.5 %down_rows.1 = (bf16[1024,1536]{1,0:T(8,128)(2,1)}, f32[1024,1536]{1,0:T(8,128)}, bf16[1024,1536]{1,0:T(8,128)(2,1)}, bf16[1024,64]{1,0:T(8,128)(2,1)}, f32[8,1536]{1,0:T(8,128)}, /*index=5*/f32[8,1536]{1,0:T(8,128)}) custom-call(bf16[1024,4096]{1,0:T(8,128)(2,1)} %get-tuple-element.54.refs_0_, ...), custom_call_target="tpu_custom_call" | custom-call | flops 12884901888 | bytes 33554432 | tf_op jit(solution)/shard_map/down_rows/pallas_call | solution.py:151
  458.0 20.5 %convolution_convert_fusion.2 = bf16[4096,1536]{1,0:T(8,128)(2,1)} fusion(bf16[1024,4096]{1,0:T(8,128)(2,1)} %get-tuple-element.54.refs_0_, bf16[1024,1536]{1,0:T(8,128)(2,1)} %get-tuple-element.58.left_ref), kind=kOutput, calls=%fused_computation.2 | convolution fusion | flops 12891193344 | bytes 24117248 | tf_op jit(solution)/shard_map/dot_general | solution.py:38
  485.2 5.1 collective-permute-start.28
  490.3 33.1 %gate_up_back.1 = (bf16[1024,4096]{1,0:T(8,128)(2,1)}, bf16[1024,4096]{1,0:T(8,128)(2,1)}) custom-call(bf16[1024,1536]{1,0:T(8,128)(2,1)} %get-tuple-element.58.left_ref, bf16[4096,1536]{1,0:T(8,128)(2,1)} %all-gather.8.cloned.1.call-done.refs_1_.weight_ref, bf16[1024,4096]{1,0:T(8,128)(2,1)} %get-tuple-element.59.gate_ref, ...), custom_call_target="tpu_custom_call" | custom-call | flops 12884901888 | bytes 46137344 | tf_op jit(solution)/shard_map/gate_up_back/pallas_call | solution.py:602
  523.4 19.3 %convolution_convert_fusion.1 = bf16[1536,4096]{1,0:T(8,128)(2,1)} fusion(bf16[1024,1536]{1,0:T(8,128)(2,1)S(1)} %copy-done.59, bf16[1024,4096]{1,0:T(8,128)(2,1)} %get-tuple-element.62.refs_0_), kind=kOutput, calls=%fused_computation.1 | convolution fusion | flops 12891193344 | bytes 24117248 | tf_op jit(solution)/shard_map/dot_general | solution.py:38
  542.7 20.0 %convolution_convert_fusion = bf16[1536,4096]{1,0:T(8,128)(2,1)} fusion(bf16[1024,1536]{1,0:T(8,128)(2,1)} %get-tuple-element.53.left_ref, bf16[1024,4096]{1,0:T(8,128)(2,1)} %get-tuple-element.64.refs_1_), kind=kOutput, calls=%fused_computation | convolution fusion | flops 12891193344 | bytes 24117248 | tf_op jit(solution)/shard_map/dot_general | solution.py:38
  562.8 53.0 %ffn_back_rows.1 = (f32[1024,1536]{1,0:T(8,128)}, bf16[1024,1536]{1,0:T(8,128)(2,1)}, f32[8,1536]{1,0:T(8,128)}, f32[8,1536]{1,0:T(8,128)}) custom-call(bf16[1024,4096]{1,0:T(8,128)(2,1)} %get-tuple-element.62.refs_0_, bf16[1024,4096]{1,0:T(8,128)(2,1)} %get-tuple-element.64.refs_1_, ...), custom_call_target="tpu_custom_call" | custom-call | flops 25769803776 | bytes 54525952 | tf_op jit(solution)/shard_map/ffn_back_rows/pallas_call | solution.py:151
  615.8 9.3 convolution_convert_fusion.4.g_ref
  625.1 80.5 %attend_back.1 = (bf16[1024,1536]{1,0:T(8,128)(2,1)}, bf16[1024,1536]{1,0:T(8,128)(2,1)}, bf16[1024,1536]{1,0:T(8,128)(2,1)}) custom-call(bf16[1024,4608]{1,0:T(8,128)(2,1)} %get-tuple-element.50.q_ref.k_ref.v_ref, bf16[1024,4608]{1,0:T(8,128)(2,1)} %get-tuple-element.50.q_ref.k_ref.v_ref, bf16[1024,4608]{1,0:T(8,128)(2,1)} %get-tuple-element.50.q_ref.k_ref.v_ref, ...), custom_call_target="tpu_custom_call" | custom-call | flops 128849018880 | bytes 25165824 | tf_op jit(solution)/shard_map/attend_back/pallas_call | solution.py:509
  705.5 19.1 %turn_back.1 = (bf16[1024,3072]{1,0:T(8,128)(2,1)}, f32[8,1536]{1,0:T(8,128)}) custom-call(bf16[1024,1536]{1,0:T(8,128)(2,1)} %get-tuple-element.69.gq_ref, bf16[1024,1536]{1,0:T(8,128)(2,1)} %get-tuple-element.70.gk_ref, bf16[1024,3072]{1,0:T(8,128)(2,1)} %get-tuple-element.71.hat_ref, f32[1024,256]{1,0:T(8,128)} %get-tuple-element.72.inv_ref, ...), custom_call_target="tpu_custom_call" | custom-call | flops 62914560 | bytes 18874368 | tf_op jit(solution)/shard_map/turn_back/pallas_call | solution.py:766
  727.8 6.3 constant_dynamic-update-slice_fusion.34
  736.1 33.2 %project_back_rows.1 = (bf16[1024,1536]{1,0:T(8,128)(2,1)}, bf16[1024,64]{1,0:T(8,128)(2,1)}, f32[8,1536]{1,0:T(8,128)}) custom-call(bf16[1024,4608]{1,0:T(8,128)(2,1)} %constant_dynamic-update-slice_fusion.33.refs_0_.back_ref, bf16[1536,4608]{1,0:T(8,128)(2,1)} %get-tuple-element.75.refs_1_, f32[1024,1536]{1,0:T(8,128)} %get-tuple-element.52.refs_2_, ...), custom_call_target="tpu_custom_call" | custom-call | flops 14495514624 | bytes 36175872 | tf_op jit(solution)/shard_map/project_back_rows/pallas_call | solution.py:151
  785.8 5.5 concatenate.189
  798.0 4.9 collective-permute-start.31
  805.0 13.5 %attention_grads.5 = bf16[1536,2048]{1,0:T(8,128)(2,1)} custom-call(bf16[1024,1536]{1,0:T(8,128)(2,1)} %get-tuple-element.86.left_ref, bf16[1024,4608]{1,0:T(8,128)(2,1)} %constant_dynamic-update-slice_fusion.33.refs_0_.back_ref, bf16[1024,1536]{1,0:T(8,128)(2,1)} %get-tuple-element.51.refs_0_.o_ref.other_ref, ...), custom_call_target="tpu_custom_call" | custom-call | flops 6442450944 | bytes 18874368 | tf_op jit(solution)/shard_map/attention_grads/pallas_call | solution.py:357
  818.5 13.5 %attention_grads.4 = bf16[1536,2048]{1,0:T(8,128)(2,1)} custom-call(bf16[1024,1536]{1,0:T(8,128)(2,1)} %get-tuple-element.86.left_ref, bf16[1024,4608]{1,0:T(8,128)(2,1)} %constant_dynamic-update-slice_fusion.33.refs_0_.back_ref, bf16[1024,1536]{1,0:T(8,128)(2,1)} %get-tuple-element.51.refs_0_.o_ref.other_ref, ...), custom_call_target="tpu_custom_call" | custom-call | flops 6442450944 | bytes 18874368 | tf_op jit(solution)/shard_map/attention_grads/pallas_call | solution.py:357
  832.0 13.5 %attention_grads.3 = bf16[1536,2048]{1,0:T(8,128)(2,1)} custom-call(bf16[1024,1536]{1,0:T(8,128)(2,1)} %get-tuple-element.86.left_ref, bf16[1024,4608]{1,0:T(8,128)(2,1)} %constant_dynamic-update-slice_fusion.33.refs_0_.back_ref, bf16[1024,1536]{1,0:T(8,128)(2,1)} %get-tuple-element.51.refs_0_.o_ref.other_ref, ...), custom_call_target="tpu_custom_call" | custom-call | flops 6442450944 | bytes 18874368 | tf_op jit(solution)/shard_map/attention_grads/pallas_call | solution.py:357
  874.3 4.1 slice.933
  878.8 4.0 slice.891
  890.9 3.4 collective-permute-start.40
  900.8 8.6 collective-permute-done.35
  911.8 5.9 collective-permute-done.36
  918.8 7.2 collective-permute-done.37
  926.2 3.1 collective-permute-start.38
  930.3 9.9 collective-permute-done.38
  942.2 3.7 add_convert_fusion
  946.1 3.7 add_convert_fusion.1
  952.2 3.7 add_convert_fusion.2
  956.9 3.5 reshape.258
  962.6 25.2 %collective-permute-done.55 = bf16[384,2048]{1,0:T(8,128)(2,1)} collective-permute-done((bf16[384,2048]{1,0:T(8,128)(2,1)}, bf16[384,2048]{1,0:T(8,128)(2,1)}, u32[]{:S(2)}, u32[]{:S(2)}) %collective-permute-start.55) | collective-permute-done | bytes 1572896 | tf_op jit(solution)/shard_map/ppermute | solution.py:949
  997.6 9.3 collective-permute-done.56
  1029.9 12.9 %collective-permute-done.58 = bf16[48,2048]{1,0:T(8,128)(2,1)S(1)} collective-permute-done((bf16[48,2048]{1,0:T(8,128)(2,1)S(1)}, bf16[48,2048]{1,0:T(8,128)(2,1)S(1)}, u32[]{:S(2)}, u32[]{:S(2)}) %collective-permute-start.58) | collective-permute-done | bytes 196640 | tf_op jit(solution)/shard_map/ppermute | solution.py:949
  (472 shorter events, 230.9 us)
Async XLA Ops:
  7.2 344.9 %all-gather.4.cloned.1.call-start = ((), (), s32[]{:S(2)}) async-start(), calls=%async_computation.3 | async-start | bytes 4866048 | tf_op jit(solution)/shard_map/all_gather | solution.py:917
  7.9 364.9 %all-gather.6.cloned.1.call-start = ((), (), s32[]{:S(2)}) async-start(), calls=%async_computation.4 | async-start | bytes 25952256 | tf_op jit(solution)/shard_map/all_gather | solution.py:917
  8.7 405.8 %all-gather.8.cloned.1.call-start = ((), (), s32[]{:S(2)}) async-start(), calls=%async_computation.5 | async-start | bytes 12976128 | tf_op jit(solution)/shard_map/all_gather | solution.py:917
  9.6 30.4 %collective-permute-start = (bf16[8,64,32]{1,2,0:T(8,128)(2,1)S(1)}, bf16[8,64,32]{1,2,0:T(8,128)(2,1)S(1)}, u32[]{:S(2)}, u32[]{:S(2)}) collective-permute-start(bf16[8,64,32]{1,2,0:T(8,128)(2,1)S(1)} %get-tuple-element.181), channel_id=1, source_target_pairs={{0,16},{16,0},{1,17},{17,1},{2,18},{18,2},{3,19},{19,3},{4,20},{20... | collective-permute-start | bytes 98312 | tf_op jit(solution)/shard_map/ppermute | solution.py:795
  17.4 26.4 %collective-permute-start.3 = (bf16[64,256]{1,0:T(8,128)(2,1)S(1)}, bf16[64,256]{1,0:T(8,128)(2,1)S(1)}, u32[]{:S(2)}, u32[]{:S(2)}) collective-permute-start(bf16[64,256]{1,0:T(8,128)(2,1)S(1)} %pad_maximum_fusion.25), channel_id=1, source_target_pairs={{0,8},{2,10},{4,12},{6,14},{8,0},{10,2},{12,4},{14,6},{1,9},{3,11}... | collective-permute-start | bytes 98312 | tf_op jit(solution)/shard_map/ppermute | solution.py:949
  22.1 44.1 %collective-permute-start.23 = (bf16[48,1536]{1,0:T(8,128)(2,1)S(1)}, bf16[48,1536]{1,0:T(8,128)(2,1)S(1)}, u32[]{:S(2)}, u32[]{:S(2)}) collective-permute-start(bf16[48,1536]{1,0:T(8,128)(2,1)S(1)} %get-tuple-element.156), channel_id=1, source_target_pairs={{0,8},{2,10},{4,12},{6,14},{8,0},{10,2},{12,4},{14,6},{1,9},{3,11}... | collective-permute-start | bytes 442376 | tf_op jit(solution)/shard_map/ppermute | solution.py:949
  22.4 46.1 %collective-permute-start.13 = (bf16[48,1536]{1,0:T(8,128)(2,1)}, bf16[48,1536]{1,0:T(8,128)(2,1)S(1)}, u32[]{:S(2)}, u32[]{:S(2)}) collective-permute-start(bf16[48,1536]{1,0:T(8,128)(2,1)} %get-tuple-element.160), channel_id=1, source_target_pairs={{0,8},{2,10},{4,12},{6,14},{8,0},{10,2},{12,4},{14,6},{1,9},{3,11}... | collective-permute-start | bytes 442376 | tf_op jit(solution)/shard_map/ppermute | solution.py:949
  25.0 45.7 %collective-permute-start.18 = (bf16[48,1536]{1,0:T(8,128)(2,1)}, bf16[48,1536]{1,0:T(8,128)(2,1)}, u32[]{:S(2)}, u32[]{:S(2)}) collective-permute-start(bf16[48,1536]{1,0:T(8,128)(2,1)} %get-tuple-element.161), channel_id=1, source_target_pairs={{0,8},{2,10},{4,12},{6,14},{8,0},{10,2},{12,4},{14,6},{1,9},{3,11}... | collective-permute-start | bytes 442376 | tf_op jit(solution)/shard_map/ppermute | solution.py:949
  25.3 1027.1 %reduce-scatter.8.cloned.1.call-start = ((), (), s32[]{:S(2)}) async-start(), calls=%async_computation.8 | async-start | bytes 12976128 | tf_op jit(solution)/shard_map/reduce_scatter | solution.py:921
  46.8 16.4 %collective-permute-start.4 = (bf16[128,256]{1,0:T(8,128)(2,1)}, bf16[128,256]{1,0:T(8,128)(2,1)}, u32[]{:S(2)}, u32[]{:S(2)}) collective-permute-start(bf16[128,256]{1,0:T(8,128)(2,1)} %pad_maximum_fusion.19), channel_id=1, source_target_pairs={{0,4},{2,6},{4,0},{6,2},{8,12},{10,14},{12,8},{14,10},{1,5},{3,7},... | collective-permute-start | bytes 196616 | tf_op jit(solution)/shard_map/ppermute | solution.py:949
  70.2 23.3 %collective-permute-start.14 = (bf16[96,1536]{1,0:T(8,128)(2,1)S(1)}, bf16[96,1536]{1,0:T(8,128)(2,1)S(1)}, u32[]{:S(2)}, u32[]{:S(2)}) collective-permute-start(bf16[96,1536]{1,0:T(8,128)(2,1)S(1)} %pad_maximum_fusion.9), channel_id=1, source_target_pairs={{0,4},{2,6},{4,0},{6,2},{8,12},{10,14},{12,8},{14,10},{1,5},{3,7},... | collective-permute-start | bytes 884744 | tf_op jit(solution)/shard_map/ppermute | solution.py:949
  71.7 24.8 %collective-permute-start.19 = (bf16[96,1536]{1,0:T(8,128)(2,1)S(1)}, bf16[96,1536]{1,0:T(8,128)(2,1)S(1)}, u32[]{:S(2)}, u32[]{:S(2)}) collective-permute-start(bf16[96,1536]{1,0:T(8,128)(2,1)S(1)} %pad_maximum_fusion.10), channel_id=1, source_target_pairs={{0,2},{2,0},{4,6},{6,4},{8,10},{10,8},{12,14},{14,12},{1,3},{3,1},... | collective-permute-start | bytes 884744 | tf_op jit(solution)/shard_map/ppermute | solution.py:949
  77.4 15.9 %collective-permute-start.6 = (bf16[512,256]{1,0:T(8,128)(2,1)S(1)}, bf16[512,256]{1,0:T(8,128)(2,1)S(1)}, u32[]{:S(2)}, u32[]{:S(2)}) collective-permute-start(bf16[512,256]{1,0:T(8,128)(2,1)S(1)} %get-tuple-element.178), channel_id=1, source_target_pairs={{0,2},{2,0},{4,6},{6,4},{8,10},{10,8},{12,14},{14,12},{1,3},{3,1},... | collective-permute-start | bytes 786440 | tf_op jit(solution)/shard_map/ppermute | solution.py:949
  80.7 47.9 %collective-permute-start.25 = (bf16[192,1536]{1,0:T(8,128)(2,1)}, bf16[192,1536]{1,0:T(8,128)(2,1)}, u32[]{:S(2)}, u32[]{:S(2)}) collective-permute-start(bf16[192,1536]{1,0:T(8,128)(2,1)} %pad_maximum_fusion.6), channel_id=1, source_target_pairs={{0,2},{2,0},{4,6},{6,4},{8,10},{10,8},{12,14},{14,12},{1,3},{3,1},... | collective-permute-start | bytes 1769480 | tf_op jit(solution)/shard_map/ppermute | solution.py:949
  95.3 30.4 %collective-permute-start.15 = (bf16[192,1536]{1,0:T(8,128)(2,1)}, bf16[192,1536]{1,0:T(8,128)(2,1)}, u32[]{:S(2)}, u32[]{:S(2)}) collective-permute-start(bf16[192,1536]{1,0:T(8,128)(2,1)} %pad_maximum_fusion.4), channel_id=1, source_target_pairs={{0,16},{16,0},{1,17},{17,1},{2,18},{18,2},{3,19},{19,3},{4,20},{20... | collective-permute-start | bytes 1769480 | tf_op jit(solution)/shard_map/ppermute | solution.py:949
  98.4 23.9 %collective-permute-start.20 = (bf16[192,1536]{1,0:T(8,128)(2,1)}, bf16[192,1536]{1,0:T(8,128)(2,1)}, u32[]{:S(2)}, u32[]{:S(2)}) collective-permute-start(bf16[192,1536]{1,0:T(8,128)(2,1)} %pad_maximum_fusion.5), channel_id=1, source_target_pairs={{0,4},{2,6},{4,0},{6,2},{8,12},{10,14},{12,8},{14,10},{1,5},{3,7},... | collective-permute-start | bytes 1769480 | tf_op jit(solution)/shard_map/ppermute | solution.py:949
  103.1 20.7 %collective-permute-start.8 = (f32[64,7680]{1,0:T(8,128)}, f32[64,7680]{1,0:T(8,128)}, u32[]{:S(2)}, u32[]{:S(2)}) collective-permute-start(f32[64,7680]{1,0:T(8,128)} %slice.823), channel_id=1, source_target_pairs={{0,1},{1,0},{2,3},{3,2},{4,5},{5,4},{6,7},{7,6},{8,9},{9,8},{10,11... | collective-permute-start | bytes 5898248 | tf_op jit(solution)/shard_map/ppermute | solution.py:949
  123.6 75.3 %collective-permute-start.21 = (bf16[384,1536]{1,0:T(8,128)(2,1)S(1)}, bf16[384,1536]{1,0:T(8,128)(2,1)S(1)}, u32[]{:S(2)}, u32[]{:S(2)}) collective-permute-start(bf16[384,1536]{1,0:T(8,128)(2,1)S(1)} %pad_maximum_fusion.1), channel_id=1, source_target_pairs={{0,16},{16,0},{1,17},{17,1},{2,18},{18,2},{3,19},{19,3},{4,20},{20... | collective-permute-start | bytes 3538952 | tf_op jit(solution)/shard_map/ppermute | solution.py:949
  125.2 35.9 %collective-permute-start.9 = (f32[32,7680]{1,0:T(8,128)S(1)}, f32[32,7680]{1,0:T(8,128)S(1)}, u32[]{:S(2)}, u32[]{:S(2)}) collective-permute-start(f32[32,7680]{1,0:T(8,128)S(1)} %slice_add_fusion), channel_id=1, source_target_pairs={{0,2},{2,0},{4,6},{6,4},{8,10},{10,8},{12,14},{14,12},{1,3},{3,1},... | collective-permute-start | bytes 2949128 | tf_op jit(solution)/shard_map/ppermute | solution.py:949
  127.1 66.7 %collective-permute-start.16 = (bf16[384,1536]{1,0:T(8,128)(2,1)S(1)}, bf16[384,1536]{1,0:T(8,128)(2,1)S(1)}, u32[]{:S(2)}, u32[]{:S(2)}) collective-permute-start(bf16[384,1536]{1,0:T(8,128)(2,1)S(1)} %pad_maximum_fusion), channel_id=1, source_target_pairs={{0,2},{2,0},{4,6},{6,4},{8,10},{10,8},{12,14},{14,12},{1,3},{3,1},... | collective-permute-start | bytes 3538952 | tf_op jit(solution)/shard_map/ppermute | solution.py:949
  129.7 48.1 %collective-permute-start.26 = (bf16[384,1536]{1,0:T(8,128)(2,1)S(1)}, bf16[384,1536]{1,0:T(8,128)(2,1)S(1)}, u32[]{:S(2)}, u32[]{:S(2)}) collective-permute-start(bf16[384,1536]{1,0:T(8,128)(2,1)S(1)} %pad_maximum_fusion.2), channel_id=1, source_target_pairs={{0,4},{2,6},{4,0},{6,2},{8,12},{10,14},{12,8},{14,10},{1,5},{3,7},... | collective-permute-start | bytes 3538952 | tf_op jit(solution)/shard_map/ppermute | solution.py:949
  162.2 15.8 %collective-permute-start.10 = (f32[16,7680]{1,0:T(8,128)S(1)}, f32[16,7680]{1,0:T(8,128)S(1)}, u32[]{:S(2)}, u32[]{:S(2)}) collective-permute-start(f32[16,7680]{1,0:T(8,128)S(1)} %slice_add_fusion.1), channel_id=1, source_target_pairs={{0,16},{16,0},{1,17},{17,1},{2,18},{18,2},{3,19},{19,3},{4,20},{20... | collective-permute-start | bytes 1474568 | tf_op jit(solution)/shard_map/ppermute | solution.py:949
  177.9 31.7 %collective-permute-start.27 = (bf16[768,1536]{1,0:T(8,128)(2,1)S(1)}, bf16[768,1536]{1,0:T(8,128)(2,1)S(1)}, u32[]{:S(2)}, u32[]{:S(2)}) collective-permute-start(bf16[768,1536]{1,0:T(8,128)(2,1)S(1)} %constant_dynamic-update-slice_fusion.28.refs_11_), channel_id=1, source_target_pairs={{0,1},{1,0},{2,3},{3,2},{4,5},{5,4},{6,7},{7,6},{8,9},{9,8},{10,11... | collective-permute-start | bytes 7077896 | tf_op jit(solution)/shard_map/ppermute | solution.py:949
  193.8 15.7 %collective-permute-start.17 = (bf16[768,1536]{1,0:T(8,128)(2,1)S(1)}, bf16[768,1536]{1,0:T(8,128)(2,1)S(1)}, u32[]{:S(2)}, u32[]{:S(2)}) collective-permute-start(bf16[768,1536]{1,0:T(8,128)(2,1)S(1)} %constant_dynamic-update-slice_fusion.18.refs_7_), channel_id=1, source_target_pairs={{0,1},{1,0},{2,3},{3,2},{4,5},{5,4},{6,7},{7,6},{8,9},{9,8},{10,11... | collective-permute-start | bytes 7077896 | tf_op jit(solution)/shard_map/ppermute | solution.py:949
  478.5 575.8 %reduce-scatter.4.cloned.1.call-start = ((), (), s32[]{:S(2)}) async-start(), calls=%async_computation.6 | async-start | bytes 12976128 | tf_op jit(solution)/shard_map/reduce_scatter | solution.py:921
  483.9 362.3 %collective-permute-start.29 = (f32[65,1,16]{0,2,1:T(8,128)}, f32[65,1,16]{0,2,1:T(8,128)}, u32[]{:S(2)}, u32[]{:S(2)}) collective-permute-start(f32[65,1,16]{0,2,1:T(8,128)} %copy.146), channel_id=1, source_target_pairs={{2,0},{4,2},{6,4},{8,6},{10,8},{12,10},{14,12},{3,1},{5,3},{7,5},{... | collective-permute-start | bytes 12488 | tf_op jit(solution)/shard_map/ppermute | solution.py:841
  485.2 361.0 %collective-permute-start.28 = (f32[65,1,16]{0,2,1:T(8,128)}, f32[65,1,16]{0,2,1:T(8,128)}, u32[]{:S(2)}, u32[]{:S(2)}) collective-permute-start(f32[65,1,16]{0,2,1:T(8,128)} %copy.145), channel_id=1, source_target_pairs={{0,2},{2,4},{4,6},{6,8},{8,10},{10,12},{12,14},{1,3},{3,5},{5,7},{... | collective-permute-start | bytes 12488 | tf_op jit(solution)/shard_map/ppermute | solution.py:841
  562.7 491.6 %reduce-scatter.6.cloned.1.call-start = ((), (), s32[]{:S(2)}) async-start(), calls=%async_computation.7 | async-start | bytes 12976128 | tf_op jit(solution)/shard_map/reduce_scatter | solution.py:921
  772.3 118.6 %collective-permute-start.39 = (bf16[16,1920]{1,0:T(8,128)(2,1)S(1)}, bf16[16,1920]{1,0:T(8,128)(2,1)S(1)}, u32[]{:S(2)}, u32[]{:S(2)}) collective-permute-start(bf16[16,1920]{1,0:T(8,128)(2,1)S(1)} %convert_element_type.330), channel_id=1, source_target_pairs={{0,8},{2,10},{4,12},{6,14},{8,0},{10,2},{12,4},{14,6},{1,9},{3,11}... | collective-permute-start | bytes 184328 | tf_op jit(solution)/shard_map/ppermute | solution.py:949
  796.7 49.4 %collective-permute-start.32 = (f32[65,1,16]{0,2,1:T(8,128)S(1)}, f32[65,1,16]{0,2,1:T(8,128)S(1)}, u32[]{:S(2)}, u32[]{:S(2)}) collective-permute-start(f32[65,1,16]{0,2,1:T(8,128)S(1)} %copy.154), channel_id=1, source_target_pairs={{2,0},{4,2},{6,4},{8,6},{10,8},{12,10},{14,12},{3,1},{5,3},{7,5},{... | collective-permute-start | bytes 12488 | tf_op jit(solution)/shard_map/ppermute | solution.py:841
  798.0 48.1 %collective-permute-start.31 = (f32[65,1,16]{0,2,1:T(8,128)S(1)}, f32[65,1,16]{0,2,1:T(8,128)S(1)}, u32[]{:S(2)}, u32[]{:S(2)}) collective-permute-start(f32[65,1,16]{0,2,1:T(8,128)S(1)} %copy.153), channel_id=1, source_target_pairs={{0,2},{2,4},{4,6},{6,8},{8,10},{10,12},{12,14},{1,3},{3,5},{5,7},{... | collective-permute-start | bytes 12488 | tf_op jit(solution)/shard_map/ppermute | solution.py:841
  857.1 31.0 %collective-permute-start.30 = (f32[4,64,32]{1,2,0:T(8,128)S(1)}, f32[4,64,32]{1,2,0:T(8,128)}, u32[]{:S(2)}, u32[]{:S(2)}) collective-permute-start(f32[4,64,32]{1,2,0:T(8,128)S(1)} %bitcast.185), channel_id=1, source_target_pairs={{16,0},{0,16},{17,1},{1,17},{18,2},{2,18},{19,3},{3,19},{20,4},{4,... | collective-permute-start | bytes 98312 | tf_op jit(solution)/shard_map/ppermute | solution.py:817
  868.9 19.2 %collective-permute-start.33 = (f32[4,64,32]{1,2,0:T(8,128)}, f32[4,64,32]{1,2,0:T(8,128)}, u32[]{:S(2)}, u32[]{:S(2)}) collective-permute-start(f32[4,64,32]{1,2,0:T(8,128)} %bitcast.48), channel_id=1, source_target_pairs={{16,0},{0,16},{17,1},{1,17},{18,2},{2,18},{19,3},{3,19},{20,4},{4,... | collective-permute-start | bytes 98312 | tf_op jit(solution)/shard_map/ppermute | solution.py:817
  874.2 20.7 %collective-permute-start.34 = (f32[768,256]{0,1:T(8,128)}, f32[768,256]{0,1:T(8,128)S(1)}, u32[]{:S(2)}, u32[]{:S(2)}) collective-permute-start(f32[768,256]{0,1:T(8,128)} %copy.167), channel_id=1, source_target_pairs={{0,1},{1,0},{2,3},{3,2},{4,5},{5,4},{6,7},{7,6},{8,9},{9,8},{10,11... | collective-permute-start | bytes 2359304 | tf_op jit(solution)/shard_map/ppermute | solution.py:949
  878.5 63.8 %collective-permute-start.54 = (bf16[768,2048]{1,0:T(8,128)(2,1)}, bf16[768,2048]{1,0:T(8,128)(2,1)}, u32[]{:S(2)}, u32[]{:S(2)}) collective-permute-start(bf16[768,2048]{1,0:T(8,128)(2,1)} %slice.933), channel_id=1, source_target_pairs={{0,1},{1,0},{2,3},{3,2},{4,5},{5,4},{6,7},{7,6},{8,9},{9,8},{10,11... | collective-permute-start | bytes 9437192 | tf_op jit(solution)/shard_map/ppermute | solution.py:949
  888.0 58.1 %collective-permute-start.49 = (bf16[768,2048]{1,0:T(8,128)(2,1)}, bf16[768,2048]{1,0:T(8,128)(2,1)}, u32[]{:S(2)}, u32[]{:S(2)}) collective-permute-start(bf16[768,2048]{1,0:T(8,128)(2,1)} %slice.912), channel_id=1, source_target_pairs={{0,1},{1,0},{2,3},{3,2},{4,5},{5,4},{6,7},{7,6},{8,9},{9,8},{10,11... | collective-permute-start | bytes 9437192 | tf_op jit(solution)/shard_map/ppermute | solution.py:949
  888.1 64.1 %collective-permute-start.44 = (bf16[768,2048]{1,0:T(8,128)(2,1)}, bf16[768,2048]{1,0:T(8,128)(2,1)}, u32[]{:S(2)}, u32[]{:S(2)}) collective-permute-start(bf16[768,2048]{1,0:T(8,128)(2,1)} %slice.891), channel_id=1, source_target_pairs={{0,1},{1,0},{2,3},{3,2},{4,5},{5,4},{6,7},{7,6},{8,9},{9,8},{10,11... | collective-permute-start | bytes 9437192 | tf_op jit(solution)/shard_map/ppermute | solution.py:949
  911.2 18.1 %collective-permute-start.42 = (bf16[128,1920]{1,0:T(8,128)(2,1)S(1)}, bf16[128,1920]{1,0:T(8,128)(2,1)S(1)}, u32[]{:S(2)}, u32[]{:S(2)}) collective-permute-start(bf16[128,1920]{1,0:T(8,128)(2,1)S(1)} %pad_maximum_fusion.8), channel_id=1, source_target_pairs={{0,2},{2,0},{4,6},{6,4},{8,10},{10,8},{12,14},{14,12},{1,3},{3,1},... | collective-permute-start | bytes 1474568 | tf_op jit(solution)/shard_map/ppermute | solution.py:949
  930.3 25.6 %collective-permute-start.43 = (bf16[256,1920]{1,0:T(8,128)(2,1)}, bf16[256,1920]{1,0:T(8,128)(2,1)S(1)}, u32[]{:S(2)}, u32[]{:S(2)}) collective-permute-start(bf16[256,1920]{1,0:T(8,128)(2,1)} %get-tuple-element.154), channel_id=1, source_target_pairs={{0,1},{1,0},{2,3},{3,2},{4,5},{5,4},{6,7},{7,6},{8,9},{9,8},{10,11... | collective-permute-start | bytes 2949128 | tf_op jit(solution)/shard_map/ppermute | solution.py:949
  945.9 41.9 %collective-permute-start.55 = (bf16[384,2048]{1,0:T(8,128)(2,1)}, bf16[384,2048]{1,0:T(8,128)(2,1)}, u32[]{:S(2)}, u32[]{:S(2)}) collective-permute-start(bf16[384,2048]{1,0:T(8,128)(2,1)} %add_convert_fusion), channel_id=1, source_target_pairs={{0,4},{2,6},{4,0},{6,2},{8,12},{10,14},{12,8},{14,10},{1,5},{3,7},... | collective-permute-start | bytes 4718600 | tf_op jit(solution)/shard_map/ppermute | solution.py:949
  949.8 41.3 %collective-permute-start.50 = (bf16[384,2048]{1,0:T(8,128)(2,1)}, bf16[384,2048]{1,0:T(8,128)(2,1)}, u32[]{:S(2)}, u32[]{:S(2)}) collective-permute-start(bf16[384,2048]{1,0:T(8,128)(2,1)} %add_convert_fusion.1), channel_id=1, source_target_pairs={{0,16},{16,0},{1,17},{17,1},{2,18},{18,2},{3,19},{19,3},{4,20},{20... | collective-permute-start | bytes 4718600 | tf_op jit(solution)/shard_map/ppermute | solution.py:949
  955.9 37.8 %collective-permute-start.45 = (bf16[384,2048]{1,0:T(8,128)(2,1)}, bf16[384,2048]{1,0:T(8,128)(2,1)}, u32[]{:S(2)}, u32[]{:S(2)}) collective-permute-start(bf16[384,2048]{1,0:T(8,128)(2,1)} %add_convert_fusion.2), channel_id=1, source_target_pairs={{0,2},{2,0},{4,6},{6,4},{8,10},{10,8},{12,14},{14,12},{1,3},{3,1},... | collective-permute-start | bytes 4718600 | tf_op jit(solution)/shard_map/ppermute | solution.py:949
  989.8 17.1 %collective-permute-start.56 = (bf16[192,2048]{1,0:T(8,128)(2,1)S(1)}, bf16[192,2048]{1,0:T(8,128)(2,1)S(1)}, u32[]{:S(2)}, u32[]{:S(2)}) collective-permute-start(bf16[192,2048]{1,0:T(8,128)(2,1)S(1)} %add_convert_fusion.3), channel_id=1, source_target_pairs={{0,2},{2,0},{4,6},{6,4},{8,10},{10,8},{12,14},{14,12},{1,3},{3,1},... | collective-permute-start | bytes 2359304 | tf_op jit(solution)/shard_map/ppermute | solution.py:949
  993.1 17.3 %collective-permute-start.51 = (bf16[192,2048]{1,0:T(8,128)(2,1)S(1)}, bf16[192,2048]{1,0:T(8,128)(2,1)S(1)}, u32[]{:S(2)}, u32[]{:S(2)}) collective-permute-start(bf16[192,2048]{1,0:T(8,128)(2,1)S(1)} %add_convert_fusion.4), channel_id=1, source_target_pairs={{0,4},{2,6},{4,0},{6,2},{8,12},{10,14},{12,8},{14,10},{1,5},{3,7},... | collective-permute-start | bytes 2359304 | tf_op jit(solution)/shard_map/ppermute | solution.py:949
  995.7 20.5 %collective-permute-start.46 = (bf16[192,2048]{1,0:T(8,128)(2,1)S(1)}, bf16[192,2048]{1,0:T(8,128)(2,1)S(1)}, u32[]{:S(2)}, u32[]{:S(2)}) collective-permute-start(bf16[192,2048]{1,0:T(8,128)(2,1)S(1)} %add_convert_fusion.5), channel_id=1, source_target_pairs={{0,16},{16,0},{1,17},{17,1},{2,18},{18,2},{3,19},{19,3},{4,20},{20... | collective-permute-start | bytes 2359304 | tf_op jit(solution)/shard_map/ppermute | solution.py:949
  1023.3 19.5 %collective-permute-start.58 = (bf16[48,2048]{1,0:T(8,128)(2,1)S(1)}, bf16[48,2048]{1,0:T(8,128)(2,1)S(1)}, u32[]{:S(2)}, u32[]{:S(2)}) collective-permute-start(bf16[48,2048]{1,0:T(8,128)(2,1)S(1)} %add_convert_fusion.9), channel_id=1, source_target_pairs={{0,8},{2,10},{4,12},{6,14},{8,0},{10,2},{12,4},{14,6},{1,9},{3,11}... | collective-permute-start | bytes 589832 | tf_op jit(solution)/shard_map/ppermute | solution.py:949
  1025.5 21.5 %collective-permute-start.53 = (bf16[48,2048]{1,0:T(8,128)(2,1)S(1)}, bf16[48,2048]{1,0:T(8,128)(2,1)S(1)}, u32[]{:S(2)}, u32[]{:S(2)}) collective-permute-start(bf16[48,2048]{1,0:T(8,128)(2,1)S(1)} %add_convert_fusion.10), channel_id=1, source_target_pairs={{0,8},{2,10},{4,12},{6,14},{8,0},{10,2},{12,4},{14,6},{1,9},{3,11}... | collective-permute-start | bytes 589832 | tf_op jit(solution)/shard_map/ppermute | solution.py:949
  1028.8 20.6 %collective-permute-start.48 = (bf16[48,2048]{1,0:T(8,128)(2,1)S(1)}, bf16[48,2048]{1,0:T(8,128)(2,1)S(1)}, u32[]{:S(2)}, u32[]{:S(2)}) collective-permute-start(bf16[48,2048]{1,0:T(8,128)(2,1)S(1)} %add_convert_fusion.11), channel_id=1, source_target_pairs={{0,8},{2,10},{4,12},{6,14},{8,0},{10,2},{12,4},{14,6},{1,9},{3,11}... | collective-permute-start | bytes 589832 | tf_op jit(solution)/shard_map/ppermute | solution.py:949
  (81 other events, 1570.2 us)
Sparse Core Ops, SparseCore 0:
  10.9 85.5 all-gather.3
  99.3 182.9 all-gather.5
  285.2 94.2 all-gather.7
  478.6 155.9 reduce-scatter.7
  641.6 155.8 reduce-scatter.3
  803.3 166.9 reduce-scatter.5

commit v2 on v1

v2 whole, which is shorter than its diff:
```python
from functools import partial

import jax
import jax.numpy as jnp
from jax import lax
from jax.experimental import pallas as pl
from jax.experimental.pallas import tpu as pltpu
from jax.sharding import PartitionSpec as P

D = 1536
HEADS = 24
HD = 64
FF = 4096
CHANNELS = 4
PIN = 64
IMGS = 4
CELL = 16
LANES = 128
ALL = ("rows", "cols", "fsdp")

epsilon = 1e-06
highest = lax.Precision.HIGHEST
mask_level = 256.0
f32 = jnp.float32
bf16 = jnp.bfloat16
vmem_bytes = 60 * 1024 * 1024
SHRINK = 2
WAIT_FOR_GATE_UP = False


def estimate(flops, bytes_accessed, transcendentals):
    return pl.CostEstimate(
        flops=flops // SHRINK, bytes_accessed=bytes_accessed // SHRINK, transcendentals=0
    )


def ordered(kernel, count):
    return lambda *refs: kernel(*refs[count:])


def unread(arrays):
    return [pl.BlockSpec(memory_space=pl.ANY)] * len(arrays)


def held_until(value, *others):
    return pl.pallas_call(
        lambda *refs: None,
        in_specs=unread((value,) + others),
        out_specs=pl.BlockSpec(memory_space=pl.ANY),
        out_shape=jax.ShapeDtypeStruct(value.shape, value.dtype),
        input_output_aliases={0: 0},
        name="held_until",
    )(value, *others)


def dot_nn(left, right):
    return lax.dot_general(left, right, (((1,), (0,)), ((), ())), preferred_element_type=f32)


def dot_nt(left, right):
    return lax.dot_general(left, right, (((1,), (1,)), ((), ())), preferred_element_type=f32)


def dot_tn(left, right):
    return lax.dot_general(left, right, (((0,), (0,)), ((), ())), preferred_element_type=f32)


def row_mean(values):
    return jnp.mean(values, axis=-1, keepdims=True)


def inverse_rms(values):
    return lax.rsqrt(row_mean(values * values) + epsilon)


def whole(shape):
    zeros = (0,) * len(shape)
    return pl.BlockSpec(shape, lambda i: zeros, pipeline_mode=pl.Buffered(1))


def picked(image, table):
    choice = table[IMGS - 1 : IMGS, :]
    for index in range(IMGS - 2, -1, -1):
        choice = jnp.where(image == index, table[index : index + 1, :], choice)
    return choice


def image_sums(onehot, product):
    upper = product.astype(bf16)
    lower = (product - upper.astype(f32)).astype(bf16)
    return dot_nn(onehot, upper) + dot_nn(onehot, lower)


def matmul_rows(
    name, lefts, weight, kind, depth_tile, row_ins, consts, row_outs, sum_rows, chunk_body,
    before=None, after=None, block_scratch=(), wait=(), shape=None, column=0,
):
    tokens = lefts[0].shape[0]
    depth, width = shape or (weight.shape if kind == "nn" else weight.shape[::-1])
    block = min(256, tokens)
    chunk = 64
    tiles = depth // depth_tile
    blocks = tokens // block
    counts = (len(lefts), len(row_ins), len(consts), len(row_outs), len(sum_rows))
    ends = []
    for left in lefts:
        ends.append((ends[-1] if ends else 0) + left.shape[1] // depth_tile)
    starts = [0] + ends[:-1]

    def kernel(*refs):
        refs = list(refs)
        take = lambda n: [refs.pop(0) for _ in range(n)]
        left_refs = take(counts[0])
        weight_ref = take(1)[0]
        in_refs, const_refs = take(counts[1]), take(counts[2])
        out_refs, sum_refs = take(counts[3]), take(counts[4])
        total = refs.pop(0)
        scratch = refs
        step = pl.program_id(0)
        product = dot_nn if kind == "nn" else dot_nt

        @pl.when(step == 0)
        def _():
            total[...] = product(left_refs[0][...], weight_ref[...])
            for ref in sum_refs:
                ref[...] = jnp.zeros_like(ref)

        for left_ref, low, high in zip(left_refs, starts, ends):

            @pl.when((step >= max(low, 1)) & (step < high))
            def _():
                total[...] += product(left_ref[...], weight_ref[...])

        @pl.when(step >= tiles)
        def _():
            start = pl.multiple_of((step - tiles) * block, block)
            if before is not None:
                before(in_refs, const_refs, out_refs, scratch)
            for low in range(0, block, chunk):
                chunk_body(
                    total[pl.ds(pl.multiple_of(start + low, chunk), chunk), :],
                    pl.ds(low, chunk), in_refs, const_refs, out_refs, scratch,
                )
            if after is not None:
                after(in_refs, const_refs, out_refs, sum_refs, scratch)

    def row_map(i):
        return (jnp.maximum(i - tiles, 0), 0)

    def col_map(i):
        return (0, jnp.maximum(i - tiles, 0))

    def left_map(low, high):
        return lambda i: (0, jnp.clip(i - low, 0, high - low - 1))

    if kind == "nn":
        weight_spec = pl.BlockSpec(
            (depth_tile, width), lambda i: (jnp.minimum(i, tiles - 1), column)
        )
    else:
        weight_spec = pl.BlockSpec((width, depth_tile), lambda i: (0, jnp.minimum(i, tiles - 1)))
    in_specs = [
        pl.BlockSpec((tokens, depth_tile), left_map(low, high)) for low, high in zip(starts, ends)
    ]
    in_specs.append(weight_spec)
    for array in row_ins:
        if array.shape[0] == tokens:
            in_specs.append(pl.BlockSpec((block, array.shape[1]), row_map))
        else:
            in_specs.append(pl.BlockSpec((array.shape[0], block), col_map))
    in_specs += [whole(array.shape) for array in consts]
    out_specs = [pl.BlockSpec((block, cols), row_map) for cols, _ in row_outs]
    out_specs += [pl.BlockSpec((count, width), lambda i: (0, 0)) for count in sum_rows]
    out_shape = [jax.ShapeDtypeStruct((tokens, cols), kind_) for cols, kind_ in row_outs]
    out_shape += [jax.ShapeDtypeStruct((count, width), f32) for count in sum_rows]
    return pl.pallas_call(
        ordered(kernel, len(wait)),
        grid=(tiles + blocks,),
        in_specs=unread(wait) + in_specs,
        out_specs=out_specs,
        out_shape=out_shape,
        scratch_shapes=[pltpu.VMEM((tokens, width), f32)]
        + [pltpu.VMEM((block, cols), kind_) for cols, kind_ in block_scratch],
        compiler_params=pltpu.CompilerParams(vmem_limit_bytes=vmem_bytes),
        cost_estimate=estimate(
            flops=2 * tokens * width * depth,
            bytes_accessed=2 * (width * depth + tokens * depth) + 8 * tokens * width,
            transcendentals=0,
        ),
        name=name,
    )(*wait, *lefts, weight, *row_ins, *consts)


def swapped(values, first):
    return jnp.where(first, pltpu.roll(values, LANES - 16, 1), pltpu.roll(values, 16, 1))


def first_lanes(rows):
    lane = lax.broadcasted_iota(jnp.int32, (rows, LANES), 1)
    return lax.rem(lane, 32) < 16


def project_rows(patches, image, cosine, sine, w_embed, pre_table, w_project, gains):
    tokens = patches.shape[0]
    chunk = min(128, tokens)
    tile = 256
    blocks = D // tile

    def kernel(
        patches_ref, image_ref, cos_ref, sin_ref, embed_ref, pre_ref, weight_ref, gain_ref,
        embedded_ref, normed_ref, out_ref, hat_ref, inverse_ref, total,
    ):
        step = pl.program_id(0)

        @pl.when(step == 0)
        def _():
            total[...] = dot_nt(patches_ref[...], embed_ref[...])

            for low in range(0, tokens, chunk):
                rows = pl.ds(low, chunk)
                value = total[rows, :]
                embedded_ref[rows, :] = value
                normed_ref[rows, :] = (
                    value * inverse_rms(value) * picked(image_ref[rows, :1], pre_ref[...])
                ).astype(bf16)

        for index in range(blocks):
            cols = slice(index * tile, (index + 1) * tile)
            total[:, cols] = dot_nn(normed_ref[...], weight_ref[:, cols])

        @pl.when(step < 2)
        def _():
            gain = gain_ref[pl.ds(step, 1), :]

            for low in range(0, tokens, chunk):
                rows = pl.ds(low, chunk)
                value = total[rows, :]
                inverse = inverse_rms(value)
                hat = value * inverse
                hat_ref[rows, :] = hat.astype(bf16)
                inverse_ref[rows, :] = jnp.broadcast_to(inverse, (chunk, LANES))
                scaled = hat * gain
                first = first_lanes(chunk)
                cos_rows = cos_ref[rows, :]
                sin_rows = sin_ref[rows, :]
                for lane in range(0, D, LANES):
                    part = scaled[:, lane : lane + LANES]
                    turned = part * cos_rows + swapped(part, first) * sin_rows
                    out_ref[rows, lane : lane + LANES] = turned.astype(bf16)

        @pl.when(step == 2)
        def _():
            out_ref[...] = total[...].astype(bf16)

    return pl.pallas_call(
        kernel,
        grid=(3,),
        in_specs=[
            whole(patches.shape),
            whole(image.shape),
            whole(cosine.shape),
            whole(sine.shape),
            whole(w_embed.shape),
            whole(pre_table.shape),
            pl.BlockSpec((D, D), lambda i: (0, i)),
            whole(gains.shape),
        ],
        out_specs=[
            pl.BlockSpec((tokens, D), lambda i: (0, 0), pipeline_mode=pl.Buffered(1)),
            pl.BlockSpec((tokens, D), lambda i: (0, 0), pipeline_mode=pl.Buffered(1)),
            pl.BlockSpec((tokens, D), lambda i: (0, i)),
            pl.BlockSpec((tokens, D), lambda i: (0, jnp.minimum(i, 1))),
            pl.BlockSpec((tokens, LANES), lambda i: (0, jnp.minimum(i, 1))),
        ],
        out_shape=[
            jax.ShapeDtypeStruct((tokens, D), f32),
            jax.ShapeDtypeStruct((tokens, D), bf16),
            jax.ShapeDtypeStruct((tokens, 3 * D), bf16),
            jax.ShapeDtypeStruct((tokens, 2 * D), bf16),
            jax.ShapeDtypeStruct((tokens, 2 * LANES), f32),
        ],
        scratch_shapes=[pltpu.VMEM((tokens, D), f32)],
        compiler_params=pltpu.CompilerParams(vmem_limit_bytes=vmem_bytes),
        cost_estimate=estimate(
            flops=6 * tokens * D * D, bytes_accessed=6 * D * D + 24 * tokens * D, transcendentals=0
        ),
        name="project_rows",
    )(patches, image, cosine, sine, w_embed, pre_table, w_project, gains)


def arrange(pairs, place, used=None):
    count = len(pairs)
    devices = len(place[1][0])
    half = devices // 2
    stride = pairs[0][0].shape[0] // half
    share = stride if used is None else used
    width = pairs[0][0].shape[1]

    def kernel(*refs):
        me_ref, out_ref, sems = refs[2 * count :]
        step = pl.program_id(0)
        for part in range(count):

            @pl.when(step == part)
            def _():
                listed = []
                for index, mask in enumerate(place[1][part]):
                    low = pl.multiple_of((me_ref[0] ^ mask) * share, share)
                    listed.append(
                        pltpu.make_async_copy(
                            refs[2 * part + index // half].at[
                                pl.ds(index % half * stride, share), :
                            ],
                            out_ref.at[pl.ds(low, share), :],
                            sems.at[index],
                        )
                    )
                for copy in listed:
                    copy.start()
                for copy in listed:
                    copy.wait()

    return pl.pallas_call(
        kernel,
        grid=(count,),
        in_specs=[pl.BlockSpec(memory_space=pl.ANY)] * (2 * count)
        + [pl.BlockSpec(memory_space=pltpu.SMEM)],
        out_specs=pl.BlockSpec((devices * share, width), lambda i: (0, i)),
        out_shape=jax.ShapeDtypeStruct((devices * share, count * width), bf16),
        scratch_shapes=[pltpu.SemaphoreType.DMA((devices,))],
        compiler_params=pltpu.CompilerParams(vmem_limit_bytes=vmem_bytes),
        cost_estimate=estimate(
            flops=0, bytes_accessed=4 * devices * share * count * width, transcendentals=0
        ),
        name="arrange",
    )(*[value for pair in pairs for value in pair], place[0])


def small_grads_near(embed_back, patches, final, grad_patches, rows, place):
    masks = place[1][0]
    share = D // len(masks)
    half = len(masks) // 2

    def kernel(e_ref, p_ref, f_ref, g_ref, rows_ref, me_ref, kept_ref, sent_ref, held, sems):
        held[:, :PIN] = dot_tn(e_ref[...], p_ref[...])
        held[:, PIN : 2 * PIN] = dot_tn(f_ref[...], g_ref[...])
        tall = jnp.concatenate([rows_ref[...], jnp.zeros((LANES - 8, D), f32)], axis=0)
        held[:, LANES:] = tall.T
        listed = []
        for index, mask in enumerate(masks):
            low = pl.multiple_of((me_ref[0] ^ mask) * share, share)
            target = kept_ref if index < half else sent_ref
            listed.append(
                pltpu.make_async_copy(
                    held.at[pl.ds(low, share), :],
                    target.at[pl.ds(index % half * share, share), :],
                    sems.at[index],
                )
            )
        for copy in listed:
            copy.start()
        for copy in listed:
            copy.wait()

    return pl.pallas_call(
        kernel,
        in_specs=[pl.BlockSpec(memory_space=pltpu.VMEM)] * 5
        + [pl.BlockSpec(memory_space=pltpu.SMEM)],
        out_specs=[pl.BlockSpec(memory_space=pl.ANY)] * 2,
        out_shape=[jax.ShapeDtypeStruct((D // 2, 2 * LANES), f32)] * 2,
        scratch_shapes=[
            pltpu.VMEM((D, 2 * LANES), f32),
            pltpu.SemaphoreType.DMA((len(masks),)),
        ],
        compiler_params=pltpu.CompilerParams(vmem_limit_bytes=vmem_bytes),
        cost_estimate=estimate(
            flops=4 * patches.shape[0] * D * PIN, bytes_accessed=8 * patches.shape[0] * D,
            transcendentals=0,
        ),
        name="small_grads_near",
    )(embed_back, patches, final, grad_patches, rows, place[0])


def gain_rows(sums, factors, scales, turn_sums):
    wide = 5 * D // 2

    def kernel(*refs):
        sum_refs, factor_refs = refs[:5], refs[5:10]
        scale_refs, turn_ref, rows_ref, out_ref = refs[10:14], refs[14], refs[15], refs[16]
        rows_ref[...] = jnp.zeros_like(rows_ref)
        for spot, index in enumerate((0, 3, 4, 5)):
            rows_ref[index : index + 1, :] = jnp.sum(
                scale_refs[spot][...] * sum_refs[spot][:IMGS, :], axis=0, keepdims=True
            )
        rows_ref[1:3, :] = turn_ref[0:2, :]
        flat = [factor_refs[k][...] * sum_refs[k][:IMGS, :] for k in range(5)]
        middle = wide - 2 * D
        out_ref[:IMGS, :] = jnp.concatenate(flat[:2] + [flat[2][:, :middle]], axis=1).astype(bf16)
        out_ref[IMGS:, :] = jnp.concatenate([flat[2][:, middle:]] + flat[3:], axis=1).astype(bf16)

    return pl.pallas_call(
        kernel,
        out_shape=[
            jax.ShapeDtypeStruct((8, D), f32),
            jax.ShapeDtypeStruct((2 * IMGS, wide), bf16),
        ],
        name="gain_rows",
    )(*sums, *factors, *scales, turn_sums)


def gate_up_grads(normed_ffn, gate_back, up_back, after=()):
    tokens = normed_ffn.shape[0]
    tile = 1024
    tiles = FF // tile

    def kernel(left_ref, gate_ref, up_ref, out_ref):
        step = pl.program_id(0)

        @pl.when(step < tiles)
        def _():
            out_ref[...] = dot_tn(left_ref[...], gate_ref[...]).astype(bf16)

        @pl.when(step >= tiles)
        def _():
            out_ref[...] = dot_tn(left_ref[...], up_ref[...]).astype(bf16)

    return pl.pallas_call(
        ordered(kernel, len(after)),
        grid=(2 * tiles,),
        in_specs=unread(after)
        + [
            whole(normed_ffn.shape),
            pl.BlockSpec((tokens, tile), lambda i: (0, jnp.minimum(i, tiles - 1))),
            pl.BlockSpec((tokens, tile), lambda i: (0, jnp.maximum(i - tiles, 0))),
        ],
        out_specs=pl.BlockSpec((D, tile), lambda i: (0, i)),
        out_shape=jax.ShapeDtypeStruct((D, 2 * FF), bf16),
        compiler_params=pltpu.CompilerParams(vmem_limit_bytes=vmem_bytes),
        cost_estimate=estimate(
            flops=4 * tokens * D * FF, bytes_accessed=4 * D * FF + 4 * tokens * FF, transcendentals=0
        ),
        name="gate_up_grads",
    )(*after, normed_ffn, gate_back, up_back)


def masked_grads(left, right, column, width, place, which, whole_width, offset, into=(), after=()):
    tokens = left.shape[0]
    tile = width if width <= 768 else width // 2
    tiles = width // tile
    masks = place[1][which]
    share = D // len(masks)

    half = len(masks) // 2

    def kernel(left_ref, right_ref, me_ref, *rest):
        kept_ref, sent_ref, held, sems = rest[-4:]
        step = pl.program_id(0)

        def copies(number):
            slot = number % 2
            listed = []
            for index, mask in enumerate(masks):
                low = pl.multiple_of((me_ref[0] ^ mask) * share, share)
                target = kept_ref if index < half else sent_ref
                block = pl.ds(index % half * share, share)
                listed.append(
                    pltpu.make_async_copy(
                        held.at[slot, pl.ds(low, share), :],
                        target.at[block, pl.ds(offset + number * tile, tile)],
                        sems.at[slot, index],
                    )
                )
            return listed

        for number in range(tiles):

            @pl.when(step == number)
            def _():
                if number >= 2:
                    for copy in copies(number - 2):
                        copy.wait()
                held[number % 2] = dot_tn(left_ref[...], right_ref[...]).astype(bf16)
                for copy in copies(number):
                    copy.start()
                if number == tiles - 1:
                    for past in range(max(tiles - 2, 0), tiles):
                        for copy in copies(past):
                            copy.wait()

    return pl.pallas_call(
        ordered(kernel, len(after)),
        grid=(tiles,),
        in_specs=unread(after)
        + [
            whole(left.shape),
            pl.BlockSpec((tokens, tile), lambda i: (0, i + column * tiles)),
            pl.BlockSpec(memory_space=pltpu.SMEM),
        ]
        + unread(into),
        input_output_aliases={len(after) + 3 + index: index for index in range(len(into))},
        out_specs=[pl.BlockSpec(memory_space=pl.ANY)] * 2,
        out_shape=[jax.ShapeDtypeStruct((D // 2, whole_width), bf16)] * 2,
        scratch_shapes=[
            pltpu.VMEM((2, D, tile), bf16),
            pltpu.SemaphoreType.DMA((2, len(masks))),
        ],
        compiler_params=pltpu.CompilerParams(vmem_limit_bytes=vmem_bytes),
        cost_estimate=estimate(
            flops=2 * tokens * D * width,
            bytes_accessed=2 * (D + tokens) * width + 2 * tokens * D,
            transcendentals=0,
        ),
        name="masked_grads",
    )(*after, left, right, place[0], *into)


def third_grads(hidden, ffn_back, place, total, offset, after=()):
    tokens, length = hidden.shape
    width = D // 3
    masks = place[1]
    count = len(masks[0])
    share = length // count
    half = count // 2

    def kernel(left_ref, right_ref, me_ref, *rest):
        targets, held, sems = rest[:6], rest[6], rest[7]
        step = pl.program_id(0)

        def copies(part):
            listed = []
            for index, mask in enumerate(masks[part]):
                low = pl.multiple_of((me_ref[0] ^ mask) * share, share)
                listed.append(
                    pltpu.make_async_copy(
                        held.at[part, pl.ds(low, share), :],
                        targets[2 * part + index // half].at[
                            pl.ds(index % half * share, share), pl.ds(offset, width)
                        ],
                        sems.at[part, index],
                    )
                )
            return listed

        for part in range(3):

            @pl.when(step == part)
            def _():
                held[part] = dot_tn(left_ref[...], right_ref[...]).astype(bf16)
                for copy in copies(part):
                    copy.start()
                if part == 2:
                    for past in range(3):
                        for copy in copies(past):
                            copy.wait()

    results = pl.pallas_call(
        ordered(kernel, len(after)),
        grid=(3,),
        in_specs=unread(after)
        + [
            whole(hidden.shape),
            pl.BlockSpec((tokens, width), lambda i: (0, i)),
            pl.BlockSpec(memory_space=pltpu.SMEM),
        ],
        out_specs=[pl.BlockSpec(memory_space=pl.ANY)] * 6,
        out_shape=[jax.ShapeDtypeStruct((length // 2, total), bf16)] * 6,
        scratch_shapes=[
            pltpu.VMEM((3, length, width), bf16),
            pltpu.SemaphoreType.DMA((3, count)),
        ],
        compiler_params=pltpu.CompilerParams(vmem_limit_bytes=vmem_bytes),
        cost_estimate=estimate(
            flops=2 * tokens * D * length,
            bytes_accessed=2 * (tokens + D) * length + 2 * tokens * D,
            transcendentals=0,
        ),
        name="third_grads",
    )(*after, hidden, ffn_back, place[0])
    return [(results[2 * part], results[2 * part + 1]) for part in range(3)]


def head_lanes(shape, axis, head):
    lane = lax.broadcasted_iota(jnp.int32, shape, axis)
    return (lane >= HD) == (head == 1)


def attend(queries, keys, values, spec_of, width, query_image, key_image):
    length = queries.shape[0]
    pairs = width // LANES
    part = min(1024, length)

    def kernel(q_ref, k_ref, v_ref, qi_ref, ki_ref, out_ref, log_ref):
        key_block = k_ref[...]
        value_turned = v_ref[...].T
        key_parts = []
        value_parts = []
        for head in range(2):
            mine = head_lanes((length, LANES), 1, head)
            key_parts.append(jnp.where(mine, key_block, ki_ref[...]))
            value_parts.append(
                jnp.where(head_lanes((LANES, length), 0, head), value_turned, jnp.ones((), bf16))
            )

        for low in range(0, length, part):
            rows = pl.ds(low, part)
            query = q_ref[rows, :] * jnp.asarray(HD ** (-0.5), bf16)
            scores = []
            for head in range(2):
                mine = head_lanes((part, LANES), 1, head)
                scores.append(
                    dot_nt(key_parts[head], jnp.where(mine, query, qi_ref[rows, :]))
                )
            tops = [jnp.max(score, axis=0, keepdims=True) for score in scores]
            raised = [jnp.exp(score - top).astype(bf16) for score, top in zip(scores, tops)]
            results = [dot_nn(value_parts[head], raised[head]) for head in range(2)]
            turned = []
            for head in range(2):
                lane = HD * (1 - head)
                count = results[head][lane : lane + 1, :]
                turned.append(results[head][head * HD : (head + 1) * HD, :] / count)
                log_ref[0, pl.ds(head, 1), rows] = tops[head] + jnp.log(count)
            out_ref[rows, :] = jnp.concatenate(turned, axis=0).T.astype(bf16)

    return pl.pallas_call(
        kernel,
        grid=(pairs,),
        in_specs=[
            pl.BlockSpec((length, LANES), spec_of(0)),
            pl.BlockSpec((length, LANES), spec_of(1)),
            pl.BlockSpec((length, LANES), spec_of(2)),
            whole(query_image.shape),
            whole(key_image.shape),
        ],
        out_specs=[
            pl.BlockSpec((length, LANES), lambda i: (0, i)),
            pl.BlockSpec((1, 2, length), lambda i: (i, 0, 0)),
        ],
        out_shape=[
            jax.ShapeDtypeStruct((length, width), bf16),
            jax.ShapeDtypeStruct((pairs, 2, length), f32),
        ],
        compiler_params=pltpu.CompilerParams(vmem_limit_bytes=vmem_bytes),
        cost_estimate=estimate(
            flops=16 * pairs * length * length * HD * 4,
            bytes_accessed=8 * length * width,
            transcendentals=2 * pairs * length * length,
        ),
        name="attend",
    )(queries, keys, values, query_image, key_image)


def attend_back(
    queries, keys, values, spec_of, width, attended, grads, log_total, query_image, key_image,
    pairs, first, before, after=(),
):
    length = queries.shape[0]
    part = min(1024, length)
    score_scale = HD ** (-0.5)

    def kernel(
        q_ref, k_ref, v_ref, o_ref, g_ref, log_ref, qi_ref, ki_ref, *rest
    ):
        dq_ref, dk_ref, dv_ref, key_sum, value_sum = rest[-5:]
        key_block = k_ref[...]
        value_block = v_ref[...]
        key_turned = key_block.T
        key_parts = []
        value_parts = []
        for head in range(2):
            mine = head_lanes((length, LANES), 1, head)
            key_parts.append(jnp.where(mine, key_block, ki_ref[...]))
            value_parts.append(jnp.where(mine, value_block, jnp.zeros((), bf16)))
        key_sum[...] = jnp.zeros_like(key_sum)
        value_sum[...] = jnp.zeros_like(value_sum)
        sel_rows = lax.broadcasted_iota(jnp.int32, (8, LANES), 0)
        sel_lanes = lax.broadcasted_iota(jnp.int32, (8, LANES), 1)
        select = jnp.where(
            sel_rows == jnp.where(sel_lanes >= HD, 1, 0), jnp.ones((), f32), jnp.zeros((), f32)
        ).astype(bf16)

        for low in range(0, length, part):
            rows = pl.ds(low, part)
            query = q_ref[rows, :] * jnp.asarray(score_scale, bf16)
            grad = g_ref[rows, :]
            product = grad.astype(f32) * o_ref[rows, :].astype(f32)
            upper = product.astype(bf16)
            lower = (product - upper.astype(f32)).astype(bf16)
            inner = dot_nt(select, upper) + dot_nt(select, lower)
            turned = []
            for head in range(2):
                mine = head_lanes((part, LANES), 1, head)
                scores = dot_nt(key_parts[head], jnp.where(mine, query, qi_ref[rows, :]))
                chances = jnp.exp(scores - log_ref[0, pl.ds(head, 1), rows])
                grad_chances = dot_nt(value_parts[head], grad)
                grad_scores = (chances * (grad_chances - inner[head : head + 1, :])).astype(bf16)
                value_sum[head] += dot_nn(chances.astype(bf16), grad)
                key_sum[head] += dot_nn(grad_scores, query)
                result = dot_nn(key_turned, grad_scores)
                turned.append(result[head * HD : (head + 1) * HD, :])
            dq_ref[rows, :] = (jnp.concatenate(turned, axis=0).T * score_scale).astype(bf16)
        lower_lanes = head_lanes((length, LANES), 1, 0)
        dk_ref[...] = jnp.where(lower_lanes, key_sum[0], key_sum[1]).astype(bf16)
        dv_ref[...] = jnp.where(lower_lanes, value_sum[0], value_sum[1]).astype(bf16)

    column = pl.BlockSpec((length, LANES), lambda i: (0, i + first))
    moved = lambda which: (lambda i: spec_of(which)(i + first))
    held = list(before or [])
    return pl.pallas_call(
        ordered(kernel, len(after)),
        grid=(pairs,),
        in_specs=unread(after)
        + [
            pl.BlockSpec((length, LANES), moved(0)),
            pl.BlockSpec((length, LANES), moved(1)),
            pl.BlockSpec((length, LANES), moved(2)),
            column,
            column,
            pl.BlockSpec((1, 2, length), lambda i: (i + first, 0, 0)),
            whole(query_image.shape),
            whole(key_image.shape),
        ]
        + [pl.BlockSpec(memory_space=pl.ANY)] * len(held),
        input_output_aliases={len(after) + 8 + index: index for index in range(len(held))},
        out_specs=[column] * 3,
        out_shape=[jax.ShapeDtypeStruct((length, width), bf16)] * 3,
        scratch_shapes=[
            pltpu.VMEM((2, length, LANES), f32),
            pltpu.VMEM((2, length, LANES), f32),
        ],
        compiler_params=pltpu.CompilerParams(vmem_limit_bytes=vmem_bytes),
        cost_estimate=estimate(
            flops=40 * pairs * length * length * HD * 4,
            bytes_accessed=16 * length * width,
            transcendentals=2 * pairs * length * length,
        ),
        name="attend_back",
    )(*after, queries, keys, values, attended, grads, log_total, query_image, key_image, *held)


def gate_up_rows(normed, weight):
    tokens = normed.shape[0]
    tile = 512
    tiles = FF // tile

    def kernel(left_ref, gate_weight, up_weight, hidden_ref, gate_ref, up_ref):
        gate = dot_nn(left_ref[...], gate_weight[...])
        up = dot_nn(left_ref[...], up_weight[...])
        hidden_ref[...] = (gate / (1.0 + jnp.exp(-gate)) * up).astype(bf16)
        gate_ref[...] = gate.astype(bf16)
        up_ref[...] = up.astype(bf16)

    out = pl.BlockSpec((tokens, tile), lambda i: (0, i))
    return pl.pallas_call(
        kernel,
        grid=(tiles,),
        in_specs=[
            whole(normed.shape),
            pl.BlockSpec((D, tile), lambda i: (0, i)),
            pl.BlockSpec((D, tile), lambda i: (0, i + tiles)),
        ],
        out_specs=[out] * 3,
        out_shape=[jax.ShapeDtypeStruct((tokens, FF), bf16)] * 3,
        compiler_params=pltpu.CompilerParams(vmem_limit_bytes=vmem_bytes),
        cost_estimate=estimate(
            flops=4 * tokens * D * FF, bytes_accessed=4 * D * FF + 6 * tokens * FF, transcendentals=0
        ),
        name="gate_up_rows",
    )(normed, weight, weight)


def gate_up_back(ffn_back, weight, gate, up, after=()):
    tokens = ffn_back.shape[0]
    tile = 512
    tiles = FF // tile

    def kernel(left_ref, weight_ref, gate_ref, up_ref, gate_back, up_back):
        grad = dot_nt(left_ref[...], weight_ref[...])
        gate_rows = gate_ref[...].astype(f32)
        share = 1.0 / (1.0 + jnp.exp(-gate_rows))
        active = gate_rows * share
        up_back[...] = (grad * active).astype(bf16)
        slope = share + active * (1.0 - share)
        gate_back[...] = (grad * up_ref[...].astype(f32) * slope).astype(bf16)

    column = pl.BlockSpec((tokens, tile), lambda i: (0, i))
    return pl.pallas_call(
        ordered(kernel, len(after)),
        grid=(tiles,),
        in_specs=unread(after)
        + [
            whole(ffn_back.shape),
            pl.BlockSpec((tile, D), lambda i: (i, 0)),
            column,
            column,
        ],
        out_specs=[column] * 2,
        out_shape=[jax.ShapeDtypeStruct((tokens, FF), bf16)] * 2,
        compiler_params=pltpu.CompilerParams(vmem_limit_bytes=vmem_bytes),
        cost_estimate=estimate(
            flops=2 * tokens * D * FF, bytes_accessed=2 * D * FF + 8 * tokens * FF, transcendentals=0
        ),
        name="gate_up_back",
    )(*after, ffn_back, weight, gate, up)


def output_rows(attended, weight, column, embedded, image, post_table, pre_table):
    def body(value, rows, ins, consts, outs, scratch):
        hat = value * inverse_rms(value)
        image_rows = ins[1][rows, :1]
        mixed = ins[0][rows, :] + picked(image_rows, consts[0][...]) * hat
        outs[0][rows, :] = value
        outs[1][rows, :] = mixed
        outs[2][rows, :] = (
            mixed * inverse_rms(mixed) * picked(image_rows, consts[1][...])
        ).astype(bf16)

    return matmul_rows(
        "output_rows", [attended], weight, "nn", 768, [embedded, image], [post_table, pre_table],
        [(D, f32), (D, f32), (D, bf16)], [], body, shape=(D, D), column=column,
    )


def down_rows(hidden, weight, mixed, image, onehot, grad_patches, post_table, out_table, w_final):
    def before(ins, consts, outs, scratch):
        scratch[0][...] = dot_nt(ins[3][...], consts[2][...])

    def body(value, rows, ins, consts, outs, scratch):
        inverse = inverse_rms(value)
        hat = value * inverse
        image_rows = ins[1][rows, :1]
        post = picked(image_rows, consts[0][...])
        final_state = ins[0][rows, :] + post * hat
        centred = final_state - row_mean(final_state)
        spread = inverse_rms(centred)
        levelled = centred * spread
        scale = picked(image_rows, consts[1][...])
        outs[0][rows, :] = (levelled * scale).astype(bf16)
        grad = scratch[0][rows, :]
        scratch[1][rows, :] = grad * levelled
        back = grad * scale
        late = spread * (back - row_mean(back) - levelled * row_mean(back * levelled))
        outs[1][rows, :] = late
        scratch[2][rows, :] = late * hat
        back = late * post
        outs[2][rows, :] = (inverse * (back - hat * row_mean(back * hat))).astype(bf16)

    def after(ins, consts, outs, sums, scratch):
        outs[3][...] = dot_nn(outs[0][...], consts[2][...]).astype(bf16)
        one = ins[2][...]
        sums[0][...] += image_sums(one, scratch[1][...])
        sums[1][...] += image_sums(one, scratch[2][...])

    return matmul_rows(
        "down_rows", [hidden], weight, "nn", 1024, [mixed, image, onehot, grad_patches],
        [post_table, out_table, w_final],
        [(D, bf16), (D, f32), (D, bf16), (PIN, bf16)], [8, 8], body,
        before=before, after=after, block_scratch=[(D, f32)] * 3,
    )


def ffn_back_rows(
    gate_back, up_back, weight, late, mixed, attn_out, image, onehot, post_table, pre_table,
    wait=(),
):
    def body(value, rows, ins, consts, outs, scratch):
        image_rows = ins[3][rows, :1]
        mixed_rows = ins[1][rows, :]
        inverse = inverse_rms(mixed_rows)
        hat = mixed_rows * inverse
        scratch[0][rows, :] = value * hat
        back = value * picked(image_rows, consts[1][...])
        early = ins[0][rows, :] + inverse * (back - hat * row_mean(back * hat))
        outs[0][rows, :] = early
        attn_rows = ins[2][rows, :]
        inverse = inverse_rms(attn_rows)
        hat = attn_rows * inverse
        scratch[1][rows, :] = early * hat
        back = early * picked(image_rows, consts[0][...])
        outs[1][rows, :] = (inverse * (back - hat * row_mean(back * hat))).astype(bf16)

    def after(ins, consts, outs, sums, scratch):
        one = ins[4][...]
        sums[0][...] += image_sums(one, scratch[0][...])
        sums[1][...] += image_sums(one, scratch[1][...])

    return matmul_rows(
        "ffn_back_rows", [gate_back, up_back], weight, "nt", 1024,
        [late, mixed, attn_out, image, onehot], [post_table, pre_table],
        [(D, f32), (D, bf16)], [8, 8], body, after=after, block_scratch=[(D, f32)] * 2,
        wait=wait,
    )


def project_back_rows(
    backs, weight, embedded, late, image, onehot, pre_table, w_embed, wait=()
):
    def body(value, rows, ins, consts, outs, scratch):
        embedded_rows = ins[0][rows, :]
        inverse = inverse_rms(embedded_rows)
        hat = embedded_rows * inverse
        scratch[0][rows, :] = value * hat
        back = value * picked(ins[2][rows, :1], consts[0][...])
        early = inverse * (back - hat * row_mean(back * hat))
        outs[0][rows, :] = (early + ins[1][rows, :]).astype(bf16)

    def after(ins, consts, outs, sums, scratch):
        outs[1][...] = dot_nn(outs[0][...], consts[1][...]).astype(bf16)
        sums[0][...] += image_sums(ins[3][...], scratch[0][...])

    return matmul_rows(
        "project_back_rows", backs, weight, "nt", D,
        [embedded, late, image, onehot], [pre_table, w_embed],
        [(D, bf16), (PIN, bf16)], [8], body, after=after, block_scratch=[(D, f32)], wait=wait,
        shape=(3 * D, D),
    )


def turn_back(grad_q, grad_k, hats, inverses, cosine, sine, gains, after=()):
    tokens = grad_q.shape[0]
    block = min(256, tokens)
    chunk = 64

    def kernel(gq_ref, gk_ref, hat_ref, inv_ref, cos_ref, sin_ref, gain_ref, out_ref, sum_ref):
        @pl.when(pl.program_id(0) == 0)
        def _():
            sum_ref[...] = jnp.zeros_like(sum_ref)

        for which, grad_ref in enumerate((gq_ref, gk_ref)):
            gain = gain_ref[which : which + 1, :]

            total = jnp.zeros((8, D), f32)
            for low in range(0, block, chunk):
                rows = pl.ds(low, chunk)
                first = first_lanes(chunk)
                cos_rows = cos_ref[rows, :]
                sin_rows = sin_ref[rows, :]
                pieces = []
                for lane in range(0, D, LANES):
                    part = grad_ref[rows, lane : lane + LANES].astype(f32)
                    pieces.append(part * cos_rows - swapped(part, first) * sin_rows)
                turned = jnp.concatenate(pieces, axis=1)
                hat = hat_ref[rows, which * D : (which + 1) * D].astype(f32)
                inverse = inv_ref[rows, which * LANES : which * LANES + 1]
                back = turned * gain
                out_ref[rows, which * D : (which + 1) * D] = (
                    inverse * (back - hat * row_mean(back * hat))
                ).astype(bf16)
                total = total + jnp.sum((turned * hat).reshape(chunk // 8, 8, D), axis=0)
            sum_ref[which : which + 1, :] += jnp.sum(total, axis=0, keepdims=True)

    row = lambda cols: pl.BlockSpec((block, cols), lambda i: (i, 0))
    return pl.pallas_call(
        ordered(kernel, len(after)),
        grid=(tokens // block,),
        in_specs=unread(after)
        + [
            row(D), row(D), row(2 * D), row(2 * LANES), row(LANES), row(LANES), whole(gains.shape)
        ],
        out_specs=[row(2 * D), pl.BlockSpec((8, D), lambda i: (0, 0))],
        out_shape=[
            jax.ShapeDtypeStruct((tokens, 2 * D), bf16),
            jax.ShapeDtypeStruct((8, D), f32),
        ],
        compiler_params=pltpu.CompilerParams(vmem_limit_bytes=vmem_bytes),
        cost_estimate=estimate(
            flops=40 * tokens * D, bytes_accessed=12 * tokens * D, transcendentals=0
        ),
        name="turn_back",
    )(*after, grad_q, grad_k, hats, inverses, cosine, sine, gains)


def to_strips(tiles):
    micros = tiles.shape[0]
    count = lax.axis_size("rows")
    parts = count // micros
    me = lax.axis_index("rows")
    slots = []
    for shift in range(micros):
        pairs = [(q, ((q % micros - shift) % micros) * parts + q // micros) for q in range(count)]
        sent = lax.dynamic_index_in_dim(tiles, (me % micros - shift) % micros, 0, keepdims=False)
        if any(a != b for a, b in pairs):
            sent = lax.ppermute(sent, "rows", pairs)
        slots.append(sent)
    stacked = jnp.stack(slots)
    order = (jnp.arange(micros) - me // parts) % micros
    ordered = jnp.concatenate(
        [lax.dynamic_index_in_dim(stacked, order[d], 0) for d in range(micros)], axis=0
    )
    kinds, height, width = ordered.shape[1:]
    return ordered.transpose(1, 0, 2, 3).reshape(kinds, micros * height, width)


def from_strips(strip, micros):
    count = lax.axis_size("rows")
    parts = count // micros
    me = lax.axis_index("rows")
    kinds, height, width = strip.shape
    tiles = strip.reshape(kinds, micros, height // micros, width).transpose(1, 0, 2, 3)
    slots = []
    for shift in range(micros):
        pairs = [(((q % micros - shift) % micros) * parts + q // micros, q) for q in range(count)]
        sent = lax.dynamic_index_in_dim(tiles, (me // parts + shift) % micros, 0, keepdims=False)
        if any(a != b for a, b in pairs):
            sent = lax.ppermute(sent, "rows", pairs)
        slots.append(sent)
    stacked = jnp.stack(slots)
    return jnp.concatenate(
        [
            lax.dynamic_index_in_dim(stacked, (me % micros - m) % micros, 0)
            for m in range(micros)
        ],
        axis=0,
    )


def neighbour_pairs(axis, parts):
    count = lax.axis_size(axis)
    ups = [(i, i + 1) for i in range(count - 1) if (i + 1) % parts != 0]
    return ups, [(b, a) for a, b in ups]


def neighbours(values, axis, dim, parts):
    ups, downs = neighbour_pairs(axis, parts)
    head = lax.slice_in_dim(values, 0, 1, axis=dim)
    tail = lax.slice_in_dim(values, values.shape[dim] - 1, values.shape[dim], axis=dim)
    if len(ups) == 0:
        return jnp.zeros_like(head), jnp.zeros_like(tail)
    return lax.ppermute(tail, axis, ups), lax.ppermute(head, axis, downs)


def sides(parts):
    return (("cols", 1, lax.axis_size("cols")), ("rows", 0, parts))


def window_filter(turned):
    values = jnp.eye(PIN, dtype=bf16).reshape(PIN, CHANNELS, 4, 4)
    return values[:, :, ::-1, ::-1].transpose(1, 0, 2, 3) if turned else values


def extract_patches(strip, parts):
    for axis, dim, span in sides(parts):
        before, after = neighbours(strip, axis, dim + 1, span)
        strip = jnp.concatenate([before, strip, after], axis=dim + 1)
    kinds, height, width = strip.shape
    sets = kinds // CHANNELS
    rows, cols = height // 2 - 1, width // 2 - 1
    windows = lax.conv_general_dilated(
        strip.reshape(sets, CHANNELS, height, width),
        window_filter(False),
        (2, 2),
        "VALID",
        dimension_numbers=("NCHW", "OIHW", "NHWC"),
        preferred_element_type=f32,
    )
    return windows.astype(bf16).reshape(sets, rows * cols, PIN)


def fold_patches(pieces, rows, cols):
    canvas = lax.conv_general_dilated(
        pieces.reshape(1, rows, cols, PIN),
        window_filter(True),
        (1, 1),
        ((3, 3), (3, 3)),
        lhs_dilation=(2, 2),
        dimension_numbers=("NHWC", "OIHW", "NCHW"),
        preferred_element_type=f32,
    )
    return canvas[0]


def share_rims(canvas, parts):
    for axis, dim, span in sides(parts):
        dim += 1
        before, after = neighbours(canvas, axis, dim, span)
        size = canvas.shape[dim]
        middle = list(canvas.shape)
        middle[dim] = size - 4
        canvas = lax.slice_in_dim(canvas, 1, size - 1, axis=dim)
        canvas = canvas + jnp.concatenate([before, jnp.zeros(middle, f32), after], axis=dim)
    return canvas


def strip_layout(heights, seq_rows):
    starts = jnp.cumsum(heights) - heights
    rows_all = jnp.arange(seq_rows, dtype=jnp.int32)
    image_of = jnp.sum((rows_all[:, None] >= starts[None, 1:]).astype(jnp.int32), axis=1)
    start_of = jnp.sum(
        jnp.where(
            image_of[:, None] == jnp.arange(IMGS, dtype=jnp.int32)[None, :], starts[None, :], 0
        ),
        axis=1,
    )
    return (image_of, rows_all - start_of)


def rope_tables(row_place, column):
    quarter = HD // 4
    lane = jnp.arange(LANES, dtype=jnp.int32)
    frequency = 10000.0 ** (-(lane % quarter).astype(f32) / quarter)
    spot = jnp.where((lane % HD < HD // 2)[None, :], row_place[:, None], column[:, None])
    angles = spot.astype(f32) * frequency[None, :]
    sign = jnp.where(lane % 32 < 16, -1.0, 1.0)
    return (jnp.cos(angles), jnp.sin(angles) * sign[None, :])


def gather_all(shard):
    return lax.all_gather(shard, ALL, axis=0, tiled=True)


def scatter_all(part):
    return lax.psum_scatter(part, ALL, scatter_dimension=0, tiled=True)


def bits_of(axis):
    return lax.axis_size(axis).bit_length() - 1


def orders():
    first = [("fsdp", bit) for bit in range(bits_of("fsdp"))]
    main = [("cols", 0), ("rows", 0), ("cols", 1)]
    rest = [("rows", bit) for bit in range(1, bits_of("rows"))]
    rest += [("cols", bit) for bit in range(2, bits_of("cols"))]
    return [first + main[turn:] + main[:turn] + rest for turn in range(3)]


def block_masks(order):
    base = {"fsdp": 0, "cols": bits_of("fsdp"), "rows": bits_of("fsdp") + bits_of("cols")}
    steps = len(order)
    return [
        sum(
            ((index >> (steps - 1 - step)) & 1) << (base[axis] + bit)
            for step, (axis, bit) in enumerate(order)
        )
        for index in range(1 << steps)
    ]


def swap(values, axis, bit):
    return lax.ppermute(values, axis, [(i, i ^ (1 << bit)) for i in range(lax.axis_size(axis))])


class Gather:
    def __init__(self, values, picks):
        self.steps = [list(reversed(order)) for order in picks]
        self.held = list(values)
        self.step = 0
        self.received = []

    def start(self):
        self.received = [
            swap(value, *self.steps[k][self.step]) for k, value in enumerate(self.held)
        ]

    def finish(self):
        self.step += 1
        if self.done():
            self.held = list(zip(self.held, self.received))
        else:
            self.held = [jnp.concatenate(pair, axis=0) for pair in zip(self.held, self.received)]

    def done(self):
        return self.step == len(self.steps[0])


class Scatter:
    def __init__(self, halves, picks):
        self.steps = picks
        self.terms = [[kept] for kept, _ in halves]
        self.sent = [sent for _, sent in halves]
        self.kinds = [kept.dtype for kept, _ in halves]
        self.step = 0
        self.received = []

    def total(self, values):
        return sum(value.astype(f32) for value in values)

    def sent_next(self):
        sent = []
        for terms, kind in zip(self.terms, self.kinds):
            half = terms[0].shape[0] // 2
            sent.append(self.total([term[half:] for term in terms]).astype(kind))
        return sent

    def start(self):
        if self.step > 0:
            self.sent = self.sent_next()
            self.terms = [[term[: term.shape[0] // 2] for term in terms] for terms in self.terms]
        self.received = [
            swap(sent, *order[self.step]) for sent, order in zip(self.sent, self.steps)
        ]

    def finish(self):
        self.step += 1
        self.terms = [terms + [value] for terms, value in zip(self.terms, self.received)]

    def done(self):
        return self.step == len(self.steps[0])

    def sums(self):
        return [self.total(values) for values in self.terms]


def halves_of(values):
    half = values.shape[0] // 2
    return values[:half], values[half:]


def wait_for(chain, *others):
    chain.received[0] = held_until(chain.received[0], *others)


def step_all(value, *chains):
    for chain in chains:
        wait_for(chain, value)
    go_on(*chains)


def arrived(*chains):
    return tuple(value for chain in chains for value in chain.received)


def go_on(*chains):
    for chain in chains:
        chain.finish()
        if not chain.done():
            chain.start()


def exchange_heads(parts, micros):
    groups = [[m * parts + s for s in range(parts)] for m in range(micros)]

    def spread(values):
        return lax.all_to_all(
            values, "rows", split_axis=1, concat_axis=0, tiled=True, axis_index_groups=groups
        )

    def collect(values):
        return lax.all_to_all(
            values, "rows", split_axis=0, concat_axis=1, tiled=True, axis_index_groups=groups
        )

    return spread, collect


def shards(
    latent,
    time_embed,
    image_rows,
    pred_grad,
    embed_weight,
    adaptive_weight,
    project_weight,
    output_weight,
    gate_up_weight,
    down_weight,
    final_weight,
    norm_gains,
):
    micros = latent.shape[0]
    row_devices = lax.axis_size("rows")
    parts = row_devices // micros
    row_index = lax.axis_index("rows")
    micro, piece = row_index // parts, row_index % parts
    device = (row_index * lax.axis_size("cols") + lax.axis_index("cols")) * lax.axis_size(
        "fsdp"
    ) + lax.axis_index("fsdp")
    rows = latent.shape[3] // 2 * micros
    cols = latent.shape[4] // 2
    tokens = rows * cols
    seq_rows = rows * parts
    length = seq_rows * cols

    devices = lax.axis_size(ALL)
    share = D // devices
    near = share % 16 == 0 and FF // devices % LANES == 0
    picks = orders()
    place = None
    if near:
        place = (device.astype(jnp.int32).reshape(1), [block_masks(order) for order in picks])

    tiles = jnp.concatenate([latent[:, 0], pred_grad[:, 0]], axis=1)
    small = jnp.concatenate(
        [
            embed_weight,
            final_weight,
            norm_gains,
            jnp.zeros((norm_gains.shape[0], 2 * LANES - 2 * PIN - 6), bf16),
        ],
        axis=1,
    )
    temb = lax.dynamic_index_in_dim(time_embed, micro, 0, keepdims=False)[0, 0]
    condition = jax.nn.silu(temb).astype(bf16)
    rows_held = adaptive_weight.shape[0]
    if near:
        wide = condition.reshape(-1, 2 * LANES)
        side = Gather([jnp.concatenate([small, wide], axis=0)], picks[:1])
        side.start()
        while not side.done():
            go_on(side)
        small_pairs = side.held
        both = jnp.concatenate(side.held[0], axis=0)
        both = both.reshape(devices, share + wide.shape[0], 2 * LANES)
        conditions = both[:, share:].reshape(devices * IMGS, condition.shape[1])
        conditions = lax.dynamic_slice_in_dim(conditions, device * rows_held, rows_held, axis=1)
        per_image = dot_nn(conditions, adaptive_weight)
        side = Scatter([halves_of(per_image)], picks[:1])
        side.start()
        while not side.done():
            go_on(side)
        joined = gather_all(jnp.concatenate([project_weight, output_weight], axis=1))
        w_project = joined
        w_output = joined[:, 3 * D :]
        w_down = gather_all(down_weight)
        per_image = side.sums()[0]
        source = jnp.asarray(place[1][0], jnp.int32)
        count = len(picks[0])
        small = arrange(small_pairs, place, share)
    else:
        small = gather_all(small)
        conditions = gather_all(condition)
        conditions = lax.dynamic_slice_in_dim(conditions, device * rows_held, rows_held, axis=1)
        per_image = scatter_all(dot_nn(conditions, adaptive_weight))
        w_project = gather_all(project_weight)
        w_output = gather_all(output_weight)
        joined = w_output
        w_down = gather_all(down_weight)
    w_embed = small[:, :PIN]
    w_final = small[:, PIN : 2 * PIN]
    gains = small[:, 2 * PIN : 2 * PIN + 6].astype(f32).T

    w_gate_up = gather_all(gate_up_weight)

    patches, grad_patches = extract_patches(to_strips(tiles), parts)

    heights = lax.dynamic_index_in_dim(image_rows, micro, 0, keepdims=False)[0, 0]
    row_image, row_place = strip_layout(heights, seq_rows)
    first_row = piece * rows
    my_image = lax.dynamic_slice_in_dim(row_image, first_row, rows)
    my_place = lax.dynamic_slice_in_dim(row_place, first_row, rows)
    token_image = jnp.repeat(my_image, cols)
    cosine, sine = rope_tables(
        jnp.repeat(my_place, cols), jnp.tile(jnp.arange(cols, dtype=jnp.int32), rows)
    )
    image = jnp.broadcast_to(token_image[:, None], (tokens, LANES))
    onehot = (token_image[None, :] == jnp.arange(8, dtype=jnp.int32)[:, None]).astype(bf16)
    strip_image = jnp.repeat(row_image, cols)
    head_lane = jnp.arange(LANES, dtype=jnp.int32)[None, :] % HD
    same = strip_image[:, None] == head_lane
    query_image = jnp.where(same, -mask_level, 0.0).astype(bf16)
    key_image = jnp.where(same | (head_lane >= IMGS), 0.0, mask_level).astype(bf16)

    modulation = per_image.reshape(IMGS, 5, D)
    scale_attn = 1.0 + modulation[:, 0]
    gate_attn = jnp.tanh(modulation[:, 1])
    scale_ffn = 1.0 + modulation[:, 2]
    gate_ffn = jnp.tanh(modulation[:, 3])
    scale_out = 1.0 + modulation[:, 4]
    table = lambda values: jnp.concatenate([values, values], axis=0)
    attn_pre = table(scale_attn * gains[0])
    attn_post = table(gate_attn * gains[3])
    ffn_pre = table(scale_ffn * gains[4])
    ffn_post = table(gate_ffn * gains[5])
    out_scale = table(scale_out)
    turn_gains = jnp.concatenate([gains[1:3], jnp.zeros((6, D), f32)], axis=0)
    factors = [
        jnp.broadcast_to(gains[0], (IMGS, D)),
        (1.0 - gate_attn * gate_attn) * gains[3],
        jnp.broadcast_to(gains[4], (IMGS, D)),
        (1.0 - gate_ffn * gate_ffn) * gains[5],
        jnp.ones((IMGS, D), f32),
    ]

    embedded, normed, projected, hats, inverses = project_rows(
        patches, image, cosine, sine, w_embed, attn_pre, w_project, turn_gains
    )
    if parts == 1:
        pairs = D // LANES
        heads = (projected, projected, projected)
        spec_of = lambda which: (lambda i: (0, which * pairs + i))
        width = D
    else:
        spread, collect = exchange_heads(parts, micros)
        heads = tuple(spread(projected[:, w * D : (w + 1) * D]) for w in range(3))
        spec_of = lambda which: (lambda i: (0, i))
        width = D // parts
    attended_heads, log_total = attend(*heads, spec_of, width, query_image, key_image)
    attended = attended_heads if parts == 1 else collect(attended_heads)
    attn_out, mixed, normed_ffn = output_rows(
        attended, joined, 3 if near else 0, embedded, image, attn_post, ffn_pre
    )
    hidden, gate, up = gate_up_rows(normed_ffn, w_gate_up)
    final, late, ffn_back, pieces, sum_out, sum_ffn_post = down_rows(
        hidden, w_down, mixed, image, onehot, grad_patches, ffn_post, out_scale, w_final
    )
    if near:
        down_parts = third_grads(hidden, ffn_back, place, D // 3, 0)
        down_chain = Scatter(down_parts, picks)
        down_chain.start()
        gate_back, up_back = gate_up_back(
            ffn_back, w_down, gate, up, after=[part[0] for part in down_parts]
        )
        waits = arrived(down_chain)
        step_all(gate_back, down_chain)
        waits += tuple(down_chain.sent)
        gate_up_grad = gate_up_grads(normed_ffn, gate_back, up_back, after=waits)
        gate_up_share = scatter_all(gate_up_grad)
        waits = arrived(down_chain) + (gate_up_grad,)
        step_all(gate_up_grad, down_chain)
        waits += tuple(down_chain.sent)
    else:
        down_share = scatter_all(dot_tn(hidden, ffn_back).astype(bf16))
        gate_back, up_back = gate_up_back(ffn_back, w_down, gate, up)
        gate_up_share = scatter_all(gate_up_grads(normed_ffn, gate_back, up_back))
        waits = ()
    early, attn_back, sum_ffn_pre, sum_attn_post = ffn_back_rows(
        gate_back, up_back, w_gate_up, late, mixed, attn_out, image, onehot, attn_post, ffn_pre,
        wait=waits,
    )
    grad_attended = dot_nt(attn_back, w_output).astype(bf16)
    if parts > 1:
        grad_attended = spread(grad_attended)
    back = partial(
        attend_back,
        *heads, spec_of, width, attended_heads, grad_attended, log_total, query_image, key_image,
    )
    if near:
        group = width // LANES // 2
        waits = arrived(down_chain)
        step_all(grad_attended, down_chain)
        waits += tuple(down_chain.sent)
        grads = back(width // LANES, 0, None, after=waits)
    else:
        grads = back(width // LANES, 0, None)
    if parts > 1:
        grads = tuple(collect(grad) for grad in grads)
    grad_q, grad_k, grad_v = grads
    waits = ()
    if near:
        waits = arrived(down_chain)
        step_all(grad_q, down_chain)
        waits += tuple(down_chain.sent)
    turned, sum_turn = turn_back(
        grad_q, grad_k, hats, inverses, cosine, sine, turn_gains, after=waits
    )
    waits = ()
    if near:
        side_width = D // 3
        grad_parts = third_grads(
            attended, attn_back, place, D + side_width, D, after=(grads[0],)
        )
        for k, (back_values, column) in enumerate(((turned, 0), (turned, 1), (grad_v, 0))):
            grad_parts[k] = masked_grads(
                normed, back_values, column, D, place, k, D + side_width, 0, into=grad_parts[k]
            )
        main = Scatter(grad_parts, picks)
        main.start()
        pieces = held_until(pieces, grad_parts[1][0])
    folded = fold_patches(pieces, rows, cols)
    if near:
        waits = arrived(down_chain) + tuple(part[0] for part in grad_parts) + (folded,)
    embed_back, grad_pieces, sum_attn_pre = project_back_rows(
        [turned, grad_v], w_project, embedded, early, image, onehot, attn_pre, w_embed, wait=waits
    )
    if near:
        while not down_chain.done():
            go_on(down_chain)
        down_share = jnp.concatenate(down_chain.sums(), axis=1)
        if WAIT_FOR_GATE_UP:
            wait_for(main, gate_up_share)
        main.finish()
        first_sent = main.sent_next()
        embed_back = held_until(embed_back, *first_sent[1:])
        sum_attn_pre = held_until(sum_attn_pre, *first_sent[1:])
    gain_grads, grad_modulation = gain_rows(
        [sum_attn_pre, sum_attn_post, sum_ffn_pre, sum_ffn_post, sum_out], factors,
        [scale_attn, gate_attn, scale_ffn, gate_ffn], sum_turn,
    )
    if near:
        side = Scatter(
            [small_grads_near(embed_back, patches, final, grad_patches, gain_grads, place)],
            picks[:1],
        )
        side.start()
        side.finish()
        main.terms[0] = [
            jnp.concatenate([large, tiny.astype(bf16)], axis=1)
            for large, tiny in zip(main.terms[0], side.terms[0])
        ]
        main.start()
        grad_modulation = held_until(grad_modulation, main.received[1])
        spread_sums = Gather([grad_modulation], picks[:1])
        spread_sums.start()
        grad_pieces = held_until(grad_pieces, main.received[1])
        while not main.done():
            go_on(main)
        while not spread_sums.done():
            go_on(spread_sums)
        grad_modulations = jnp.concatenate(spread_sums.held[0], axis=0)
        held = main.sums()
        project_share = jnp.concatenate([value[:, :D] for value in held], axis=1)
        output_share = jnp.concatenate([value[:, D : D + side_width] for value in held], axis=1)
        small_share = held[0][:, D + side_width :]
    else:
        grad_modulations = gather_all(grad_modulation)
        small_grads = jnp.concatenate(
            [dot_tn(embed_back, patches), dot_tn(final, grad_patches), gain_grads.T], axis=1
        )
        small_share = scatter_all(
            jnp.pad(small_grads, ((0, 0), (0, 2 * LANES - small_grads.shape[1])))
        )
        project_back = jnp.concatenate([turned, grad_v], axis=1)
        project_share = scatter_all(dot_tn(normed, project_back).astype(bf16))
        output_share = scatter_all(dot_tn(attended, attn_back).astype(bf16))
    prediction = from_strips(share_rims(folded, parts), micros)
    latent_grad = from_strips(
        share_rims(fold_patches(grad_pieces, rows, cols), parts), micros
    )

    spaced = jnp.pad(
        conditions.reshape(devices, IMGS, rows_held), ((0, 0), (0, IMGS), (0, 0))
    )
    adaptive_share = jnp.concatenate(
        [
            dot_tn(values.reshape(2 * devices * IMGS, rows_held), grad_modulations)
            for values in (spaced, jnp.roll(spaced, IMGS, axis=1))
        ],
        axis=1,
    )
    return (
        prediction[:, None],
        latent_grad[:, None],
        small_share[:, :PIN],
        adaptive_share,
        project_share.astype(f32),
        output_share.astype(f32),
        gate_up_share.astype(f32),
        down_share.astype(f32),
        small_share[:, PIN : 2 * PIN],
        small_share[:, 2 * PIN : 2 * PIN + 6],
    )


def solution(mesh):
    canvas = P(None, "fsdp", None, "rows", "cols")
    weight = P(ALL, None)
    return jax.shard_map(
        shards,
        mesh=mesh,
        in_specs=(canvas, P(None, "fsdp", "cols", None, None), P(None, "fsdp", "cols", None), canvas)
        + (weight,) * 8,
        out_specs=(canvas, canvas) + (weight,) * 8,
        check_vma=False,
    )
```

time: 1070 us -> 1010 us (0.944)
  waiting for transfers between devices: 179 us -> 265 us
  local copies, waits for them, and re-layouts: 130 us -> 64 us
  Pallas kernels: 505 us -> 444 us
  matrix products: 79.4 us -> 38.9 us
  other arithmetic: 71.3 us -> 95.8 us
    all_gather x3, waiting for transfers between devices: 0.01 us -> 145 us  [gather_all(): return lax.all_gather(shard, ALL, axis=0, tiled=True)]
    ppermute x50 -> x46, waiting for transfers between devices: 178 us -> 96 us  [swap(): lax.ppermute(values, axis, [(i, i ^ 1 << bit) for i in range(lax.axis_siz...]
    dot_general x5 -> x2, matrix products: 64.8 us -> 0.99 us  [dot_tn(): lax.dot_general(left, right, (((0,), (0,)), ((), ())), preferred_element_...]
    pallas_call x1, Pallas kernels: 79.7 us -> 37 us  [attend(): pl.pallas_call(kernel, grid=(pairs,), in_specs=[pl.BlockSpec((length, LAN...]
    conv_general_dilated x0 -> x3, matrix products: none -> 25.9 us  [the longest x2 22 us: fold_patches(): lax.conv_general_dilated(pieces.reshape(1, rows, cols, PIN), window_filte...]
    pallas_call x1, Pallas kernels: 59.9 us -> 35.9 us  [project_rows(): pl.pallas_call(kernel, grid=(3,), in_specs=[whole(patches.shape), whole(i...]
    convert_element_type x16 -> x26, other arithmetic: 29.6 us -> 52.4 us  [the longest x24 50 us: sent_next(): sent.append(self.total([term[half:] for term in terms]).astype(kind))]
    ppermute x6, waiting for transfers between devices: 0.02 us -> 20.9 us  [neighbours(): return (lax.ppermute(tail, axis, ups), lax.ppermute(head, axis, downs))]
  transfers between devices with their start and end apart: 65 -> 59, of which waited for: 20 -> 25; matrix products, arithmetic and copies ran while one was open for 24% -> 19% of each run, Pallas kernels for 43% -> 39%
where the time goes in v2:
time: 1010 us; the launch traced here: 1000 us
  Pallas kernels  444 us (44%)
  waiting for transfers between devices  265 us (26%)
  other arithmetic  95.8 us (9%)
  starting transfers between devices  77.9 us (8%)
  local copies, waits for them, and re-layouts  64 us (6%)
  matrix products  38.9 us (4%)
  between operations  19.2 us (2%)
    all_gather x3, waiting for transfers between devices, gather_all(): return lax.all_gather(shard, ALL, axis=0, tiled=True)  145 us
    pallas_call x4, Pallas kernels, matmul_rows(): pl.pallas_call(ordered(kernel, len(wait)), grid=(tiles + blocks,), in_spe...  128 us
    ppermute x46, waiting for transfers between devices, swap(): lax.ppermute(values, axis, [(i, i ^ 1 << bit) for i in range(lax.axis_siz...  96 us
    pallas_call x1, Pallas kernels, attend_back(): pl.pallas_call(ordered(kernel, len(after)), grid=(pairs,), in_specs=unrea...  67.2 us
    ppermute x46, starting transfers between devices, swap(): lax.ppermute(values, axis, [(i, i ^ 1 << bit) for i in range(lax.axis_siz...  58.1 us
    convert_element_type x24, other arithmetic, sent_next(): sent.append(self.total([term[half:] for term in terms]).astype(kind))  50 us
    pallas_call x1, Pallas kernels, attend(): pl.pallas_call(kernel, grid=(pairs,), in_specs=[pl.BlockSpec((length, LAN...  37 us
    pallas_call x1, Pallas kernels, project_rows(): pl.pallas_call(kernel, grid=(3,), in_specs=[whole(patches.shape), whole(i...  35.9 us
  transfers between devices with their start and end apart: 59, of which 25 were waited for; matrix products, arithmetic and copies ran while one was open for 19% of the time, Pallas kernels for 39%

profile of v2, /device:TPU:0, one launch (start us, length us, event | category | flops | bytes accessed | tf_op | source)
XLA Modules:
  0.0 1004.8 jit_solution(2936169361673485677)
XLA Ops:
  11.2 4.1 collective-permute-start.3
  23.9 5.8 collective-permute-done.5
  31.5 4.7 collective-permute-done.6
  48.0 3.1 sine_multiply_fusion
  64.8 18.3 %collective-permute-done.1 = bf16[8,128,1]{1,2,0:T(2,128)(2,1)S(1)} collective-permute-done((bf16[8,128,1]{1,2,0:T(2,128)(2,1)S(1)}, bf16[8,128,1]{1,2,0:T(2,128)(2,1)S(1)}, u32[]{:S(2)}, u32[]{:S(2)}) %collective-permute-start.1) | collective-permute-done | bytes 2080 | tf_op jit(solution)/shard_map/ppermute | solution.py:1028
  85.3 8.1 copy.103
  97.0 3.9 convolution_convert_fusion
  106.6 13.4 %collective-permute-done.10 = f32[16,7680]{1,0:T(8,128)} collective-permute-done((f32[16,7680]{1,0:T(8,128)}, f32[16,7680]{1,0:T(8,128)}, u32[]{:S(2)}, u32[]{:S(2)}) %collective-permute-start.10) | collective-permute-done | bytes 491552 | tf_op jit(solution)/shard_map/ppermute | solution.py:1139
  124.0 4.9 collective-permute-done.11
  130.1 4.7 collective-permute-start.12
  135.5 4.0 collective-permute-done.12
  144.0 14.6 %all-gather.4.cloned.1.call-done.weight_ref.refs_1_.refs_9_ = bf16[1536,6144]{1,0:T(8,128)(2,1)} async-done(((bf16[48,6144]{1,0:T(8,128)(2,1)}), bf16[1536,6144]{1,0:T(8,128)(2,1)}) %all-gather.4.cloned.1.call-update) | async-done | bytes 18874384 | tf_op jit(solution)/shard_map/all_gather | solution.py:1107
  159.6 35.9 %project_rows.1 = (f32[1024,1536]{1,0:T(8,128)}, bf16[1024,1536]{1,0:T(8,128)(2,1)}, bf16[1024,4608]{1,0:T(8,128)(2,1)}, bf16[1024,3072]{1,0:T(8,128)(2,1)}, f32[1024,256]{1,0:T(8,128)}) custom-call(bf16[1024,64]{1,0:T(8,128)(2,1)} %bitcast.81, s32[1024,128]{1,0:T(8,128)} %broadcast_in_dim.98.image_ref.refs_3_.refs_13_.refs_12_, ...), custom_call_target="tpu_custom_call" | custom-call | flops 7247757312 | bytes 25952256 | tf_op jit(solution)/shard_map/project_rows/pallas_call | solution.py:255
  195.5 37.0 %attend.1 = (bf16[1024,1536]{1,0:T(8,128)(2,1)}, f32[12,2,1024]{2,1,0:T(2,128)}) custom-call(bf16[1024,4608]{1,0:T(8,128)(2,1)} %get-tuple-element.65.q_ref.k_ref.v_ref.refs_6_.refs_7_.refs_8_, bf16[1024,4608]{1,0:T(8,128)(2,1)} %get-tuple-element.65.q_ref.k_ref.v_ref.refs_6_.refs_7_.refs_8_, ...), custom_call_target="tpu_custom_call" | custom-call | flops 25769803776 | bytes 6291456 | tf_op jit(solution)/shard_map/attend/pallas_call | solution.py:624
  232.5 17.8 %output_rows.1 = (f32[1024,1536]{1,0:T(8,128)}, f32[1024,1536]{1,0:T(8,128)}, bf16[1024,1536]{1,0:T(8,128)(2,1)}) custom-call(bf16[1024,1536]{1,0:T(8,128)(2,1)} %get-tuple-element.66.refs_0_.refs_9_.refs_1_, bf16[1536,6144]{1,0:T(8,128)(2,1)} %all-gather.4.cloned.1.call-done.weight_ref.refs_1_.refs_9_, f32[1024,1536]{1,0:T(8,128)} %get-tuple-element.67.refs_2_.refs_10_, ...), custom_call_target="tpu_custom_call" | custom-call | flops 2415919104 | bytes 10223616 | tf_op jit(solution)/shard_map/output_rows/pallas_call | solution.py:176
  250.3 65.3 %all-gather.6.cloned.1.call-done.gate_weight.up_weight.refs_9_ = bf16[1536,8192]{1,0:T(8,128)(2,1)} async-done(((bf16[48,8192]{1,0:T(8,128)(2,1)}), bf16[1536,8192]{1,0:T(8,128)(2,1)}) %all-gather.6.cloned.1.call-update) | async-done | bytes 25165840 | tf_op jit(solution)/shard_map/all_gather | solution.py:1107
  315.5 32.2 %gate_up_rows.1 = (bf16[1024,4096]{1,0:T(8,128)(2,1)}, bf16[1024,4096]{1,0:T(8,128)(2,1)}, bf16[1024,4096]{1,0:T(8,128)(2,1)}) custom-call(bf16[1024,1536]{1,0:T(8,128)(2,1)} %get-tuple-element.68.left_ref.refs_6_, bf16[1536,8192]{1,0:T(8,128)(2,1)} %all-gather.6.cloned.1.call-done.gate_weight.up_weight.refs_9_, ...), custom_call_target="tpu_custom_call" | custom-call | flops 12884901888 | bytes 25165824 | tf_op jit(solution)/shard_map/gate_up_rows/pallas_call | solution.py:753
  347.7 64.9 %all-gather.8.cloned.1.call-done.refs_1_.refs_4_ = bf16[4096,1536]{1,0:T(8,128)(2,1)} async-done(((bf16[128,1536]{1,0:T(8,128)(2,1)}), bf16[4096,1536]{1,0:T(8,128)(2,1)}) %all-gather.8.cloned.1.call-update) | async-done | bytes 12582928 | tf_op jit(solution)/shard_map/all_gather | solution.py:1107
  412.6 32.8 %down_rows.1 = (bf16[1024,1536]{1,0:T(8,128)(2,1)}, f32[1024,1536]{1,0:T(8,128)}, bf16[1024,1536]{1,0:T(8,128)(2,1)}, bf16[1024,64]{1,0:T(8,128)(2,1)}, f32[8,1536]{1,0:T(8,128)}, /*index=5*/f32[8,1536]{1,0:T(8,128)}) custom-call(bf16[1024,4096]{1,0:T(8,128)(2,1)} %get-tuple-element.69.refs_0_, ...), custom_call_target="tpu_custom_call" | custom-call | flops 6442450944 | bytes 16777216 | tf_op jit(solution)/shard_map/down_rows/pallas_call | solution.py:176
  445.4 20.8 %third_grads.2 = (bf16[2048,512]{1,0:T(8,128)(2,1)}, bf16[2048,512]{1,0:T(8,128)(2,1)}, bf16[2048,512]{1,0:T(8,128)(2,1)}, bf16[2048,512]{1,0:T(8,128)(2,1)}, bf...) custom-call(bf16[1024,4096]{1,0:T(8,128)(2,1)} %get-tuple-element.69.refs_0_, ...), custom_call_target="tpu_custom_call" | custom-call | flops 6442450944 | bytes 12058624 | tf_op jit(solution)/shard_map/third_grads/pallas_call | solution.py:556
  467.7 26.1 %gate_up_back.1 = (bf16[1024,4096]{1,0:T(8,128)(2,1)}, bf16[1024,4096]{1,0:T(8,128)(2,1)}) custom-call(bf16[2048,512]{1,0:T(8,128)(2,1)} %get-tuple-element.74.refs_0_, bf16[2048,512]{1,0:T(8,128)(2,1)} %get-tuple-element.76.refs_1_, bf16[2048,512]{1,0:T(8,128)(2,1)} %get-tuple-element.77.refs_2_, bf16[1024,1536]{1,0:T(8,128)(2,1)} %get-tuple-element.73.refs_1_.refs_3_, ...), custom_call_target="tpu_custom_call" | custom-call | flops 6442450944 | bytes 23068672 | tf_op jit(solution)/shard_map/gate_up_back/pallas_call | solution.py:786
  508.0 32.8 %gate_up_grads.1.refs_1_.refs_3_ = bf16[1536,8192]{1,0:T(8,128)(2,1)} custom-call(bf16[2048,512]{1,0:T(8,128)(2,1)} %copy-done.10, bf16[2048,512]{1,0:T(8,128)(2,1)} %collective-permute-done.15.refs_1_, bf16[2048,512]{1,0:T(8,128)(2,1)} %collective-permute-done.16.refs_2_, bf16[1024,512]{1,0:T(8,128)(2,1)} %add_convert_fusion.5.refs_3_, ...), custom_call_target="tpu_custom_call" | custom-call | flops 12884901888 | bytes 20971520 | tf_op jit(solution)/shard_map/gate_up_grads/pallas_call | solution.py:427
  551.9 47.8 %ffn_back_rows.1 = (f32[1024,1536]{1,0:T(8,128)}, bf16[1024,1536]{1,0:T(8,128)(2,1)}, f32[8,1536]{1,0:T(8,128)}, f32[8,1536]{1,0:T(8,128)}) custom-call(bf16[1024,512]{1,0:T(8,128)(2,1)} %copy-done.14, bf16[1024,512]{1,0:T(8,128)(2,1)} %collective-permute-done.18.refs_1_, bf16[1024,512]{1,0:T(8,128)(2,1)} %collective-permute-done.19.refs_2_, ...), custom_call_target="tpu_custom_call" | custom-call | flops 12884901888 | bytes 27262976 | tf_op jit(solution)/shard_map/ffn_back_rows/pallas_call | solution.py:176
  599.7 9.5 fusion.2.refs_1_.refs_10_
  618.5 67.2 %attend_back.1 = (bf16[1024,1536]{1,0:T(8,128)(2,1)}, bf16[1024,1536]{1,0:T(8,128)(2,1)}, bf16[1024,1536]{1,0:T(8,128)(2,1)}) custom-call(bf16[512,512]{1,0:T(8,128)(2,1)} %copy-done.36, bf16[512,512]{1,0:T(8,128)(2,1)} %collective-permute-done.21.refs_1_, bf16[512,512]{1,0:T(8,128)(2,1)} %collective-permute-done.23.refs_2_, bf16[256,512]{1,0:T(8,128)(2,1)} %copy-done.37, ...), custom_call_target="tpu_custom_call" | custom-call | flops 64424509440 | bytes 12582912 | tf_op jit(solution)/shard_map/attend_back/pallas_call | solution.py:708
  685.7 10.2 %third_grads.3 = (bf16[768,2048]{1,0:T(8,128)(2,1)}, bf16[768,2048]{1,0:T(8,128)(2,1)}, bf16[768,2048]{1,0:T(8,128)(2,1)}, bf16[768,2048]{1,0:T(8,128)(2,1)}, bf...) custom-call(bf16[1024,1536]{1,0:T(8,128)(2,1)} %get-tuple-element.88.refs_1_.refs_6_.refs_0_, ...), custom_call_target="tpu_custom_call" | custom-call | flops 2415919104 | bytes 5505024 | tf_op jit(solution)/shard_map/third_grads/pallas_call | solution.py:556
  695.9 9.9 masked_grads.5
  714.7 13.2 %turn_back.1 = (bf16[1024,3072]{1,0:T(8,128)(2,1)}, f32[8,1536]{1,0:T(8,128)}) custom-call(bf16[256,512]{1,0:T(8,128)(2,1)} %copy-done.22, bf16[256,512]{1,0:T(8,128)(2,1)} %copy-done.25, bf16[256,512]{1,0:T(8,128)(2,1)} %copy-done.23, bf16[128,512]{1,0:T(8,128)(2,1)} %add_convert_fusion.23.refs_3_, bf16[128,512]{1,0:T(8,128)(2,1)} %add_convert_fusion.22.refs_4_, ...), custom_call_target="tpu_custom_call" | custom-call | flops 31457280 | bytes 9437184 | tf_op jit(solution)/shard_map/turn_back/pallas_call | solution.py:952
  727.9 10.2 %masked_grads.3 = (bf16[768,2048]{1,0:T(8,128)(2,1)}, bf16[768,2048]{1,0:T(8,128)(2,1)}) custom-call(bf16[1024,1536]{1,0:T(8,128)(2,1)} %get-tuple-element.72.refs_0_, bf16[1024,3072]{1,0:T(8,128)(2,1)} %get-tuple-element.92.refs_1_.refs_7_, s32[1]{0:T(128)} %bitcast.11.refs_2_.refs_3_.me_ref, ...), custom_call_target="tpu_custom_call", output_to_operand_aliasing={{0}: (3, {}), {1}: (4, {})} | custom-call | flops 2415919104 | bytes 5505024 | tf_op jit(solution)/shard_map/masked_grads/pallas_call | solution.py:490
  738.2 9.9 masked_grads.4
  748.7 10.7 %fusion.13 = f32[1,4,130,34]{1,0,3,2:T(1,128)S(1)} fusion(bf16[1,64,16,64]{3,2,1,0:T(8,128)(2,1)} %bitcast.92, s32[4,4,4]{0,2,1:T(4,128)S(1)} %copy-done.48), kind=kOutput, calls=%fused_computation.52 | convolution fusion | flops 8392704 | bytes 202048 | tf_op jit(solution)/shard_map/conv_general_dilated | solution.py:1059
  766.0 3.9 collective-permute-start.25
  769.9 3.3 collective-permute-done.28.refs_0_
  773.8 29.6 %project_back_rows.1 = (bf16[1024,1536]{1,0:T(8,128)(2,1)}, bf16[1024,64]{1,0:T(8,128)(2,1)}, f32[8,1536]{1,0:T(8,128)}) custom-call(bf16[128,512]{1,0:T(8,128)(2,1)} %copy-done.34, bf16[128,512]{1,0:T(8,128)(2,1)} %collective-permute-done.29.refs_1_, bf16[128,512]{1,0:T(8,128)(2,1)} %collective-permute-done.30.refs_2_, ...), custom_call_target="tpu_custom_call" | custom-call | flops 7247757312 | bytes 18087936 | tf_op jit(solution)/shard_map/project_back_rows/pallas_call | solution.py:176
  803.5 3.4 add_convert_fusion.1.refs_2_
  806.9 3.2 add_convert_fusion.2.refs_1_
  817.4 6.8 small_grads_near.1
  834.7 9.8 collective-permute-done.51
  847.4 11.3 %fusion.11 = f32[1,4,130,34]{1,0,3,2:T(1,128)} fusion(bf16[1,64,16,64]{3,2,1,0:T(8,128)(2,1)} %bitcast.95, s32[4,4,4]{0,2,1:T(4,128)S(1)} %copy-done.48), kind=kOutput, calls=%fused_computation.50 | convolution fusion | flops 8392704 | bytes 202048 | tf_op jit(solution)/shard_map/conv_general_dilated | solution.py:1059
  858.7 5.5 copy.111
  868.0 5.5 collective-permute-start.33
  883.5 7.9 collective-permute-start.48
  912.5 3.4 collective-permute-done.44
  918.6 4.4 collective-permute-done.45
  934.5 6.5 collective-permute-done.53
  946.9 8.4 collective-permute-done.54
  964.2 10.5 %collective-permute-done.41 = bf16[96,2304]{1,0:T(8,128)(2,1)S(1)} collective-permute-done((bf16[96,2304]{1,0:T(8,128)(2,1)S(1)}, bf16[96,2304]{1,0:T(8,128)(2,1)S(1)}, u32[]{:S(2)}, u32[]{:S(2)}) %collective-permute-start.41) | collective-permute-done | bytes 442400 | tf_op jit(solution)/shard_map/ppermute | solution.py:1139
  978.3 9.3 collective-permute-done.42
  (371 shorter events, 209.5 us)
Async XLA Ops:
  7.2 151.4 %all-gather.4.cloned.1.call-start = ((), (), s32[]{:S(2)}) async-start(), calls=%async_computation.1 | async-start | bytes 19464192 | tf_op jit(solution)/shard_map/all_gather | solution.py:1107
  9.3 306.2 %all-gather.6.cloned.1.call-start = ((), (), s32[]{:S(2)}) async-start(), calls=%async_computation.2 | async-start | bytes 25952256 | tf_op jit(solution)/shard_map/all_gather | solution.py:1107
  10.0 402.6 %all-gather.8.cloned.1.call-start = ((), (), s32[]{:S(2)}) async-start(), calls=%async_computation.3 | async-start | bytes 12976128 | tf_op jit(solution)/shard_map/all_gather | solution.py:1107
  10.8 984.7 %reduce-scatter.2.cloned.1.call-start = ((), (), s32[]{:S(2)}) async-start(), calls=%async_computation.4 | async-start | bytes 25952256 | tf_op jit(solution)/shard_map/reduce_scatter | solution.py:1111
  22.1 7.7 collective-permute-start.5
  44.3 16.2 %collective-permute-start = (bf16[8,64,32]{1,2,0:T(8,128)(2,1)S(1)}, bf16[8,64,32]{1,2,0:T(8,128)(2,1)S(1)}, u32[]{:S(2)}, u32[]{:S(2)}) collective-permute-start(bf16[8,64,32]{1,2,0:T(8,128)(2,1)S(1)} %get-tuple-element.209), channel_id=1, source_target_pairs={{0,16},{16,0},{1,17},{17,1},{2,18},{18,2},{3,19},{19,3},{4,20},{20... | collective-permute-start | bytes 98312 | tf_op jit(solution)/shard_map/ppermute | solution.py:982
  54.1 39.3 %collective-permute-start.9 = (f32[32,7680]{1,0:T(8,128)}, f32[32,7680]{1,0:T(8,128)S(1)}, u32[]{:S(2)}, u32[]{:S(2)}) collective-permute-start(f32[32,7680]{1,0:T(8,128)} %slice_add_fusion), channel_id=1, source_target_pairs={{0,2},{2,0},{4,6},{6,4},{8,10},{10,8},{12,14},{14,12},{1,3},{3,1},... | collective-permute-start | bytes 2949128 | tf_op jit(solution)/shard_map/ppermute | solution.py:1139
  60.9 22.2 %collective-permute-start.1 = (bf16[8,128,1]{1,2,0:T(2,128)(2,1)S(1)}, bf16[8,128,1]{1,2,0:T(2,128)(2,1)S(1)}, u32[]{:S(2)}, u32[]{:S(2)}) collective-permute-start(bf16[8,128,1]{1,2,0:T(2,128)(2,1)S(1)} %get-tuple-element.225), channel_id=1, source_target_pairs={{0,2},{2,4},{4,6},{6,8},{8,10},{10,12},{12,14},{1,3},{3,5},{5,7},{... | collective-permute-start | bytes 6152 | tf_op jit(solution)/shard_map/ppermute | solution.py:1028
  63.5 21.6 %collective-permute-start.2 = (bf16[8,128,1]{1,2,0:T(2,128)(2,1)S(1)}, bf16[8,128,1]{1,2,0:T(2,128)(2,1)S(1)}, u32[]{:S(2)}, u32[]{:S(2)}) collective-permute-start(bf16[8,128,1]{1,2,0:T(2,128)(2,1)S(1)} %get-tuple-element.226), channel_id=1, source_target_pairs={{2,0},{4,2},{6,4},{8,6},{10,8},{12,10},{14,12},{3,1},{5,3},{7,5},{... | collective-permute-start | bytes 6152 | tf_op jit(solution)/shard_map/ppermute | solution.py:1028
  95.5 24.5 %collective-permute-start.10 = (f32[16,7680]{1,0:T(8,128)}, f32[16,7680]{1,0:T(8,128)}, u32[]{:S(2)}, u32[]{:S(2)}) collective-permute-start(f32[16,7680]{1,0:T(8,128)} %slice_add_fusion.1), channel_id=1, source_target_pairs={{0,16},{16,0},{1,17},{17,1},{2,18},{18,2},{3,19},{19,3},{4,20},{20... | collective-permute-start | bytes 1474568 | tf_op jit(solution)/shard_map/ppermute | solution.py:1139
  130.1 9.4 collective-permute-start.12
  466.2 27.5 %collective-permute-start.13 = (bf16[2048,512]{1,0:T(8,128)(2,1)}, bf16[2048,512]{1,0:T(8,128)(2,1)S(1)}, u32[]{:S(2)}, u32[]{:S(2)}) collective-permute-start(bf16[2048,512]{1,0:T(8,128)(2,1)} %get-tuple-element.75), channel_id=1, source_target_pairs={{0,1},{1,0},{2,3},{3,2},{4,5},{5,4},{6,7},{7,6},{8,9},{9,8},{10,11... | collective-permute-start | bytes 6291464 | tf_op jit(solution)/shard_map/ppermute | solution.py:1139
  466.6 34.9 %collective-permute-start.15 = (bf16[2048,512]{1,0:T(8,128)(2,1)}, bf16[2048,512]{1,0:T(8,128)(2,1)}, u32[]{:S(2)}, u32[]{:S(2)}) collective-permute-start(bf16[2048,512]{1,0:T(8,128)(2,1)} %get-tuple-element.81), channel_id=1, source_target_pairs={{0,1},{1,0},{2,3},{3,2},{4,5},{5,4},{6,7},{7,6},{8,9},{9,8},{10,11... | collective-permute-start | bytes 6291464 | tf_op jit(solution)/shard_map/ppermute | solution.py:1139
  466.8 37.8 %collective-permute-start.16 = (bf16[2048,512]{1,0:T(8,128)(2,1)}, bf16[2048,512]{1,0:T(8,128)(2,1)}, u32[]{:S(2)}, u32[]{:S(2)}) collective-permute-start(bf16[2048,512]{1,0:T(8,128)(2,1)} %get-tuple-element.82), channel_id=1, source_target_pairs={{0,1},{1,0},{2,3},{3,2},{4,5},{5,4},{6,7},{7,6},{8,9},{9,8},{10,11... | collective-permute-start | bytes 6291464 | tf_op jit(solution)/shard_map/ppermute | solution.py:1139
  500.0 48.3 %collective-permute-start.14 = (bf16[1024,512]{1,0:T(8,128)(2,1)}, bf16[1024,512]{1,0:T(8,128)(2,1)S(1)}, u32[]{:S(2)}, u32[]{:S(2)}) collective-permute-start(bf16[1024,512]{1,0:T(8,128)(2,1)} %add_convert_fusion.5.refs_3_), channel_id=1, source_target_pairs={{0,2},{2,0},{4,6},{6,4},{8,10},{10,8},{12,14},{14,12},{1,3},{3,1},... | collective-permute-start | bytes 3145736 | tf_op jit(solution)/shard_map/ppermute | solution.py:1139
  503.9 36.9 %collective-permute-start.18 = (bf16[1024,512]{1,0:T(8,128)(2,1)}, bf16[1024,512]{1,0:T(8,128)(2,1)}, u32[]{:S(2)}, u32[]{:S(2)}) collective-permute-start(bf16[1024,512]{1,0:T(8,128)(2,1)} %add_convert_fusion.4.refs_4_), channel_id=1, source_target_pairs={{0,16},{16,0},{1,17},{17,1},{2,18},{18,2},{3,19},{19,3},{4,20},{20... | collective-permute-start | bytes 3145736 | tf_op jit(solution)/shard_map/ppermute | solution.py:1139
  507.1 37.2 %collective-permute-start.19 = (bf16[1024,512]{1,0:T(8,128)(2,1)}, bf16[1024,512]{1,0:T(8,128)(2,1)}, u32[]{:S(2)}, u32[]{:S(2)}) collective-permute-start(bf16[1024,512]{1,0:T(8,128)(2,1)} %add_convert_fusion.3.refs_5_), channel_id=1, source_target_pairs={{0,4},{2,6},{4,0},{6,2},{8,12},{10,14},{12,8},{14,10},{1,5},{3,7},... | collective-permute-start | bytes 3145736 | tf_op jit(solution)/shard_map/ppermute | solution.py:1139
  543.2 66.0 %collective-permute-start.21 = (bf16[512,512]{1,0:T(8,128)(2,1)}, bf16[512,512]{1,0:T(8,128)(2,1)}, u32[]{:S(2)}, u32[]{:S(2)}) collective-permute-start(bf16[512,512]{1,0:T(8,128)(2,1)} %add_convert_fusion.10.refs_5_), channel_id=1, source_target_pairs={{0,4},{2,6},{4,0},{6,2},{8,12},{10,14},{12,8},{14,10},{1,5},{3,7},... | collective-permute-start | bytes 1572872 | tf_op jit(solution)/shard_map/ppermute | solution.py:1139
  547.1 65.4 %collective-permute-start.23 = (bf16[512,512]{1,0:T(8,128)(2,1)}, bf16[512,512]{1,0:T(8,128)(2,1)}, u32[]{:S(2)}, u32[]{:S(2)}) collective-permute-start(bf16[512,512]{1,0:T(8,128)(2,1)} %add_convert_fusion.9.refs_6_), channel_id=1, source_target_pairs={{0,2},{2,0},{4,6},{6,4},{8,10},{10,8},{12,14},{14,12},{1,3},{3,1},... | collective-permute-start | bytes 1572872 | tf_op jit(solution)/shard_map/ppermute | solution.py:1139
  551.1 64.5 %collective-permute-start.17 = (bf16[512,512]{1,0:T(8,128)(2,1)S(1)}, bf16[512,512]{1,0:T(8,128)(2,1)S(1)}, u32[]{:S(2)}, u32[]{:S(2)}) collective-permute-start(bf16[512,512]{1,0:T(8,128)(2,1)S(1)} %add_convert_fusion.11.refs_4_), channel_id=1, source_target_pairs={{0,16},{16,0},{1,17},{17,1},{2,18},{18,2},{3,19},{19,3},{4,20},{20... | collective-permute-start | bytes 1572872 | tf_op jit(solution)/shard_map/ppermute | solution.py:1139
  611.2 94.6 %collective-permute-start.22 = (bf16[256,512]{1,0:T(8,128)(2,1)}, bf16[256,512]{1,0:T(8,128)(2,1)S(1)}, u32[]{:S(2)}, u32[]{:S(2)}) collective-permute-start(bf16[256,512]{1,0:T(8,128)(2,1)} %add_convert_fusion.16.refs_4_), channel_id=1, source_target_pairs={{0,2},{2,0},{4,6},{6,4},{8,10},{10,8},{12,14},{14,12},{1,3},{3,1},... | collective-permute-start | bytes 786440 | tf_op jit(solution)/shard_map/ppermute | solution.py:1139
  614.5 94.6 %collective-permute-start.24 = (bf16[256,512]{1,0:T(8,128)(2,1)}, bf16[256,512]{1,0:T(8,128)(2,1)S(1)}, u32[]{:S(2)}, u32[]{:S(2)}) collective-permute-start(bf16[256,512]{1,0:T(8,128)(2,1)} %add_convert_fusion.15.refs_5_), channel_id=1, source_target_pairs={{0,16},{16,0},{1,17},{17,1},{2,18},{18,2},{3,19},{19,3},{4,20},{20... | collective-permute-start | bytes 786440 | tf_op jit(solution)/shard_map/ppermute | solution.py:1139
  617.8 94.3 %collective-permute-start.20 = (bf16[256,512]{1,0:T(8,128)(2,1)S(1)}, bf16[256,512]{1,0:T(8,128)(2,1)S(1)}, u32[]{:S(2)}, u32[]{:S(2)}) collective-permute-start(bf16[256,512]{1,0:T(8,128)(2,1)S(1)} %add_convert_fusion.17.refs_3_), channel_id=1, source_target_pairs={{0,4},{2,6},{4,0},{6,2},{8,12},{10,14},{12,8},{14,10},{1,5},{3,7},... | collective-permute-start | bytes 786440 | tf_op jit(solution)/shard_map/ppermute | solution.py:1139
  705.7 97.7 %collective-permute-start.36 = (bf16[768,2048]{1,0:T(8,128)(2,1)}, bf16[768,2048]{1,0:T(8,128)(2,1)}, u32[]{:S(2)}, u32[]{:S(2)}) collective-permute-start(bf16[768,2048]{1,0:T(8,128)(2,1)} %get-tuple-element.107), channel_id=1, source_target_pairs={{0,1},{1,0},{2,3},{3,2},{4,5},{5,4},{6,7},{7,6},{8,9},{9,8},{10,11... | collective-permute-start | bytes 9437192 | tf_op jit(solution)/shard_map/ppermute | solution.py:1139
  707.8 55.8 %collective-permute-start.29 = (bf16[128,512]{1,0:T(8,128)(2,1)}, bf16[128,512]{1,0:T(8,128)(2,1)}, u32[]{:S(2)}, u32[]{:S(2)}) collective-permute-start(bf16[128,512]{1,0:T(8,128)(2,1)} %add_convert_fusion.22.refs_4_), channel_id=1, source_target_pairs={{0,8},{2,10},{4,12},{6,14},{8,0},{10,2},{12,4},{14,6},{1,9},{3,11}... | collective-permute-start | bytes 393224 | tf_op jit(solution)/shard_map/ppermute | solution.py:1139
  710.4 55.6 %collective-permute-start.30 = (bf16[128,512]{1,0:T(8,128)(2,1)S(1)}, bf16[128,512]{1,0:T(8,128)(2,1)}, u32[]{:S(2)}, u32[]{:S(2)}) collective-permute-start(bf16[128,512]{1,0:T(8,128)(2,1)S(1)} %add_convert_fusion.21.refs_5_), channel_id=1, source_target_pairs={{0,8},{2,10},{4,12},{6,14},{8,0},{10,2},{12,4},{14,6},{1,9},{3,11}... | collective-permute-start | bytes 393224 | tf_op jit(solution)/shard_map/ppermute | solution.py:1139
  738.1 68.8 %collective-permute-start.31 = (bf16[768,2048]{1,0:T(8,128)(2,1)}, bf16[768,2048]{1,0:T(8,128)(2,1)}, u32[]{:S(2)}, u32[]{:S(2)}) collective-permute-start(bf16[768,2048]{1,0:T(8,128)(2,1)} %get-tuple-element.105), channel_id=1, source_target_pairs={{0,1},{1,0},{2,3},{3,2},{4,5},{5,4},{6,7},{7,6},{8,9},{9,8},{10,11... | collective-permute-start | bytes 9437192 | tf_op jit(solution)/shard_map/ppermute | solution.py:1139
  748.1 79.9 %collective-permute-start.37 = (bf16[768,2048]{1,0:T(8,128)(2,1)}, bf16[768,2048]{1,0:T(8,128)(2,1)}, u32[]{:S(2)}, u32[]{:S(2)}) collective-permute-start(bf16[768,2048]{1,0:T(8,128)(2,1)} %get-tuple-element.117), channel_id=1, source_target_pairs={{0,1},{1,0},{2,3},{3,2},{4,5},{5,4},{6,7},{7,6},{8,9},{9,8},{10,11... | collective-permute-start | bytes 9437192 | tf_op jit(solution)/shard_map/ppermute | solution.py:1139
  763.6 9.6 collective-permute-start.28
  766.0 114.4 %collective-permute-start.25 = (f32[4,130,1]{2,1,0:T(8,128)}, f32[4,130,1]{2,1,0:T(8,128)}, u32[]{:S(2)}, u32[]{:S(2)}) collective-permute-start(f32[4,130,1]{2,1,0:T(8,128)} %get-tuple-element.184), channel_id=1, source_target_pairs={{0,2},{2,4},{4,6},{6,8},{8,10},{10,12},{12,14},{1,3},{3,5},{5,7},{... | collective-permute-start | bytes 6248 | tf_op jit(solution)/shard_map/ppermute | solution.py:1028
  806.8 37.6 %collective-permute-start.51 = (bf16[384,2048]{1,0:T(8,128)(2,1)}, bf16[384,2048]{1,0:T(8,128)(2,1)}, u32[]{:S(2)}, u32[]{:S(2)}) collective-permute-start(bf16[384,2048]{1,0:T(8,128)(2,1)} %add_convert_fusion.1.refs_2_), channel_id=1, source_target_pairs={{0,4},{2,6},{4,0},{6,2},{8,12},{10,14},{12,8},{14,10},{1,5},{3,7},... | collective-permute-start | bytes 4718600 | tf_op jit(solution)/shard_map/ppermute | solution.py:1139
  810.1 37.3 %collective-permute-start.32 = (bf16[384,2048]{1,0:T(8,128)(2,1)}, bf16[384,2048]{1,0:T(8,128)(2,1)}, u32[]{:S(2)}, u32[]{:S(2)}) collective-permute-start(bf16[384,2048]{1,0:T(8,128)(2,1)} %add_convert_fusion.2.refs_1_), channel_id=1, source_target_pairs={{0,16},{16,0},{1,17},{17,1},{2,18},{18,2},{3,19},{19,3},{4,20},{20... | collective-permute-start | bytes 4718600 | tf_op jit(solution)/shard_map/ppermute | solution.py:1139
  827.9 52.8 %collective-permute-start.26 = (f32[4,130,1]{2,1,0:T(8,128)}, f32[4,130,1]{2,1,0:T(8,128)}, u32[]{:S(2)}, u32[]{:S(2)}) collective-permute-start(f32[4,130,1]{2,1,0:T(8,128)} %get-tuple-element.185), channel_id=1, source_target_pairs={{2,0},{4,2},{6,4},{8,6},{10,8},{12,10},{14,12},{3,1},{5,3},{7,5},{... | collective-permute-start | bytes 6248 | tf_op jit(solution)/shard_map/ppermute | solution.py:1028
  832.1 97.9 %collective-permute-start.39 = (bf16[384,2304]{1,0:T(8,128)(2,1)}, bf16[384,2304]{1,0:T(8,128)(2,1)}, u32[]{:S(2)}, u32[]{:S(2)}) collective-permute-start(bf16[384,2304]{1,0:T(8,128)(2,1)} %add_convert_fusion), channel_id=1, source_target_pairs={{0,2},{2,0},{4,6},{6,4},{8,10},{10,8},{12,14},{14,12},{1,3},{3,1},... | collective-permute-start | bytes 5308424 | tf_op jit(solution)/shard_map/ppermute | solution.py:1139
  866.7 16.8 %collective-permute-start.34 = (f32[4,130,1]{2,1,0:T(8,128)}, f32[4,130,1]{2,1,0:T(8,128)}, u32[]{:S(2)}, u32[]{:S(2)}) collective-permute-start(f32[4,130,1]{2,1,0:T(8,128)} %copy.125), channel_id=1, source_target_pairs={{2,0},{4,2},{6,4},{8,6},{10,8},{12,10},{14,12},{3,1},{5,3},{7,5},{... | collective-permute-start | bytes 6248 | tf_op jit(solution)/shard_map/ppermute | solution.py:1028
  868.0 23.9 %collective-permute-start.33 = (f32[4,130,1]{2,1,0:T(8,128)}, f32[4,130,1]{2,1,0:T(8,128)}, u32[]{:S(2)}, u32[]{:S(2)}) collective-permute-start(f32[4,130,1]{2,1,0:T(8,128)} %copy.124), channel_id=1, source_target_pairs={{0,2},{2,4},{4,6},{6,8},{8,10},{10,12},{12,14},{1,3},{3,5},{5,7},{... | collective-permute-start | bytes 6248 | tf_op jit(solution)/shard_map/ppermute | solution.py:1028
  880.4 46.8 %collective-permute-start.52 = (bf16[192,2048]{1,0:T(8,128)(2,1)}, bf16[192,2048]{1,0:T(8,128)(2,1)}, u32[]{:S(2)}, u32[]{:S(2)}) collective-permute-start(bf16[192,2048]{1,0:T(8,128)(2,1)} %add_convert_fusion.7), channel_id=1, source_target_pairs={{0,2},{2,0},{4,6},{6,4},{8,10},{10,8},{12,14},{14,12},{1,3},{3,1},... | collective-permute-start | bytes 2359304 | tf_op jit(solution)/shard_map/ppermute | solution.py:1139
  880.8 29.3 %collective-permute-start.43 = (bf16[8,3840]{1,0:T(8,128)(2,1)}, bf16[8,3840]{1,0:T(8,128)(2,1)}, u32[]{:S(2)}, u32[]{:S(2)}) collective-permute-start(bf16[8,3840]{1,0:T(8,128)(2,1)} %held_until.17), channel_id=1, source_target_pairs={{0,8},{2,10},{4,12},{6,14},{8,0},{10,2},{12,4},{14,6},{1,9},{3,11}... | collective-permute-start | bytes 184328 | tf_op jit(solution)/shard_map/ppermute | solution.py:1139
  883.5 49.3 %collective-permute-start.48 = (bf16[192,2048]{1,0:T(8,128)(2,1)}, bf16[192,2048]{1,0:T(8,128)(2,1)}, u32[]{:S(2)}, u32[]{:S(2)}) collective-permute-start(bf16[192,2048]{1,0:T(8,128)(2,1)} %add_convert_fusion.8), channel_id=1, source_target_pairs={{0,4},{2,6},{4,0},{6,2},{8,12},{10,14},{12,8},{14,10},{1,5},{3,7},... | collective-permute-start | bytes 2359304 | tf_op jit(solution)/shard_map/ppermute | solution.py:1139
  923.9 20.8 %collective-permute-start.46 = (bf16[64,3840]{1,0:T(8,128)(2,1)S(1)}, bf16[64,3840]{1,0:T(8,128)(2,1)S(1)}, u32[]{:S(2)}, u32[]{:S(2)}) collective-permute-start(bf16[64,3840]{1,0:T(8,128)(2,1)S(1)} %pad_maximum_fusion.4), channel_id=1, source_target_pairs={{0,2},{2,0},{4,6},{6,4},{8,10},{10,8},{12,14},{14,12},{1,3},{3,1},... | collective-permute-start | bytes 1474568 | tf_op jit(solution)/shard_map/ppermute | solution.py:1139
  928.8 12.1 %collective-permute-start.53 = (bf16[96,2048]{1,0:T(8,128)(2,1)S(1)}, bf16[96,2048]{1,0:T(8,128)(2,1)S(1)}, u32[]{:S(2)}, u32[]{:S(2)}) collective-permute-start(bf16[96,2048]{1,0:T(8,128)(2,1)S(1)} %add_convert_fusion.13), channel_id=1, source_target_pairs={{0,16},{16,0},{1,17},{17,1},{2,18},{18,2},{3,19},{19,3},{4,20},{20... | collective-permute-start | bytes 1179656 | tf_op jit(solution)/shard_map/ppermute | solution.py:1139
  931.8 29.9 %collective-permute-start.40 = (bf16[192,2304]{1,0:T(8,128)(2,1)S(1)}, bf16[192,2304]{1,0:T(8,128)(2,1)S(1)}, u32[]{:S(2)}, u32[]{:S(2)}) collective-permute-start(bf16[192,2304]{1,0:T(8,128)(2,1)S(1)} %add_convert_fusion.6), channel_id=1, source_target_pairs={{0,16},{16,0},{1,17},{17,1},{2,18},{18,2},{3,19},{19,3},{4,20},{20... | collective-permute-start | bytes 2654216 | tf_op jit(solution)/shard_map/ppermute | solution.py:1139
  934.4 10.5 %collective-permute-start.49 = (bf16[96,2048]{1,0:T(8,128)(2,1)S(1)}, bf16[96,2048]{1,0:T(8,128)(2,1)S(1)}, u32[]{:S(2)}, u32[]{:S(2)}) collective-permute-start(bf16[96,2048]{1,0:T(8,128)(2,1)S(1)} %add_convert_fusion.14), channel_id=1, source_target_pairs={{0,2},{2,0},{4,6},{6,4},{8,10},{10,8},{12,14},{14,12},{1,3},{3,1},... | collective-permute-start | bytes 1179656 | tf_op jit(solution)/shard_map/ppermute | solution.py:1139
  942.3 13.0 %collective-permute-start.54 = (bf16[48,2048]{1,0:T(8,128)(2,1)S(1)}, bf16[48,2048]{1,0:T(8,128)(2,1)S(1)}, u32[]{:S(2)}, u32[]{:S(2)}) collective-permute-start(bf16[48,2048]{1,0:T(8,128)(2,1)S(1)} %add_convert_fusion.19), channel_id=1, source_target_pairs={{0,8},{2,10},{4,12},{6,14},{8,0},{10,2},{12,4},{14,6},{1,9},{3,11}... | collective-permute-start | bytes 589832 | tf_op jit(solution)/shard_map/ppermute | solution.py:1139
  944.8 18.4 %collective-permute-start.47 = (bf16[128,3840]{1,0:T(8,128)(2,1)S(1)}, bf16[128,3840]{1,0:T(8,128)(2,1)S(1)}, u32[]{:S(2)}, u32[]{:S(2)}) collective-permute-start(bf16[128,3840]{1,0:T(8,128)(2,1)S(1)} %get-tuple-element.180), channel_id=1, source_target_pairs={{0,1},{1,0},{2,3},{3,2},{4,5},{5,4},{6,7},{7,6},{8,9},{9,8},{10,11... | collective-permute-start | bytes 2949128 | tf_op jit(solution)/shard_map/ppermute | solution.py:1139
  946.2 12.7 %collective-permute-start.50 = (bf16[48,2048]{1,0:T(8,128)(2,1)S(1)}, bf16[48,2048]{1,0:T(8,128)(2,1)S(1)}, u32[]{:S(2)}, u32[]{:S(2)}) collective-permute-start(bf16[48,2048]{1,0:T(8,128)(2,1)S(1)} %add_convert_fusion.20), channel_id=1, source_target_pairs={{0,8},{2,10},{4,12},{6,14},{8,0},{10,2},{12,4},{14,6},{1,9},{3,11}... | collective-permute-start | bytes 589832 | tf_op jit(solution)/shard_map/ppermute | solution.py:1139
  963.1 11.6 %collective-permute-start.41 = (bf16[96,2304]{1,0:T(8,128)(2,1)S(1)}, bf16[96,2304]{1,0:T(8,128)(2,1)S(1)}, u32[]{:S(2)}, u32[]{:S(2)}) collective-permute-start(bf16[96,2304]{1,0:T(8,128)(2,1)S(1)} %add_convert_fusion.12), channel_id=1, source_target_pairs={{0,4},{2,6},{4,0},{6,2},{8,12},{10,14},{12,8},{14,10},{1,5},{3,7},... | collective-permute-start | bytes 1327112 | tf_op jit(solution)/shard_map/ppermute | solution.py:1139
  975.9 11.6 %collective-permute-start.42 = (bf16[48,2304]{1,0:T(8,128)(2,1)S(1)}, bf16[48,2304]{1,0:T(8,128)(2,1)S(1)}, u32[]{:S(2)}, u32[]{:S(2)}) collective-permute-start(bf16[48,2304]{1,0:T(8,128)(2,1)S(1)} %add_convert_fusion.18), channel_id=1, source_target_pairs={{0,8},{2,10},{4,12},{6,14},{8,0},{10,2},{12,4},{14,6},{1,9},{3,11}... | collective-permute-start | bytes 663560 | tf_op jit(solution)/shard_map/ppermute | solution.py:1139
  (64 other events, 542.1 us)
Sparse Core Ops, SparseCore 0:
  11.5 147.0 all-gather.3
  161.5 153.9 all-gather.5
  318.4 94.1 all-gather.7
  540.9 256.1 reduce-scatter.1

commit v3 on v2

--- a/solution.py
+++ b/solution.py
@@ -1404,9 +1404,7 @@
         waits += tuple(down_chain.sent)
         gate_up_grad = gate_up_grads(normed_ffn, gate_back, up_back, after=waits)
         gate_up_share = scatter_all(gate_up_grad)
-        waits = arrived(down_chain) + (gate_up_grad,)
-        step_all(gate_up_grad, down_chain)
-        waits += tuple(down_chain.sent)
+        waits = (gate_up_grad,)
     else:
         down_share = scatter_all(dot_tn(hidden, ffn_back).astype(bf16))
         gate_back, up_back = gate_up_back(ffn_back, w_down, gate, up)
@@ -1458,6 +1456,8 @@
     folded = fold_patches(pieces, rows, cols)
     if near:
         waits = arrived(down_chain) + tuple(part[0] for part in grad_parts) + (folded,)
+        step_all(grad_parts[0][0], down_chain)
+        waits += tuple(down_chain.sent)
     embed_back, grad_pieces, sum_attn_pre = project_back_rows(
         [turned, grad_v], w_project, embedded, early, image, onehot, attn_pre, w_embed, wait=waits
     )

time: 1010 us -> 1010 us (level)
    unnamed x127 -> x121, local copies, waits for them, and re-layouts: 19 us -> 21.1 us
where the time goes in v3:
time: 1010 us; the launch traced here: 999 us
  Pallas kernels  444 us (44%)
  waiting for transfers between devices  259 us (26%)
  other arithmetic  94.2 us (9%)
  starting transfers between devices  76.9 us (8%)
  local copies, waits for them, and re-layouts  67.8 us (7%)
  matrix products  38.3 us (4%)
  between operations  19.2 us (2%)
    all_gather x3, waiting for transfers between devices, gather_all(): return lax.all_gather(shard, ALL, axis=0, tiled=True)  142 us
    pallas_call x4, Pallas kernels, matmul_rows(): pl.pallas_call(ordered(kernel, len(wait)), grid=(tiles + blocks,), in_spe...  128 us
    ppermute x46, waiting for transfers between devices, swap(): lax.ppermute(values, axis, [(i, i ^ 1 << bit) for i in range(lax.axis_siz...  89 us
    pallas_call x1, Pallas kernels, attend_back(): pl.pallas_call(ordered(kernel, len(after)), grid=(pairs,), in_specs=unrea...  67.2 us
    ppermute x46, starting transfers between devices, swap(): lax.ppermute(values, axis, [(i, i ^ 1 << bit) for i in range(lax.axis_siz...  57.7 us
    convert_element_type x24, other arithmetic, sent_next(): sent.append(self.total([term[half:] for term in terms]).astype(kind))  48.3 us
    pallas_call x1, Pallas kernels, attend(): pl.pallas_call(kernel, grid=(pairs,), in_specs=[pl.BlockSpec((length, LAN...  37.1 us
    pallas_call x1, Pallas kernels, project_rows(): pl.pallas_call(kernel, grid=(3,), in_specs=[whole(patches.shape), whole(i...  35.9 us
  transfers between devices with their start and end apart: 59, of which 25 were waited for; matrix products, arithmetic and copies ran while one was open for 19% of the time, Pallas kernels for 39%

profile of v3, /device:TPU:0, one launch (start us, length us, event | category | flops | bytes accessed | tf_op | source)
XLA Modules:
  0.0 999.3 jit_solution(17574293388471414162)
XLA Ops:
  11.2 4.1 collective-permute-start.3
  23.9 5.8 collective-permute-done.5
  31.5 4.7 collective-permute-done.6
  46.4 3.1 sine_multiply_fusion
  49.5 3.0 slice_add_fusion
  63.2 19.9 %collective-permute-done.1 = bf16[8,128,1]{1,2,0:T(2,128)(2,1)S(1)} collective-permute-done((bf16[8,128,1]{1,2,0:T(2,128)(2,1)S(1)}, bf16[8,128,1]{1,2,0:T(2,128)(2,1)S(1)}, u32[]{:S(2)}, u32[]{:S(2)}) %collective-permute-start.1) | collective-permute-done | bytes 2080 | tf_op jit(solution)/shard_map/ppermute | solution.py:1028
  85.3 8.1 copy.103
  96.9 3.9 convolution_convert_fusion
  106.6 13.4 %collective-permute-done.10 = f32[16,7680]{1,0:T(8,128)} collective-permute-done((f32[16,7680]{1,0:T(8,128)}, f32[16,7680]{1,0:T(8,128)}, u32[]{:S(2)}, u32[]{:S(2)}) %collective-permute-start.10) | collective-permute-done | bytes 491552 | tf_op jit(solution)/shard_map/ppermute | solution.py:1139
  123.9 5.7 collective-permute-done.11
  134.2 9.3 collective-permute-done.12
  148.1 11.8 %all-gather.4.cloned.1.call-done.weight_ref.refs_1_.refs_12_ = bf16[1536,6144]{1,0:T(8,128)(2,1)} async-done(((bf16[48,6144]{1,0:T(8,128)(2,1)}), bf16[1536,6144]{1,0:T(8,128)(2,1)}) %all-gather.4.cloned.1.call-update) | async-done | bytes 18874384 | tf_op jit(solution)/shard_map/all_gather | solution.py:1107
  160.8 35.9 %project_rows.1 = (f32[1024,1536]{1,0:T(8,128)}, bf16[1024,1536]{1,0:T(8,128)(2,1)}, bf16[1024,4608]{1,0:T(8,128)(2,1)}, bf16[1024,3072]{1,0:T(8,128)(2,1)}, f32[1024,256]{1,0:T(8,128)}) custom-call(bf16[1024,64]{1,0:T(8,128)(2,1)} %bitcast.81, s32[1024,128]{1,0:T(8,128)} %broadcast_in_dim.98.image_ref.refs_3_.refs_7_.refs_15_, ...), custom_call_target="tpu_custom_call" | custom-call | flops 7247757312 | bytes 25952256 | tf_op jit(solution)/shard_map/project_rows/pallas_call | solution.py:255
  196.7 37.1 %attend.1 = (bf16[1024,1536]{1,0:T(8,128)(2,1)}, f32[12,2,1024]{2,1,0:T(2,128)}) custom-call(bf16[1024,4608]{1,0:T(8,128)(2,1)} %get-tuple-element.65.q_ref.k_ref.v_ref.refs_6_.refs_7_.refs_8_, bf16[1024,4608]{1,0:T(8,128)(2,1)} %get-tuple-element.65.q_ref.k_ref.v_ref.refs_6_.refs_7_.refs_8_, ...), custom_call_target="tpu_custom_call" | custom-call | flops 25769803776 | bytes 6291456 | tf_op jit(solution)/shard_map/attend/pallas_call | solution.py:624
  233.9 17.7 %output_rows.1 = (f32[1024,1536]{1,0:T(8,128)}, f32[1024,1536]{1,0:T(8,128)}, bf16[1024,1536]{1,0:T(8,128)(2,1)}) custom-call(bf16[1024,1536]{1,0:T(8,128)(2,1)} %get-tuple-element.66.refs_0_.refs_9_.refs_1_, bf16[1536,6144]{1,0:T(8,128)(2,1)} %all-gather.4.cloned.1.call-done.weight_ref.refs_1_.refs_12_, f32[1024,1536]{1,0:T(8,128)} %get-tuple-element.67.refs_2_.refs_13_, ...), custom_call_target="tpu_custom_call" | custom-call | flops 2415919104 | bytes 10223616 | tf_op jit(solution)/shard_map/output_rows/pallas_call | solution.py:176
  251.6 65.7 %all-gather.6.cloned.1.call-done.gate_weight.up_weight.refs_3_ = bf16[1536,8192]{1,0:T(8,128)(2,1)} async-done(((bf16[48,8192]{1,0:T(8,128)(2,1)}), bf16[1536,8192]{1,0:T(8,128)(2,1)}) %all-gather.6.cloned.1.call-update) | async-done | bytes 25165840 | tf_op jit(solution)/shard_map/all_gather | solution.py:1107
  317.3 32.2 %gate_up_rows.1 = (bf16[1024,4096]{1,0:T(8,128)(2,1)}, bf16[1024,4096]{1,0:T(8,128)(2,1)}, bf16[1024,4096]{1,0:T(8,128)(2,1)}) custom-call(bf16[1024,1536]{1,0:T(8,128)(2,1)} %get-tuple-element.68.left_ref.refs_6_, bf16[1536,8192]{1,0:T(8,128)(2,1)} %all-gather.6.cloned.1.call-done.gate_weight.up_weight.refs_3_, ...), custom_call_target="tpu_custom_call" | custom-call | flops 12884901888 | bytes 25165824 | tf_op jit(solution)/shard_map/gate_up_rows/pallas_call | solution.py:753
  349.5 64.9 %all-gather.8.cloned.1.call-done.refs_1_.refs_4_ = bf16[4096,1536]{1,0:T(8,128)(2,1)} async-done(((bf16[128,1536]{1,0:T(8,128)(2,1)}), bf16[4096,1536]{1,0:T(8,128)(2,1)}) %all-gather.8.cloned.1.call-update) | async-done | bytes 12582928 | tf_op jit(solution)/shard_map/all_gather | solution.py:1107
  414.4 32.9 %down_rows.1 = (bf16[1024,1536]{1,0:T(8,128)(2,1)}, f32[1024,1536]{1,0:T(8,128)}, bf16[1024,1536]{1,0:T(8,128)(2,1)}, bf16[1024,64]{1,0:T(8,128)(2,1)}, f32[8,1536]{1,0:T(8,128)}, /*index=5*/f32[8,1536]{1,0:T(8,128)}) custom-call(bf16[1024,4096]{1,0:T(8,128)(2,1)} %get-tuple-element.69.refs_0_, ...), custom_call_target="tpu_custom_call" | custom-call | flops 6442450944 | bytes 16777216 | tf_op jit(solution)/shard_map/down_rows/pallas_call | solution.py:176
  447.3 20.8 %third_grads.2 = (bf16[2048,512]{1,0:T(8,128)(2,1)}, bf16[2048,512]{1,0:T(8,128)(2,1)}, bf16[2048,512]{1,0:T(8,128)(2,1)}, bf16[2048,512]{1,0:T(8,128)(2,1)}, bf...) custom-call(bf16[1024,4096]{1,0:T(8,128)(2,1)} %get-tuple-element.69.refs_0_, ...), custom_call_target="tpu_custom_call" | custom-call | flops 6442450944 | bytes 12058624 | tf_op jit(solution)/shard_map/third_grads/pallas_call | solution.py:556
  469.6 26.1 %gate_up_back.1 = (bf16[1024,4096]{1,0:T(8,128)(2,1)}, bf16[1024,4096]{1,0:T(8,128)(2,1)}) custom-call(bf16[2048,512]{1,0:T(8,128)(2,1)} %get-tuple-element.74.refs_0_, bf16[2048,512]{1,0:T(8,128)(2,1)} %get-tuple-element.76.refs_1_, bf16[2048,512]{1,0:T(8,128)(2,1)} %get-tuple-element.77.refs_2_, bf16[1024,1536]{1,0:T(8,128)(2,1)} %get-tuple-element.73.refs_1_.refs_3_, ...), custom_call_target="tpu_custom_call" | custom-call | flops 6442450944 | bytes 23068672 | tf_op jit(solution)/shard_map/gate_up_back/pallas_call | solution.py:786
  509.3 32.8 %gate_up_grads.1.refs_0_ = bf16[1536,8192]{1,0:T(8,128)(2,1)} custom-call(bf16[2048,512]{1,0:T(8,128)(2,1)} %copy-done.11, bf16[2048,512]{1,0:T(8,128)(2,1)} %collective-permute-done.15.refs_1_, bf16[2048,512]{1,0:T(8,128)(2,1)} %collective-permute-done.16.refs_2_, bf16[1024,512]{1,0:T(8,128)(2,1)} %copy-done.15, ...), custom_call_target="tpu_custom_call" | custom-call | flops 12884901888 | bytes 20971520 | tf_op jit(solution)/shard_map/gate_up_grads/pallas_call | solution.py:427
  542.1 47.5 %ffn_back_rows.1 = (f32[1024,1536]{1,0:T(8,128)}, bf16[1024,1536]{1,0:T(8,128)(2,1)}, f32[8,1536]{1,0:T(8,128)}, f32[8,1536]{1,0:T(8,128)}) custom-call(bf16[1536,8192]{1,0:T(8,128)(2,1)} %gate_up_grads.1.refs_0_, bf16[1024,4096]{1,0:T(8,128)(2,1)} %get-tuple-element.80.refs_1_.refs_7_, bf16[1024,4096]{1,0:T(8,128)(2,1)} %get-tuple-element.83.refs_8_.refs_2_, ...), custom_call_target="tpu_custom_call" | custom-call | flops 12884901888 | bytes 27262976 | tf_op jit(solution)/shard_map/ffn_back_rows/pallas_call | solution.py:176
  589.6 10.1 %fusion.2.refs_1_.refs_10_ = bf16[1024,1536]{1,0:T(8,128)(2,1)} fusion(bf16[1024,1536]{1,0:T(8,128)(2,1)} %get-tuple-element.86.refs_2_, bf16[1536,6144]{1,0:T(8,128)(2,1)} %all-gather.4.cloned.1.call-done.weight_ref.refs_1_.refs_12_), kind=kOutput, calls=%fused_computation.8 | convolution fusion | flops 4833411072 | bytes 11010048 | tf_op jit(solution)/shard_map/dot_general | solution.py:61
  610.8 67.2 %attend_back.1 = (bf16[1024,1536]{1,0:T(8,128)(2,1)}, bf16[1024,1536]{1,0:T(8,128)(2,1)}, bf16[1024,1536]{1,0:T(8,128)(2,1)}) custom-call(bf16[1024,512]{1,0:T(8,128)(2,1)} %collective-permute-done.14.refs_0_, bf16[1024,512]{1,0:T(8,128)(2,1)} %collective-permute-done.18.refs_1_, bf16[1024,512]{1,0:T(8,128)(2,1)} %collective-permute-done.20.refs_2_, ...), custom_call_target="tpu_custom_call" | custom-call | flops 64424509440 | bytes 12582912 | tf_op jit(solution)/shard_map/attend_back/pallas_call | solution.py:708
  678.0 10.2 %third_grads.3 = (bf16[768,2048]{1,0:T(8,128)(2,1)}, bf16[768,2048]{1,0:T(8,128)(2,1)}, bf16[768,2048]{1,0:T(8,128)(2,1)}, bf16[768,2048]{1,0:T(8,128)(2,1)}, bf...) custom-call(bf16[1024,1536]{1,0:T(8,128)(2,1)} %get-tuple-element.88.refs_1_.refs_6_.refs_0_, ...), custom_call_target="tpu_custom_call" | custom-call | flops 2415919104 | bytes 5505024 | tf_op jit(solution)/shard_map/third_grads/pallas_call | solution.py:556
  688.1 9.8 masked_grads.5
  707.5 13.6 %turn_back.1 = (bf16[1024,3072]{1,0:T(8,128)(2,1)}, f32[8,1536]{1,0:T(8,128)}) custom-call(bf16[512,512]{1,0:T(8,128)(2,1)} %copy-done.17, bf16[512,512]{1,0:T(8,128)(2,1)} %collective-permute-done.19.refs_1_, bf16[512,512]{1,0:T(8,128)(2,1)} %collective-permute-done.21.refs_2_, bf16[256,512]{1,0:T(8,128)(2,1)} %add_convert_fusion.17.refs_3_, ...), custom_call_target="tpu_custom_call" | custom-call | flops 31457280 | bytes 9437184 | tf_op jit(solution)/shard_map/turn_back/pallas_call | solution.py:952
  721.1 9.8 masked_grads.3
  731.6 11.4 %fusion.13 = f32[1,4,130,34]{1,0,3,2:T(1,128)} fusion(bf16[1,64,16,64]{3,2,1,0:T(8,128)(2,1)} %bitcast.92, s32[4,4,4]{0,2,1:T(4,128)S(1)} %copy-done.45), kind=kOutput, calls=%fused_computation.52 | convolution fusion | flops 8392704 | bytes 202048 | tf_op jit(solution)/shard_map/conv_general_dilated | solution.py:1059
  743.0 5.7 copy.107
  749.6 10.1 %masked_grads.4 = (bf16[768,2048]{1,0:T(8,128)(2,1)}, bf16[768,2048]{1,0:T(8,128)(2,1)}) custom-call(bf16[1024,1536]{1,0:T(8,128)(2,1)} %get-tuple-element.72.refs_0_, bf16[1024,3072]{1,0:T(8,128)(2,1)} %get-tuple-element.92.refs_1_.refs_10_, s32[1]{0:T(128)} %bitcast.11.refs_2_.refs_3_.me_ref, ...), custom_call_target="tpu_custom_call", output_to_operand_aliasing={{0}: (3, {}), {1}: (4, {})} | custom-call | flops 2415919104 | bytes 5505024 | tf_op jit(solution)/shard_map/masked_grads/pallas_call | solution.py:490
  760.5 3.3 collective-permute-start.22
  770.2 29.4 %project_back_rows.1 = (bf16[1024,1536]{1,0:T(8,128)(2,1)}, bf16[1024,64]{1,0:T(8,128)(2,1)}, f32[8,1536]{1,0:T(8,128)}) custom-call(bf16[256,512]{1,0:T(8,128)(2,1)} %copy-done.25, bf16[256,512]{1,0:T(8,128)(2,1)} %collective-permute-done.26.refs_1_, bf16[256,512]{1,0:T(8,128)(2,1)} %collective-permute-done.27.refs_2_, ...), custom_call_target="tpu_custom_call" | custom-call | flops 7247757312 | bytes 18087936 | tf_op jit(solution)/shard_map/project_back_rows/pallas_call | solution.py:176
  804.0 3.4 add_convert_fusion.1.refs_2_
  808.4 3.2 add_convert_fusion.2.refs_1_
  819.6 6.8 small_grads_near.1
  837.0 11.5 %collective-permute-done.48 = bf16[384,2048]{1,0:T(8,128)(2,1)} collective-permute-done((bf16[384,2048]{1,0:T(8,128)(2,1)}, bf16[384,2048]{1,0:T(8,128)(2,1)}, u32[]{:S(2)}, u32[]{:S(2)}) %collective-permute-start.48) | collective-permute-done | bytes 1572896 | tf_op jit(solution)/shard_map/ppermute | solution.py:1139
  851.4 11.3 %fusion.11 = f32[1,4,130,34]{1,0,3,2:T(1,128)} fusion(bf16[1,64,16,64]{3,2,1,0:T(8,128)(2,1)} %bitcast.95, s32[4,4,4]{0,2,1:T(4,128)S(1)} %copy-done.45), kind=kOutput, calls=%fused_computation.50 | convolution fusion | flops 8392704 | bytes 202048 | tf_op jit(solution)/shard_map/conv_general_dilated | solution.py:1059
  862.7 5.5 copy.111
  872.0 5.5 collective-permute-start.30
  877.5 2.9 add_convert_fusion.8
  886.2 5.7 collective-permute-start.45
  915.0 3.4 collective-permute-done.41
  923.9 4.1 collective-permute-done.42
  952.5 5.3 collective-permute-done.47
  963.1 8.4 collective-permute-done.38
  976.0 6.0 collective-permute-done.39
  (365 shorter events, 210.3 us)
Async XLA Ops:
  7.2 152.6 %all-gather.4.cloned.1.call-start = ((), (), s32[]{:S(2)}) async-start(), calls=%async_computation.1 | async-start | bytes 19464192 | tf_op jit(solution)/shard_map/all_gather | solution.py:1107
  9.3 308.0 %all-gather.6.cloned.1.call-start = ((), (), s32[]{:S(2)}) async-start(), calls=%async_computation.2 | async-start | bytes 25952256 | tf_op jit(solution)/shard_map/all_gather | solution.py:1107
  10.0 404.4 %all-gather.8.cloned.1.call-start = ((), (), s32[]{:S(2)}) async-start(), calls=%async_computation.3 | async-start | bytes 12976128 | tf_op jit(solution)/shard_map/all_gather | solution.py:1107
  10.8 979.2 %reduce-scatter.2.cloned.1.call-start = ((), (), s32[]{:S(2)}) async-start(), calls=%async_computation.4 | async-start | bytes 25952256 | tf_op jit(solution)/shard_map/reduce_scatter | solution.py:1111
  42.7 16.2 %collective-permute-start = (bf16[8,64,32]{1,2,0:T(8,128)(2,1)S(1)}, bf16[8,64,32]{1,2,0:T(8,128)(2,1)S(1)}, u32[]{:S(2)}, u32[]{:S(2)}) collective-permute-start(bf16[8,64,32]{1,2,0:T(8,128)(2,1)S(1)} %get-tuple-element.209), channel_id=1, source_target_pairs={{0,16},{16,0},{1,17},{17,1},{2,18},{18,2},{3,19},{19,3},{4,20},{20... | collective-permute-start | bytes 98312 | tf_op jit(solution)/shard_map/ppermute | solution.py:982
  52.5 40.9 %collective-permute-start.9 = (f32[32,7680]{1,0:T(8,128)}, f32[32,7680]{1,0:T(8,128)S(1)}, u32[]{:S(2)}, u32[]{:S(2)}) collective-permute-start(f32[32,7680]{1,0:T(8,128)} %slice_add_fusion), channel_id=1, source_target_pairs={{0,2},{2,0},{4,6},{6,4},{8,10},{10,8},{12,14},{14,12},{1,3},{3,1},... | collective-permute-start | bytes 2949128 | tf_op jit(solution)/shard_map/ppermute | solution.py:1139
  59.3 23.7 %collective-permute-start.1 = (bf16[8,128,1]{1,2,0:T(2,128)(2,1)S(1)}, bf16[8,128,1]{1,2,0:T(2,128)(2,1)S(1)}, u32[]{:S(2)}, u32[]{:S(2)}) collective-permute-start(bf16[8,128,1]{1,2,0:T(2,128)(2,1)S(1)} %get-tuple-element.225), channel_id=1, source_target_pairs={{0,2},{2,4},{4,6},{6,8},{8,10},{10,12},{12,14},{1,3},{3,5},{5,7},{... | collective-permute-start | bytes 6152 | tf_op jit(solution)/shard_map/ppermute | solution.py:1028
  61.9 23.2 %collective-permute-start.2 = (bf16[8,128,1]{1,2,0:T(2,128)(2,1)S(1)}, bf16[8,128,1]{1,2,0:T(2,128)(2,1)S(1)}, u32[]{:S(2)}, u32[]{:S(2)}) collective-permute-start(bf16[8,128,1]{1,2,0:T(2,128)(2,1)S(1)} %get-tuple-element.226), channel_id=1, source_target_pairs={{2,0},{4,2},{6,4},{8,6},{10,8},{12,10},{14,12},{3,1},{5,3},{7,5},{... | collective-permute-start | bytes 6152 | tf_op jit(solution)/shard_map/ppermute | solution.py:1028
  95.5 24.5 %collective-permute-start.10 = (f32[16,7680]{1,0:T(8,128)}, f32[16,7680]{1,0:T(8,128)}, u32[]{:S(2)}, u32[]{:S(2)}) collective-permute-start(f32[16,7680]{1,0:T(8,128)} %slice_add_fusion.1), channel_id=1, source_target_pairs={{0,16},{16,0},{1,17},{17,1},{2,18},{18,2},{3,19},{19,3},{4,20},{20... | collective-permute-start | bytes 1474568 | tf_op jit(solution)/shard_map/ppermute | solution.py:1139
  121.2 8.4 collective-permute-start.11
  130.9 12.6 %collective-permute-start.12 = (f32[4,7680]{1,0:T(4,128)S(1)}, f32[4,7680]{1,0:T(4,128)S(1)}, u32[]{:S(2)}, u32[]{:S(2)}) collective-permute-start(f32[4,7680]{1,0:T(4,128)S(1)} %slice_add_fusion.7), channel_id=1, source_target_pairs={{0,8},{2,10},{4,12},{6,14},{8,0},{10,2},{12,4},{14,6},{1,9},{3,11}... | collective-permute-start | bytes 368648 | tf_op jit(solution)/shard_map/ppermute | solution.py:1139
  468.1 27.5 %collective-permute-start.13 = (bf16[2048,512]{1,0:T(8,128)(2,1)}, bf16[2048,512]{1,0:T(8,128)(2,1)S(1)}, u32[]{:S(2)}, u32[]{:S(2)}) collective-permute-start(bf16[2048,512]{1,0:T(8,128)(2,1)} %get-tuple-element.75), channel_id=1, source_target_pairs={{0,1},{1,0},{2,3},{3,2},{4,5},{5,4},{6,7},{7,6},{8,9},{9,8},{10,11... | collective-permute-start | bytes 6291464 | tf_op jit(solution)/shard_map/ppermute | solution.py:1139
  468.5 33.9 %collective-permute-start.15 = (bf16[2048,512]{1,0:T(8,128)(2,1)}, bf16[2048,512]{1,0:T(8,128)(2,1)}, u32[]{:S(2)}, u32[]{:S(2)}) collective-permute-start(bf16[2048,512]{1,0:T(8,128)(2,1)} %get-tuple-element.81), channel_id=1, source_target_pairs={{0,1},{1,0},{2,3},{3,2},{4,5},{5,4},{6,7},{7,6},{8,9},{9,8},{10,11... | collective-permute-start | bytes 6291464 | tf_op jit(solution)/shard_map/ppermute | solution.py:1139
  468.7 37.2 %collective-permute-start.16 = (bf16[2048,512]{1,0:T(8,128)(2,1)}, bf16[2048,512]{1,0:T(8,128)(2,1)}, u32[]{:S(2)}, u32[]{:S(2)}) collective-permute-start(bf16[2048,512]{1,0:T(8,128)(2,1)} %get-tuple-element.82), channel_id=1, source_target_pairs={{0,1},{1,0},{2,3},{3,2},{4,5},{5,4},{6,7},{7,6},{8,9},{9,8},{10,11... | collective-permute-start | bytes 6291464 | tf_op jit(solution)/shard_map/ppermute | solution.py:1139
  500.9 105.3 %collective-permute-start.14 = (bf16[1024,512]{1,0:T(8,128)(2,1)S(1)}, bf16[1024,512]{1,0:T(8,128)(2,1)}, u32[]{:S(2)}, u32[]{:S(2)}) collective-permute-start(bf16[1024,512]{1,0:T(8,128)(2,1)S(1)} %add_convert_fusion.5.refs_3_), channel_id=1, source_target_pairs={{0,2},{2,0},{4,6},{6,4},{8,10},{10,8},{12,14},{14,12},{1,3},{3,1},... | collective-permute-start | bytes 3145736 | tf_op jit(solution)/shard_map/ppermute | solution.py:1139
  504.9 94.8 %collective-permute-start.18 = (bf16[1024,512]{1,0:T(8,128)(2,1)}, bf16[1024,512]{1,0:T(8,128)(2,1)}, u32[]{:S(2)}, u32[]{:S(2)}) collective-permute-start(bf16[1024,512]{1,0:T(8,128)(2,1)} %add_convert_fusion.4.refs_4_), channel_id=1, source_target_pairs={{0,16},{16,0},{1,17},{17,1},{2,18},{18,2},{3,19},{19,3},{4,20},{20... | collective-permute-start | bytes 3145736 | tf_op jit(solution)/shard_map/ppermute | solution.py:1139
  508.4 94.3 %collective-permute-start.20 = (bf16[1024,512]{1,0:T(8,128)(2,1)}, bf16[1024,512]{1,0:T(8,128)(2,1)}, u32[]{:S(2)}, u32[]{:S(2)}) collective-permute-start(bf16[1024,512]{1,0:T(8,128)(2,1)} %add_convert_fusion.3.refs_5_), channel_id=1, source_target_pairs={{0,4},{2,6},{4,0},{6,2},{8,12},{10,14},{12,8},{14,10},{1,5},{3,7},... | collective-permute-start | bytes 3145736 | tf_op jit(solution)/shard_map/ppermute | solution.py:1139
  602.1 96.0 %collective-permute-start.19 = (bf16[512,512]{1,0:T(8,128)(2,1)}, bf16[512,512]{1,0:T(8,128)(2,1)}, u32[]{:S(2)}, u32[]{:S(2)}) collective-permute-start(bf16[512,512]{1,0:T(8,128)(2,1)} %add_convert_fusion.10.refs_4_), channel_id=1, source_target_pairs={{0,4},{2,6},{4,0},{6,2},{8,12},{10,14},{12,8},{14,10},{1,5},{3,7},... | collective-permute-start | bytes 1572872 | tf_op jit(solution)/shard_map/ppermute | solution.py:1139
  605.4 95.3 %collective-permute-start.21 = (bf16[512,512]{1,0:T(8,128)(2,1)}, bf16[512,512]{1,0:T(8,128)(2,1)}, u32[]{:S(2)}, u32[]{:S(2)}) collective-permute-start(bf16[512,512]{1,0:T(8,128)(2,1)} %add_convert_fusion.9.refs_5_), channel_id=1, source_target_pairs={{0,2},{2,0},{4,6},{6,4},{8,10},{10,8},{12,14},{14,12},{1,3},{3,1},... | collective-permute-start | bytes 1572872 | tf_op jit(solution)/shard_map/ppermute | solution.py:1139
  609.9 93.5 %collective-permute-start.17 = (bf16[512,512]{1,0:T(8,128)(2,1)S(1)}, bf16[512,512]{1,0:T(8,128)(2,1)S(1)}, u32[]{:S(2)}, u32[]{:S(2)}) collective-permute-start(bf16[512,512]{1,0:T(8,128)(2,1)S(1)} %add_convert_fusion.11.refs_3_), channel_id=1, source_target_pairs={{0,16},{16,0},{1,17},{17,1},{2,18},{18,2},{3,19},{19,3},{4,20},{20... | collective-permute-start | bytes 1572872 | tf_op jit(solution)/shard_map/ppermute | solution.py:1139
  698.0 105.3 %collective-permute-start.33 = (bf16[768,2048]{1,0:T(8,128)(2,1)}, bf16[768,2048]{1,0:T(8,128)(2,1)}, u32[]{:S(2)}, u32[]{:S(2)}) collective-permute-start(bf16[768,2048]{1,0:T(8,128)(2,1)} %get-tuple-element.107), channel_id=1, source_target_pairs={{0,1},{1,0},{2,3},{3,2},{4,5},{5,4},{6,7},{7,6},{8,9},{9,8},{10,11... | collective-permute-start | bytes 9437192 | tf_op jit(solution)/shard_map/ppermute | solution.py:1139
  699.5 66.9 %collective-permute-start.26 = (bf16[256,512]{1,0:T(8,128)(2,1)S(1)}, bf16[256,512]{1,0:T(8,128)(2,1)}, u32[]{:S(2)}, u32[]{:S(2)}) collective-permute-start(bf16[256,512]{1,0:T(8,128)(2,1)S(1)} %add_convert_fusion.16.refs_4_), channel_id=1, source_target_pairs={{0,2},{2,0},{4,6},{6,4},{8,10},{10,8},{12,14},{14,12},{1,3},{3,1},... | collective-permute-start | bytes 786440 | tf_op jit(solution)/shard_map/ppermute | solution.py:1139
  702.1 65.6 %collective-permute-start.27 = (bf16[256,512]{1,0:T(8,128)(2,1)S(1)}, bf16[256,512]{1,0:T(8,128)(2,1)}, u32[]{:S(2)}, u32[]{:S(2)}) collective-permute-start(bf16[256,512]{1,0:T(8,128)(2,1)S(1)} %add_convert_fusion.15.refs_5_), channel_id=1, source_target_pairs={{0,16},{16,0},{1,17},{17,1},{2,18},{18,2},{3,19},{19,3},{4,20},{20... | collective-permute-start | bytes 786440 | tf_op jit(solution)/shard_map/ppermute | solution.py:1139
  706.3 54.2 %collective-permute-start.25 = (bf16[256,512]{1,0:T(8,128)(2,1)}, bf16[256,512]{1,0:T(8,128)(2,1)S(1)}, u32[]{:S(2)}, u32[]{:S(2)}) collective-permute-start(bf16[256,512]{1,0:T(8,128)(2,1)} %add_convert_fusion.17.refs_3_), channel_id=1, source_target_pairs={{0,4},{2,6},{4,0},{6,2},{8,12},{10,14},{12,8},{14,10},{1,5},{3,7},... | collective-permute-start | bytes 786440 | tf_op jit(solution)/shard_map/ppermute | solution.py:1139
  730.9 76.5 %collective-permute-start.28 = (bf16[768,2048]{1,0:T(8,128)(2,1)}, bf16[768,2048]{1,0:T(8,128)(2,1)}, u32[]{:S(2)}, u32[]{:S(2)}) collective-permute-start(bf16[768,2048]{1,0:T(8,128)(2,1)} %get-tuple-element.105), channel_id=1, source_target_pairs={{0,1},{1,0},{2,3},{3,2},{4,5},{5,4},{6,7},{7,6},{8,9},{9,8},{10,11... | collective-permute-start | bytes 9437192 | tf_op jit(solution)/shard_map/ppermute | solution.py:1139
  760.5 123.9 %collective-permute-start.22 = (f32[4,130,1]{2,1,0:T(8,128)}, f32[4,130,1]{2,1,0:T(8,128)}, u32[]{:S(2)}, u32[]{:S(2)}) collective-permute-start(f32[4,130,1]{2,1,0:T(8,128)} %get-tuple-element.184), channel_id=1, source_target_pairs={{0,2},{2,4},{4,6},{6,8},{8,10},{10,12},{12,14},{1,3},{3,5},{5,7},{... | collective-permute-start | bytes 6248 | tf_op jit(solution)/shard_map/ppermute | solution.py:1028
  766.4 63.8 %collective-permute-start.34 = (bf16[768,2048]{1,0:T(8,128)(2,1)}, bf16[768,2048]{1,0:T(8,128)(2,1)}, u32[]{:S(2)}, u32[]{:S(2)}) collective-permute-start(bf16[768,2048]{1,0:T(8,128)(2,1)} %get-tuple-element.117), channel_id=1, source_target_pairs={{0,1},{1,0},{2,3},{3,2},{4,5},{5,4},{6,7},{7,6},{8,9},{9,8},{10,11... | collective-permute-start | bytes 9437192 | tf_op jit(solution)/shard_map/ppermute | solution.py:1139
  767.7 32.0 %collective-permute-start.53 = (bf16[128,512]{1,0:T(8,128)(2,1)S(1)}, bf16[128,512]{1,0:T(8,128)(2,1)S(1)}, u32[]{:S(2)}, u32[]{:S(2)}) collective-permute-start(bf16[128,512]{1,0:T(8,128)(2,1)S(1)} %add_convert_fusion.22.refs_8_), channel_id=1, source_target_pairs={{0,8},{2,10},{4,12},{6,14},{8,0},{10,2},{12,4},{14,6},{1,9},{3,11}... | collective-permute-start | bytes 393224 | tf_op jit(solution)/shard_map/ppermute | solution.py:1139
  799.6 12.9 %collective-permute-start.54 = (bf16[128,512]{1,0:T(8,128)(2,1)S(1)}, bf16[128,512]{1,0:T(8,128)(2,1)S(1)}, u32[]{:S(2)}, u32[]{:S(2)}) collective-permute-start(bf16[128,512]{1,0:T(8,128)(2,1)S(1)} %copy-done.32), channel_id=1, source_target_pairs={{0,8},{2,10},{4,12},{6,14},{8,0},{10,2},{12,4},{14,6},{1,9},{3,11}... | collective-permute-start | bytes 393224 | tf_op jit(solution)/shard_map/ppermute | solution.py:1139
  803.3 24.4 %collective-permute-start.52 = (bf16[128,512]{1,0:T(8,128)(2,1)S(1)}, bf16[128,512]{1,0:T(8,128)(2,1)}, u32[]{:S(2)}, u32[]{:S(2)}) collective-permute-start(bf16[128,512]{1,0:T(8,128)(2,1)S(1)} %copy-done.31), channel_id=1, source_target_pairs={{0,8},{2,10},{4,12},{6,14},{8,0},{10,2},{12,4},{14,6},{1,9},{3,11}... | collective-permute-start | bytes 393224 | tf_op jit(solution)/shard_map/ppermute | solution.py:1139
  807.4 41.1 %collective-permute-start.48 = (bf16[384,2048]{1,0:T(8,128)(2,1)}, bf16[384,2048]{1,0:T(8,128)(2,1)}, u32[]{:S(2)}, u32[]{:S(2)}) collective-permute-start(bf16[384,2048]{1,0:T(8,128)(2,1)} %add_convert_fusion.1.refs_2_), channel_id=1, source_target_pairs={{0,4},{2,6},{4,0},{6,2},{8,12},{10,14},{12,8},{14,10},{1,5},{3,7},... | collective-permute-start | bytes 4718600 | tf_op jit(solution)/shard_map/ppermute | solution.py:1139
  812.6 38.8 %collective-permute-start.29 = (bf16[384,2048]{1,0:T(8,128)(2,1)}, bf16[384,2048]{1,0:T(8,128)(2,1)}, u32[]{:S(2)}, u32[]{:S(2)}) collective-permute-start(bf16[384,2048]{1,0:T(8,128)(2,1)} %add_convert_fusion.2.refs_1_), channel_id=1, source_target_pairs={{0,16},{16,0},{1,17},{17,1},{2,18},{18,2},{3,19},{19,3},{4,20},{20... | collective-permute-start | bytes 4718600 | tf_op jit(solution)/shard_map/ppermute | solution.py:1139
  830.2 55.3 %collective-permute-start.23 = (f32[4,130,1]{2,1,0:T(8,128)}, f32[4,130,1]{2,1,0:T(8,128)}, u32[]{:S(2)}, u32[]{:S(2)}) collective-permute-start(f32[4,130,1]{2,1,0:T(8,128)} %get-tuple-element.185), channel_id=1, source_target_pairs={{2,0},{4,2},{6,4},{8,6},{10,8},{12,10},{14,12},{3,1},{5,3},{7,5},{... | collective-permute-start | bytes 6248 | tf_op jit(solution)/shard_map/ppermute | solution.py:1028
  834.3 98.1 %collective-permute-start.36 = (bf16[384,2304]{1,0:T(8,128)(2,1)}, bf16[384,2304]{1,0:T(8,128)(2,1)}, u32[]{:S(2)}, u32[]{:S(2)}) collective-permute-start(bf16[384,2304]{1,0:T(8,128)(2,1)} %add_convert_fusion), channel_id=1, source_target_pairs={{0,2},{2,0},{4,6},{6,4},{8,10},{10,8},{12,14},{14,12},{1,3},{3,1},... | collective-permute-start | bytes 5308424 | tf_op jit(solution)/shard_map/ppermute | solution.py:1139
  870.7 15.5 %collective-permute-start.31 = (f32[4,130,1]{2,1,0:T(8,128)}, f32[4,130,1]{2,1,0:T(8,128)}, u32[]{:S(2)}, u32[]{:S(2)}) collective-permute-start(f32[4,130,1]{2,1,0:T(8,128)} %copy.125), channel_id=1, source_target_pairs={{2,0},{4,2},{6,4},{8,6},{10,8},{12,10},{14,12},{3,1},{5,3},{7,5},{... | collective-permute-start | bytes 6248 | tf_op jit(solution)/shard_map/ppermute | solution.py:1028
  872.0 22.2 %collective-permute-start.30 = (f32[4,130,1]{2,1,0:T(8,128)}, f32[4,130,1]{2,1,0:T(8,128)}, u32[]{:S(2)}, u32[]{:S(2)}) collective-permute-start(f32[4,130,1]{2,1,0:T(8,128)} %copy.124), channel_id=1, source_target_pairs={{0,2},{2,4},{4,6},{6,8},{8,10},{10,12},{12,14},{1,3},{3,5},{5,7},{... | collective-permute-start | bytes 6248 | tf_op jit(solution)/shard_map/ppermute | solution.py:1028
  884.4 36.4 %collective-permute-start.49 = (bf16[192,2048]{1,0:T(8,128)(2,1)}, bf16[192,2048]{1,0:T(8,128)(2,1)}, u32[]{:S(2)}, u32[]{:S(2)}) collective-permute-start(bf16[192,2048]{1,0:T(8,128)(2,1)} %add_convert_fusion.7), channel_id=1, source_target_pairs={{0,2},{2,0},{4,6},{6,4},{8,10},{10,8},{12,14},{14,12},{1,3},{3,1},... | collective-permute-start | bytes 2359304 | tf_op jit(solution)/shard_map/ppermute | solution.py:1139
  885.5 27.1 %collective-permute-start.40 = (bf16[8,3840]{1,0:T(8,128)(2,1)}, bf16[8,3840]{1,0:T(8,128)(2,1)}, u32[]{:S(2)}, u32[]{:S(2)}) collective-permute-start(bf16[8,3840]{1,0:T(8,128)(2,1)} %held_until.17), channel_id=1, source_target_pairs={{0,8},{2,10},{4,12},{6,14},{8,0},{10,2},{12,4},{14,6},{1,9},{3,11}... | collective-permute-start | bytes 184328 | tf_op jit(solution)/shard_map/ppermute | solution.py:1139
  886.2 52.3 %collective-permute-start.45 = (bf16[192,2048]{1,0:T(8,128)(2,1)}, bf16[192,2048]{1,0:T(8,128)(2,1)}, u32[]{:S(2)}, u32[]{:S(2)}) collective-permute-start(bf16[192,2048]{1,0:T(8,128)(2,1)} %add_convert_fusion.8), channel_id=1, source_target_pairs={{0,4},{2,6},{4,0},{6,2},{8,12},{10,14},{12,8},{14,10},{1,5},{3,7},... | collective-permute-start | bytes 2359304 | tf_op jit(solution)/shard_map/ppermute | solution.py:1139
  919.3 8.7 collective-permute-start.42
  922.6 12.8 %collective-permute-start.50 = (bf16[96,2048]{1,0:T(8,128)(2,1)S(1)}, bf16[96,2048]{1,0:T(8,128)(2,1)S(1)}, u32[]{:S(2)}, u32[]{:S(2)}) collective-permute-start(bf16[96,2048]{1,0:T(8,128)(2,1)S(1)} %add_convert_fusion.13), channel_id=1, source_target_pairs={{0,16},{16,0},{1,17},{17,1},{2,18},{18,2},{3,19},{19,3},{4,20},{20... | collective-permute-start | bytes 1179656 | tf_op jit(solution)/shard_map/ppermute | solution.py:1139
  928.8 23.5 %collective-permute-start.43 = (bf16[64,3840]{1,0:T(8,128)(2,1)S(1)}, bf16[64,3840]{1,0:T(8,128)(2,1)S(1)}, u32[]{:S(2)}, u32[]{:S(2)}) collective-permute-start(bf16[64,3840]{1,0:T(8,128)(2,1)S(1)} %pad_maximum_fusion.4), channel_id=1, source_target_pairs={{0,2},{2,0},{4,6},{6,4},{8,10},{10,8},{12,14},{14,12},{1,3},{3,1},... | collective-permute-start | bytes 1474568 | tf_op jit(solution)/shard_map/ppermute | solution.py:1139
  934.2 26.4 %collective-permute-start.37 = (bf16[192,2304]{1,0:T(8,128)(2,1)S(1)}, bf16[192,2304]{1,0:T(8,128)(2,1)S(1)}, u32[]{:S(2)}, u32[]{:S(2)}) collective-permute-start(bf16[192,2304]{1,0:T(8,128)(2,1)S(1)} %add_convert_fusion.6), channel_id=1, source_target_pairs={{0,16},{16,0},{1,17},{17,1},{2,18},{18,2},{3,19},{19,3},{4,20},{20... | collective-permute-start | bytes 2654216 | tf_op jit(solution)/shard_map/ppermute | solution.py:1139
  936.8 8.5 collective-permute-start.51
  940.0 8.3 collective-permute-start.46
  952.4 9.6 collective-permute-start.44
  962.0 9.6 collective-permute-start.38
  972.8 9.3 collective-permute-start.39
  (61 other events, 588.8 us)
Sparse Core Ops, SparseCore 0:
  11.5 148.2 all-gather.3
  162.7 154.5 all-gather.5
  320.2 94.1 all-gather.7
  542.2 258.8 reduce-scatter.1
